TPU v7x, 32 devices: a whole 2x2x4 slice. The times are simulated.
32 devices in a mesh: groups: 1, ex: 32 (over z, y, x, core).
Axes of the slice: x: 2, y: 2, z: 4, core: 2. Of those that a mesh axis runs over, the one named last changes fastest.
Arguments:
- tokens: bfloat16 [2048, 2880], P(('groups', 'ex')), may hold values from -6 to 6
- norm_gain: float32 [2880], replicated, may hold values from 0.5 to 1.5
- expert_ids: int32 [2048, 4], P(('groups', 'ex')), may hold values from 0 to 7, all different within a row; in each aligned block of 64 rows (0 to 63, 64 to 127, ...) at most 48 rows name the same one
- gate_weights: float32 [2048, 4], P(('groups', 'ex')), may hold values from 0.05 to 0.6
- gate_proj: bfloat16 [32, 2880, 640], P('ex'), may hold values from -0.109375 to 0.109375
- up_proj: bfloat16 [32, 2880, 640], P('ex'), may hold values from -0.109375 to 0.109375
- down_proj: bfloat16 [32, 640, 2880], P('ex'), may hold values from -0.125 to 0.125
Outputs:
- mixed: bfloat16 [2048, 2880], P(('groups', 'ex'))
Inputs may be any that keep to these rules, and one draw needn't show every extreme that they name: `expert_ids`: each row names 4 different experts. In each aligned block of 64 rows (the rows of one index of ex) no expert is named by more than 48 rows, a bound that some block reaches.
All inputs are finite; a program needn't handle non-finite values.
Results may differ from a plain program's by a relative error of at most 0.0065.
Values may be sent and summed in bfloat16 or wider, within the bound.
No kernel may reach another device: no remote copies, remote signals or barrier semaphores. Data moves between devices by JAX's collectives and lax.ppermute only.
A program may use at most 128 MiB of HBM per device.

v0:
```python
import jax
import jax.numpy as jnp
from jax import lax
from jax.sharding import PartitionSpec as P

SLICES = 4


def expert_rows(routed, gate_w, up_w, down_w):
    flat_rows = routed.reshape(-1, routed.shape[-1])
    gate_act = jnp.dot(flat_rows, gate_w, preferred_element_type=jnp.float32)
    up_act = jnp.dot(flat_rows, up_w, preferred_element_type=jnp.float32)
    hidden = (jax.nn.silu(gate_act) * up_act).astype(jnp.bfloat16)
    produced = jnp.dot(hidden, down_w, preferred_element_type=jnp.float32)
    return produced.reshape(routed.shape[:-1] + (down_w.shape[1],))


def local(tokens, norm_gain, expert_ids, gate_weights, gate_proj, up_proj, down_proj):
    tok_rows, features = tokens.shape
    picks = expert_ids.shape[1]
    devices = lax.axis_size("ex")
    experts = devices // SLICES
    capacity = min(tok_rows, 4 * ((3 * tok_rows * picks + 8 * experts - 1) // (8 * experts)))
    gate_w = gate_proj[0]
    up_w = up_proj[0]
    down_w = down_proj[0]
    values = tokens.astype(jnp.float32)
    mean_sq = jnp.mean(values * values, axis=-1, keepdims=True)
    normed = (values * lax.rsqrt(mean_sq + 1e-05) * norm_gain).astype(jnp.bfloat16)
    padded = jnp.concatenate([normed, jnp.zeros((1, features), normed.dtype)], axis=0)
    flat_expert = expert_ids.reshape(-1)
    onehot = (flat_expert[:, None] == jnp.arange(experts, dtype=jnp.int32)[None, :]).astype(
        jnp.int32
    )
    before = jnp.cumsum(onehot, axis=0) - onehot
    rank_in = jnp.sum(before * onehot, axis=1)
    token_index = jnp.arange(tok_rows * picks, dtype=jnp.int32) // picks
    slot_index = flat_expert * capacity + rank_in
    table = jnp.full((experts * capacity,), tok_rows, jnp.int32).at[slot_index].set(token_index)
    buffer = padded[table].reshape(experts, capacity, features)
    outgoing = jnp.tile(buffer, (SLICES, 1, 1))
    partials = expert_rows(
        lax.all_to_all(outgoing, "ex", split_axis=0, concat_axis=0, tiled=True),
        gate_w,
        up_w,
        down_w,
    )
    returned = lax.all_to_all(partials, "ex", split_axis=0, concat_axis=0, tiled=True)
    summed = jnp.sum(returned.reshape(SLICES, experts * capacity, features), axis=0)
    gathered = summed[slot_index].reshape(tok_rows, picks, features)
    mixed = jnp.sum(gathered * gate_weights[:, :, None], axis=1)
    return mixed.astype(jnp.bfloat16)


def solution(mesh):
    in_specs = (
        P(("groups", "ex"), None),
        P(),
        P(("groups", "ex"), None),
        P(("groups", "ex"), None),
        P("ex", None, None),
        P("ex", None, None),
        P("ex", None, None),
    )
    out_specs = P(("groups", "ex"), None)
    return jax.shard_map(local, mesh=mesh, in_specs=in_specs, out_specs=out_specs, check_vma=False)
```

profile of v0, /device:TPU:0, one launch (start us, length us, event | category | flops | bytes accessed | tf_op | source)
XLA Modules:
  0.0 669.1 jit_solution(12569808963102741759)
XLA Ops:
  0.0 0.8 copy.10
  0.8 0.1 eq.29
  0.9 0.1 eq.25
  1.0 0.7 broadcast_multiply_fusion
  1.7 0.6 reduce-window.6
  2.3 0.2 slice_reduce_fusion
  2.5 0.1 copy.9
  2.6 0.1 mul.60
  2.7 0.1 fusion.9
  2.8 1.4 scatter_custom_fusion
  4.3 1.2 fusion.5
  5.4 1.2 fusion.7
  6.6 2.9 gather_fusion
  9.5 0.6 tile.11
  10.2 0.0 copy-start.1
  10.2 204.8 %all_to_all.10 = bf16[32,48,2880]{2,1,0:T(8,128)(2,1)S(1)} all-to-all(bf16[32,48,2880]{2,1,0:T(8,128)(2,1)S(1)} %bitcast.30), channel_id=1, replica_groups=mesh['groups'=1,'ex'=32] {'ex'}, dimensions={0} | all-to-all | bytes 17694720 | tf_op jit(solution)/shard_map/all_to_all | solution.py:43
  215.0 0.0 copy-done.1
  215.0 0.0 copy-start.2
  215.0 7.6 %fusion.3 = f32[1536,640]{1,0:T(8,128)S(1)} fusion(bf16[1536,2880]{1,0:T(8,128)(2,1)S(1)} %bitcast.31, bf16[1,2880,640]{2,1,0:T(8,128)(2,1)S(1)} %copy-done.1), kind=kOutput, calls=%fused_computation.8 | convolution fusion | flops 5662310400 | bytes 16465920 | tf_op jit(solution)/shard_map/dot_general | solution.py:11
  222.6 0.0 copy-done.2
  222.6 0.0 copy-start.3
  222.6 7.8 %multiply_convert_fusion = bf16[1536,640]{1,0:T(8,128)(2,1)S(1)} fusion(f32[1536,640]{1,0:T(8,128)S(1)} %fusion.3, bf16[1536,2880]{1,0:T(8,128)(2,1)S(1)} %bitcast.32, bf16[1,2880,640]{2,1,0:T(8,128)(2,1)S(1)} %copy-done.2), kind=kOutput, calls=%fused_computation.4 | convolution fusion | flops 5668208640 | bytes 18432000 | tf_op jit(solution)/shard_map/dot_general | solution.py:12
  230.4 0.0 copy-done.3
  230.4 10.7 %fusion = f32[32,48,2880]{2,1,0:T(8,128)} fusion(bf16[32,48,640]{2,1,0:T(8,128)(2,1)S(1)} %bitcast.37, bf16[1,640,2880]{1,2,0:T(8,128)(2,1)S(1)} %copy-done.3), kind=kOutput, calls=%fused_computation.5 | convolution fusion | flops 5662310400 | bytes 23347200 | tf_op jit(solution)/shard_map/dot_general | solution.py:14
  241.1 0.0 copy-start
  241.1 4.0 all-to-all-start.1
  245.1 0.0 copy-done
  245.1 0.1 copy.12
  245.2 402.1 %all-to-all-done.1 = f32[32,48,2880]{2,1,0:T(8,128)} async-done(((f32[32,48,2880]{2,1,0:T(8,128)}), f32[32,48,2880]{2,1,0:T(8,128)}, u32[]{:S(2)}, u32[]{:S(2)}) %all-to-all-start.1) | async-done | bytes 17694752 | tf_op jit(solution)/shard_map/all_to_all | solution.py:48
  647.3 9.2 %bitcast_reduce_fusion = f32[384,2880]{1,0:T(8,128)} fusion(f32[4,384,2880]{2,1,0:T(8,128)} %bitcast.29), kind=kLoop, calls=%fused_computation.3 | loop fusion | flops 3317760 | bytes 22118400 | tf_op jit(solution)/shard_map/reduce_sum | solution.py:49
  656.5 6.8 %gather_fusion.1 = f32[256,2880]{1,0:T(8,128)} fusion(f32[384,2880]{1,0:T(8,128)} %bitcast_reduce_fusion, s32[1024]{0:T(1024)S(1)} %pad_clamp_fusion), kind=kCustom, calls=%fused_computation.1 | custom fusion | bytes 5899264 | tf_op jit(solution)/shard_map/gather | solution.py:50
  663.3 3.0 reshape.74
  666.3 2.8 multiply_reduce_fusion
  (10 shorter events, 0.1 us)
Async XLA Ops:
  10.2 204.8 %copy-start.1 = (bf16[1,2880,640]{2,1,0:T(8,128)(2,1)S(1)}, bf16[1,2880,640]{2,1,0:T(8,128)(2,1)}, u32[]{:S(2)}) copy-start(bf16[1,2880,640]{2,1,0:T(8,128)(2,1)} %param.11) | copy-start | bytes 11059204
  215.0 7.6 %copy-start.2 = (bf16[1,2880,640]{2,1,0:T(8,128)(2,1)S(1)}, bf16[1,2880,640]{2,1,0:T(8,128)(2,1)}, u32[]{:S(2)}) copy-start(bf16[1,2880,640]{2,1,0:T(8,128)(2,1)} %param.12) | copy-start | bytes 11059204
  222.6 7.8 %copy-start.3 = (bf16[1,640,2880]{1,2,0:T(8,128)(2,1)S(1)}, bf16[1,640,2880]{1,2,0:T(8,128)(2,1)}, u32[]{:S(2)}) copy-start(bf16[1,640,2880]{1,2,0:T(8,128)(2,1)} %param.13) | copy-start | bytes 11059204
  241.1 4.0 copy-start
  241.1 406.2 %all-to-all-start.1 = ((f32[32,48,2880]{2,1,0:T(8,128)}), f32[32,48,2880]{2,1,0:T(8,128)}, u32[]{:S(2)}, u32[]{:S(2)}) async-start(f32[32,48,2880]{2,1,0:T(8,128)} %fusion), calls=%async_computation.1 | async-start | bytes 36175872 | tf_op jit(solution)/shard_map/all_to_all | solution.py:48
where the time goes:
time: 670 us; the launch traced here: 669 us
  waiting for transfers between devices  402 us (60%)
  blocking collectives  205 us (31%)
  matrix products  26.1 us (4%)
  local copies, waits for them, and re-layouts  16.2 us (2%)
  other arithmetic  15.8 us (2%)
    all_to_all x1, waiting for transfers between devices, local(): lax.all_to_all(partials, 'ex', split_axis=0, concat_axis=0, tiled=True)  402 us
    all_to_all x1, blocking collectives, local(): lax.all_to_all(outgoing, 'ex', split_axis=0, concat_axis=0, tiled=True)  205 us
  transfers between devices with their start and end apart: 1, of which 1 were waited for; matrix products, arithmetic and copies ran while one was open for 0% of the time, Pallas kernels for 0%

commit v1 on v0

v1 whole, which is shorter than its diff:
```python
import jax
import jax.numpy as jnp
from jax import lax
from jax.sharding import PartitionSpec as P

SLICES = 4
LANES = 128
BF16 = jnp.bfloat16
F32 = jnp.float32


def normalise(tokens, norm_gain):
    values = tokens.astype(F32)
    mean_sq = jnp.mean(values * values, axis=-1, keepdims=True)
    return (values * lax.rsqrt(mean_sq + 1e-05) * norm_gain).astype(BF16)


def expert_rows(flat_rows, gate_w, up_w, down_w):
    gate_act = jnp.dot(flat_rows, gate_w, preferred_element_type=F32)
    up_act = jnp.dot(flat_rows, up_w, preferred_element_type=F32)
    hidden = (jax.nn.silu(gate_act) * up_act).astype(BF16)
    return jnp.dot(hidden, down_w, preferred_element_type=F32)


def local_general(tokens, norm_gain, expert_ids, gate_weights, gate_proj, up_proj, down_proj):
    tok_rows, features = tokens.shape
    picks = expert_ids.shape[1]
    devices = lax.axis_size("ex")
    experts = devices // SLICES
    capacity = min(tok_rows, 4 * ((3 * tok_rows * picks + 8 * experts - 1) // (8 * experts)))
    normed = normalise(tokens, norm_gain)
    padded = jnp.concatenate([normed, jnp.zeros((1, features), normed.dtype)], axis=0)
    flat_expert = expert_ids.reshape(-1)
    onehot = (flat_expert[:, None] == jnp.arange(experts, dtype=jnp.int32)[None, :]).astype(
        jnp.int32
    )
    before = jnp.cumsum(onehot, axis=0) - onehot
    rank_in = jnp.sum(before * onehot, axis=1)
    token_index = jnp.arange(tok_rows * picks, dtype=jnp.int32) // picks
    slot_index = flat_expert * capacity + rank_in
    table = jnp.full((experts * capacity,), tok_rows, jnp.int32).at[slot_index].set(token_index)
    buffer = padded[table].reshape(experts, capacity, features)
    outgoing = jnp.tile(buffer, (SLICES, 1, 1))
    arrived = lax.all_to_all(outgoing, "ex", split_axis=0, concat_axis=0, tiled=True)
    partials = expert_rows(arrived.reshape(-1, features), gate_proj[0], up_proj[0], down_proj[0])
    partials = partials.reshape(devices, capacity, features)
    returned = lax.all_to_all(partials, "ex", split_axis=0, concat_axis=0, tiled=True)
    summed = jnp.sum(returned.reshape(SLICES, experts * capacity, features), axis=0)
    gathered = summed[slot_index].reshape(tok_rows, picks, features)
    mixed = jnp.sum(gathered * gate_weights[:, :, None], axis=1)
    return mixed.astype(BF16)


def local_cube(tokens, norm_gain, expert_ids, gate_weights, gate_proj, up_proj, down_proj):
    tok_rows, features = tokens.shape
    devices = lax.axis_size("ex")
    experts = devices // SLICES
    mine = lax.axis_index("ex") % experts
    width = -(-(features + 3 * experts) // LANES) * LANES

    def swap(array, partner):
        return lax.ppermute(array, "ex", [(i, partner(i)) for i in range(devices)])

    def first(i):
        return i ^ (2 if i % 2 == 0 else 4)

    def second(i):
        return i ^ (4 if i % 2 == 0 else 2)

    def core(i):
        return i ^ 1

    def slice_bits(j):
        return lambda i: i ^ (j * experts)

    normed = normalise(tokens, norm_gain)
    picked = expert_ids[:, :, None] == jnp.arange(experts, dtype=jnp.int32)[None, None, :]
    dense = jnp.sum(jnp.where(picked, gate_weights[:, :, None], 0.0), axis=1)
    high = lax.reduce_precision(dense, 8, 7)
    rest = dense - high
    middle = lax.reduce_precision(rest, 8, 7)
    low = rest - middle
    extra = [part.astype(BF16) for part in (high, middle, low)]
    fill = jnp.zeros((tok_rows, width - features - 3 * experts), BF16)
    rows = jnp.concatenate([normed, *extra, fill], axis=1)

    def partial(block):
        produced = expert_rows(block[:, :features], gate_proj[0], up_proj[0], down_proj[0])
        parts = block[:, features : features + 3 * experts].astype(F32)
        column = jnp.arange(3 * experts, dtype=jnp.int32) % experts == mine
        weight = jnp.sum(jnp.where(column[None, :], parts, 0.0), axis=1, keepdims=True)
        return produced * weight

    blocks = [rows] + [swap(rows, slice_bits(j)) for j in range(1, SLICES)]
    total = None
    for j, block in enumerate(blocks):
        half = jnp.concatenate([block, swap(block, first)], axis=0)
        full = jnp.concatenate([half, swap(half, second)], axis=0)
        other = swap(full, core)
        back = swap(partial(other).astype(BF16), core)
        sums = partial(full) + back.astype(F32)
        cut = 2 * tok_rows
        sums = sums[:cut] + swap(sums[cut:].astype(BF16), second).astype(F32)
        sums = sums[:tok_rows] + swap(sums[tok_rows:].astype(BF16), first).astype(F32)
        if j:
            sums = swap(sums.astype(BF16), slice_bits(j)).astype(F32)
        total = sums if total is None else total + sums
    return total.astype(BF16)


def solution(mesh):
    in_specs = (
        P(("groups", "ex"), None),
        P(),
        P(("groups", "ex"), None),
        P(("groups", "ex"), None),
        P("ex", None, None),
        P("ex", None, None),
        P("ex", None, None),
    )
    out_specs = P(("groups", "ex"), None)
    local = local_cube if mesh.shape["ex"] == 8 * SLICES else local_general
    return jax.shard_map(local, mesh=mesh, in_specs=in_specs, out_specs=out_specs, check_vma=False)
```

time: 670 us -> 244 us (0.36)
  waiting for transfers between devices: 402 us -> 70.1 us
  blocking collectives: 205 us -> 0 us
  matrix products: 26.1 us -> 83.5 us
  starting transfers between devices: 4.02 us -> 37.1 us
  local copies, waits for them, and re-layouts: 16.2 us -> 35.7 us
    all_to_all x1 -> x0, waiting for transfers between devices: 402 us -> none  [local(): lax.all_to_all(partials, 'ex', split_axis=0, concat_axis=0, tiled=True)]
    all_to_all x1 -> x0, blocking collectives: 205 us -> none  [local(): lax.all_to_all(outgoing, 'ex', split_axis=0, concat_axis=0, tiled=True)]
    ppermute x0 -> x30, waiting for transfers between devices: none -> 70.1 us  [swap(): return lax.ppermute(array, 'ex', [(i, partner(i)) for i in range(devices)])]
    dot_general x3 -> x16, matrix products: 26.1 us -> 83.5 us  [the longest x8 62.2 us: expert_rows(): return jnp.dot(hidden, down_w, preferred_element_type=F32)]
    ppermute x0 -> x30, starting transfers between devices: none -> 37.1 us  [swap(): return lax.ppermute(array, 'ex', [(i, partner(i)) for i in range(devices)])]
    ppermute x0 -> x8, local copies, waits for them, and re-layouts: none -> 18.6 us  [swap(): return lax.ppermute(array, 'ex', [(i, partner(i)) for i in range(devices)])]
    slice x1 -> x12, local copies, waits for them, and re-layouts: 0.21 us -> 12.1 us  [the longest x8 9.7 us: local_cube(): sums = sums[:cut] + swap(sums[cut:].astype(BF16), second).astype(F32)]
    reduce_sum x4 -> x3, other arithmetic: 13.3 us -> 2.28 us  [the longest x1 1.17 us: normalise(): mean_sq = jnp.mean(values * values, axis=-1, keepdims=True)]
  transfers between devices with their start and end apart: 1 -> 30, of which waited for: 1 -> 8; matrix products, arithmetic and copies ran while one was open for 0% -> 48% of each run, Pallas kernels for 0% -> 0%
where the time goes in v1:
time: 244 us; the launch traced here: 240 us
  matrix products  83.5 us (34%)
  waiting for transfers between devices  70.1 us (29%)
  starting transfers between devices  37.1 us (15%)
  local copies, waits for them, and re-layouts  35.7 us (15%)
  other arithmetic  13.6 us (6%)
    ppermute x30, waiting for transfers between devices, swap(): return lax.ppermute(array, 'ex', [(i, partner(i)) for i in range(devices)])  70.1 us
    dot_general x8, matrix products, expert_rows(): return jnp.dot(hidden, down_w, preferred_element_type=F32)  62.2 us
    ppermute x30, starting transfers between devices, swap(): return lax.ppermute(array, 'ex', [(i, partner(i)) for i in range(devices)])  37.1 us
    dot_general x8, matrix products, expert_rows(): up_act = jnp.dot(flat_rows, up_w, preferred_element_type=F32)  21.3 us
    ppermute x8, local copies, waits for them, and re-layouts, swap(): return lax.ppermute(array, 'ex', [(i, partner(i)) for i in range(devices)])  18.6 us
    slice x8, local copies, waits for them, and re-layouts, local_cube(): sums = sums[:cut] + swap(sums[cut:].astype(BF16), second).astype(F32)  9.7 us
    add x4, other arithmetic, local_cube(): sums = sums[:cut] + swap(sums[cut:].astype(BF16), second).astype(F32)  6.61 us
  transfers between devices with their start and end apart: 30, of which 8 were waited for; matrix products, arithmetic and copies ran while one was open for 48% of the time, Pallas kernels for 0%

profile of v1, /device:TPU:0, one launch (start us, length us, event | category | flops | bytes accessed | tf_op | source)
XLA Modules:
  0.0 240.3 jit_solution(4183447857683850243)
XLA Ops:
  3.5 3.0 %collective-permute-start = (bf16[64,2944]{1,0:T(8,128)(2,1)S(1)}, bf16[64,2944]{1,0:T(8,128)(2,1)S(1)}, u32[]{:S(2)}, u32[]{:S(2)}) collective-permute-start(bf16[64,2944]{1,0:T(8,128)(2,1)S(1)} %concatenate.31), channel_id=1, source_target_pairs={{0,2},{1,5},{2,0},{3,7},{4,6},{5,1},{6,4},{7,3},{8,10},{9,13},{10,... | collective-permute-start | bytes 1130504 | tf_op jit(solution)/shard_map/ppermute | solution.py:62
  6.5 2.6 %collective-permute-start.14 = (bf16[64,2944]{1,0:T(8,128)(2,1)S(1)}, bf16[64,2944]{1,0:T(8,128)(2,1)S(1)}, u32[]{:S(2)}, u32[]{:S(2)}) collective-permute-start(bf16[64,2944]{1,0:T(8,128)(2,1)S(1)} %concatenate.31), channel_id=1, source_target_pairs={{0,16},{1,17},{2,18},{3,19},{4,20},{5,21},{6,22},{7,23},{8,24},{9,... | collective-permute-start | bytes 1130504 | tf_op jit(solution)/shard_map/ppermute | solution.py:62
  12.1 2.1 collective-permute-start.1
  14.3 20.8 %collective-permute-done.14 = bf16[64,2944]{1,0:T(8,128)(2,1)S(1)} collective-permute-done((bf16[64,2944]{1,0:T(8,128)(2,1)S(1)}, bf16[64,2944]{1,0:T(8,128)(2,1)S(1)}, u32[]{:S(2)}, u32[]{:S(2)}) %collective-permute-start.14) | collective-permute-done | bytes 376864 | tf_op jit(solution)/shard_map/ppermute | solution.py:62
  35.5 1.7 collective-permute-start.23
  37.7 4.9 %collective-permute-done.15 = bf16[64,2944]{1,0:T(8,128)(2,1)S(1)} collective-permute-done((bf16[64,2944]{1,0:T(8,128)(2,1)S(1)}, bf16[64,2944]{1,0:T(8,128)(2,1)S(1)}, u32[]{:S(2)}, u32[]{:S(2)}) %collective-permute-start.15) | collective-permute-done | bytes 376864 | tf_op jit(solution)/shard_map/ppermute | solution.py:62
  43.3 6.9 %collective-permute-done.23 = bf16[64,2944]{1,0:T(8,128)(2,1)S(1)} collective-permute-done((bf16[64,2944]{1,0:T(8,128)(2,1)S(1)}, bf16[64,2944]{1,0:T(8,128)(2,1)S(1)}, u32[]{:S(2)}, u32[]{:S(2)}) %collective-permute-start.23) | collective-permute-done | bytes 376864 | tf_op jit(solution)/shard_map/ppermute | solution.py:62
  51.0 7.2 %collective-permute-done.7 = bf16[64,2944]{1,0:T(8,128)(2,1)S(1)} collective-permute-done((bf16[64,2944]{1,0:T(8,128)(2,1)S(1)}, bf16[64,2944]{1,0:T(8,128)(2,1)S(1)}, u32[]{:S(2)}, u32[]{:S(2)}) %collective-permute-start.7) | collective-permute-done | bytes 376864 | tf_op jit(solution)/shard_map/ppermute | solution.py:62
  59.4 1.8 copy-done.9
  61.2 2.2 fusion.26
  63.8 3.4 %collective-permute-start.25 = (bf16[256,2944]{1,0:T(8,128)(2,1)S(1)}, bf16[256,2944]{1,0:T(8,128)(2,1)S(1)}, u32[]{:S(2)}, u32[]{:S(2)}) collective-permute-start(bf16[256,2944]{1,0:T(8,128)(2,1)S(1)} %constant_dynamic-update-slice_fusion.6), channel_id=1, source_target_pairs={{0,1},{1,0},{2,3},{3,2},{4,5},{5,4},{6,7},{7,6},{8,9},{9,8},{10,11... | collective-permute-start | bytes 4521992 | tf_op jit(solution)/shard_map/ppermute | solution.py:62
  67.1 4.6 %collective-permute-done.8 = bf16[128,2944]{1,0:T(8,128)(2,1)S(1)} collective-permute-done((bf16[128,2944]{1,0:T(8,128)(2,1)S(1)}, bf16[128,2944]{1,0:T(8,128)(2,1)S(1)}, u32[]{:S(2)}, u32[]{:S(2)}) %collective-permute-start.8) | collective-permute-done | bytes 753696 | tf_op jit(solution)/shard_map/ppermute | solution.py:62
  71.8 3.1 %collective-permute-start.9 = (bf16[256,2944]{1,0:T(8,128)(2,1)S(1)}, bf16[256,2944]{1,0:T(8,128)(2,1)S(1)}, u32[]{:S(2)}, u32[]{:S(2)}) collective-permute-start(bf16[256,2944]{1,0:T(8,128)(2,1)S(1)} %constant_dynamic-update-slice_fusion), channel_id=1, source_target_pairs={{0,1},{1,0},{2,3},{3,2},{4,5},{5,4},{6,7},{7,6},{8,9},{9,8},{10,11... | collective-permute-start | bytes 4521992 | tf_op jit(solution)/shard_map/ppermute | solution.py:62
  76.3 2.2 fusion.18
  78.5 2.2 fusion.14
  80.7 2.3 fusion.24
  83.0 2.3 fusion.20
  87.0 7.5 %multiply_convert_fusion.2 = bf16[256,2880]{0,1:T(8,128)(2,1)} fusion(f32[256]{0:T(256)S(1)} %get-tuple-element.7, bf16[1,640,2880]{1,2,0:T(8,128)(2,1)} %param.13, f32[256,640]{1,0:T(8,128)} %fusion.20, bf16[1,2880,640]{2,1,0:T(8,128)(2,1)} %param.11, bf16[256,2944]{1,0:T(8,128)(2,1)} %copy-done.8), kind=kOutput, calls=%fused_computation.54 | convolution fusion | flops 1889894400 | bytes 11011072 | tf_op jit(solution)/shard_map/dot_general | solution.py:22
  94.5 4.0 %fusion.16 = f32[256,640]{1,0:T(8,128)S(1)} fusion(bf16[1,2880,640]{2,1,0:T(8,128)(2,1)} %param.12, bf16[256,2944]{1,0:T(8,128)(2,1)} %copy-done.6), kind=kOutput, calls=%fused_computation.20 | convolution fusion | flops 943718400 | bytes 5849088 | tf_op jit(solution)/shard_map/dot_general | solution.py:20
  98.5 7.3 %multiply_convert_fusion.1 = bf16[256,2880]{0,1:T(8,128)(2,1)} fusion(f32[256]{0:T(256)S(1)} %get-tuple-element.9, bf16[1,640,2880]{1,2,0:T(8,128)(2,1)} %param.13, f32[256,640]{1,0:T(8,128)S(1)} %fusion.16, bf16[1,2880,640]{2,1,0:T(8,128)(2,1)} %param.11, bf16[256,2944]{1,0:T(8,128)(2,1)} %copy-done.6), kind=kOutput, calls=%fused_computation.53 | convolution fusion | flops 1889894400 | bytes 11011072 | tf_op jit(solution)/shard_map/dot_general | solution.py:22
  106.4 4.7 %fusion.12 = f32[256,640]{1,0:T(8,128)} fusion(bf16[1,2880,640]{2,1,0:T(8,128)(2,1)} %param.12, bf16[256,2944]{1,0:T(8,128)(2,1)} %copy-done.7), kind=kOutput, calls=%fused_computation.16 | convolution fusion | flops 943718400 | bytes 5849088 | tf_op jit(solution)/shard_map/dot_general | solution.py:20
  111.1 7.6 %multiply_convert_fusion = bf16[256,2880]{0,1:T(8,128)(2,1)} fusion(f32[256]{0:T(256)S(1)} %get-tuple-element.11, bf16[1,640,2880]{1,2,0:T(8,128)(2,1)} %param.13, f32[256,640]{1,0:T(8,128)} %fusion.12, bf16[1,2880,640]{2,1,0:T(8,128)(2,1)} %param.11, bf16[256,2944]{1,0:T(8,128)(2,1)} %copy-done.7), kind=kOutput, calls=%fused_computation.52 | convolution fusion | flops 1889894400 | bytes 11011072 | tf_op jit(solution)/shard_map/dot_general | solution.py:22
  118.6 7.3 %multiply_convert_fusion.3 = bf16[256,2880]{0,1:T(8,128)(2,1)} fusion(f32[256]{0:T(256)S(1)} %get-tuple-element.6, bf16[1,640,2880]{1,2,0:T(8,128)(2,1)} %param.13, f32[256,640]{1,0:T(8,128)S(1)} %copy-done.13, bf16[1,2880,640]{2,1,0:T(8,128)(2,1)} %param.11, bf16[256,2944]{1,0:T(8,128)(2,1)} %copy-done.5), kind=kOutput, calls=%fused_computation.55 | convolution fusion | flops 1889894400 | bytes 11011072 | tf_op jit(solution)/shard_map/dot_general | solution.py:22
  126.5 2.6 %copy.65 = bf16[256,2880]{1,0:T(8,128)(2,1)} copy(bf16[256,2880]{0,1:T(8,128)(2,1)} %collective-permute-done.10) | data formatting | bytes 2949120 | tf_op jit(solution)/shard_map/ppermute | solution.py:62
  129.0 8.2 %convert_add_fusion.2 = f32[256,2880]{1,0:T(8,128)} fusion(bf16[256,2880]{1,0:T(8,128)(2,1)} %copy.65, f32[256]{0:T(256)S(1)} %get-tuple-element.5, bf16[1,640,2880]{1,2,0:T(8,128)(2,1)} %param.13, f32[256,640]{1,0:T(8,128)S(1)} %fusion.22, bf16[1,2880,640]{2,1,0:T(8,128)(2,1)} %param.11, bf16[256,2944]{1,0:T(8,128)(2,1)} %copy-done.4), kind=kOutput, calls=%fused_computation.50 | convolution fusion | flops 1890631680 | bytes 13960192 | tf_op jit(solution)/shard_map/dot_general | solution.py:22
  137.3 1.5 slice.280
  139.7 2.6 %copy.69 = bf16[256,2880]{1,0:T(8,128)(2,1)} copy(bf16[256,2880]{0,1:T(8,128)(2,1)} %collective-permute-done.18) | data formatting | bytes 2949120 | tf_op jit(solution)/shard_map/ppermute | solution.py:62
  142.3 8.3 %convert_add_fusion.1 = f32[256,2880]{1,0:T(8,128)} fusion(bf16[256,2880]{1,0:T(8,128)(2,1)} %copy.69, f32[256]{0:T(256)S(1)} %get-tuple-element.8, bf16[1,640,2880]{1,2,0:T(8,128)(2,1)} %param.13, f32[256,640]{1,0:T(8,128)S(1)} %copy-done.12, bf16[1,2880,640]{2,1,0:T(8,128)(2,1)} %param.11, bf16[256,2944]{1,0:T(8,128)(2,1)} %copy-done.2), kind=kOutput, calls=%fused_computation.49 | convolution fusion | flops 1890631680 | bytes 13960192 | tf_op jit(solution)/shard_map/dot_general | solution.py:22
  153.2 1.5 collective-permute-start.19
  154.7 2.6 %copy.73 = bf16[256,2880]{1,0:T(8,128)(2,1)} copy(bf16[256,2880]{0,1:T(8,128)(2,1)} %collective-permute-done.26) | data formatting | bytes 2949120 | tf_op jit(solution)/shard_map/ppermute | solution.py:62
  157.3 8.2 %convert_add_fusion = f32[256,2880]{1,0:T(8,128)} fusion(bf16[256,2880]{1,0:T(8,128)(2,1)} %copy.73, f32[256]{0:T(256)S(1)} %get-tuple-element.10, bf16[1,640,2880]{1,2,0:T(8,128)(2,1)} %param.13, f32[256,640]{1,0:T(8,128)S(1)} %copy-done.11, bf16[1,2880,640]{2,1,0:T(8,128)(2,1)} %param.11, bf16[256,2944]{1,0:T(8,128)(2,1)} %copy-done.3), kind=kOutput, calls=%fused_computation.48 | convolution fusion | flops 1890631680 | bytes 13960192 | tf_op jit(solution)/shard_map/dot_general | solution.py:22
  168.6 2.6 %copy.61 = bf16[256,2880]{1,0:T(8,128)(2,1)} copy(bf16[256,2880]{0,1:T(8,128)(2,1)} %collective-permute-done.3) | data formatting | bytes 2949120 | tf_op jit(solution)/shard_map/ppermute | solution.py:62
  171.2 7.8 %convert_add_fusion.3 = f32[256,2880]{1,0:T(8,128)} fusion(bf16[256,2880]{1,0:T(8,128)(2,1)} %copy.61, f32[256]{0:T(256)S(1)} %get-tuple-element.12, bf16[1,640,2880]{1,2,0:T(8,128)(2,1)} %param.13, f32[256,640]{1,0:T(8,128)S(1)} %copy-done.10, bf16[1,2880,640]{2,1,0:T(8,128)(2,1)} %param.11, bf16[256,2944]{1,0:T(8,128)(2,1)S(1)} %pad_maximum_fusion), kind=kOutput, calls=%fused_computation.51 | convolution fusion | flops 1890631680 | bytes 13960192 | tf_op jit(solution)/shard_map/dot_general | solution.py:22
  181.6 1.5 collective-permute-start.4
  184.5 1.5 slice_add_fusion.2
  187.2 2.3 copy.71
  189.6 1.7 slice_add_fusion.1
  192.1 1.6 collective-permute-start.20
  193.7 2.3 copy.75
  196.0 1.7 slice_add_fusion
  200.0 2.3 copy.63
  202.3 1.7 slice_add_fusion.3
  204.0 1.7 collective-permute-start.5
  205.8 3.6 %collective-permute-start.13 = (bf16[64,2880]{1,0:T(8,128)(2,1)S(1)}, bf16[64,2880]{1,0:T(8,128)(2,1)S(1)}, u32[]{:S(2)}, u32[]{:S(2)}) collective-permute-start(bf16[64,2880]{1,0:T(8,128)(2,1)S(1)} %fusion.65), channel_id=1, source_target_pairs={{0,8},{1,9},{2,10},{3,11},{4,12},{5,13},{6,14},{7,15},{8,0},{9,1},... | collective-permute-start | bytes 1105928 | tf_op jit(solution)/shard_map/ppermute | solution.py:62
  210.5 2.0 collective-permute-start.21
  213.5 1.5 collective-permute-start.29
  215.1 7.5 %collective-permute-done.13 = bf16[64,2880]{1,0:T(8,128)(2,1)S(1)} collective-permute-done((bf16[64,2880]{1,0:T(8,128)(2,1)S(1)}, bf16[64,2880]{1,0:T(8,128)(2,1)S(1)}, u32[]{:S(2)}, u32[]{:S(2)}) %collective-permute-start.13) | collective-permute-done | bytes 368672 | tf_op jit(solution)/shard_map/ppermute | solution.py:62
  222.6 16.7 %collective-permute-done.21 = bf16[64,2880]{1,0:T(8,128)(2,1)S(1)} collective-permute-done((bf16[64,2880]{1,0:T(8,128)(2,1)S(1)}, bf16[64,2880]{1,0:T(8,128)(2,1)S(1)}, u32[]{:S(2)}, u32[]{:S(2)}) %collective-permute-start.21) | collective-permute-done | bytes 368672 | tf_op jit(solution)/shard_map/ppermute | solution.py:62
  (110 shorter events, 33.0 us)
Async XLA Ops:
  3.5 8.6 %collective-permute-start = (bf16[64,2944]{1,0:T(8,128)(2,1)S(1)}, bf16[64,2944]{1,0:T(8,128)(2,1)S(1)}, u32[]{:S(2)}, u32[]{:S(2)}) collective-permute-start(bf16[64,2944]{1,0:T(8,128)(2,1)S(1)} %concatenate.31), channel_id=1, source_target_pairs={{0,2},{1,5},{2,0},{3,7},{4,6},{5,1},{6,4},{7,3},{8,10},{9,13},{10,... | collective-permute-start | bytes 1130504 | tf_op jit(solution)/shard_map/ppermute | solution.py:62
  6.5 28.5 %collective-permute-start.14 = (bf16[64,2944]{1,0:T(8,128)(2,1)S(1)}, bf16[64,2944]{1,0:T(8,128)(2,1)S(1)}, u32[]{:S(2)}, u32[]{:S(2)}) collective-permute-start(bf16[64,2944]{1,0:T(8,128)(2,1)S(1)} %concatenate.31), channel_id=1, source_target_pairs={{0,16},{1,17},{2,18},{3,19},{4,20},{5,21},{6,22},{7,23},{8,24},{9,... | collective-permute-start | bytes 1130504 | tf_op jit(solution)/shard_map/ppermute | solution.py:62
  9.1 26.4 %collective-permute-start.22 = (bf16[64,2944]{1,0:T(8,128)(2,1)S(1)}, bf16[64,2944]{1,0:T(8,128)(2,1)S(1)}, u32[]{:S(2)}, u32[]{:S(2)}) collective-permute-start(bf16[64,2944]{1,0:T(8,128)(2,1)S(1)} %concatenate.31), channel_id=1, source_target_pairs={{0,24},{1,25},{2,26},{3,27},{4,28},{5,29},{6,30},{7,31},{8,16},{9,... | collective-permute-start | bytes 1130504 | tf_op jit(solution)/shard_map/ppermute | solution.py:62
  10.4 26.7 %collective-permute-start.6 = (bf16[64,2944]{1,0:T(8,128)(2,1)S(1)}, bf16[64,2944]{1,0:T(8,128)(2,1)S(1)}, u32[]{:S(2)}, u32[]{:S(2)}) collective-permute-start(bf16[64,2944]{1,0:T(8,128)(2,1)S(1)} %concatenate.31), channel_id=1, source_target_pairs={{0,8},{1,9},{2,10},{3,11},{4,12},{5,13},{6,14},{7,15},{8,0},{9,1},... | collective-permute-start | bytes 1130504 | tf_op jit(solution)/shard_map/ppermute | solution.py:62
  12.1 47.1 %collective-permute-start.1 = (bf16[128,2944]{1,0:T(8,128)(2,1)S(1)}, bf16[128,2944]{1,0:T(8,128)(2,1)S(1)}, u32[]{:S(2)}, u32[]{:S(2)}) collective-permute-start(bf16[128,2944]{1,0:T(8,128)(2,1)S(1)} %pad_maximum_fusion.1), channel_id=1, source_target_pairs={{0,4},{1,3},{2,6},{3,1},{4,0},{5,7},{6,2},{7,5},{8,12},{9,11},{10,... | collective-permute-start | bytes 2261000 | tf_op jit(solution)/shard_map/ppermute | solution.py:62
  35.0 7.6 %collective-permute-start.15 = (bf16[64,2944]{1,0:T(8,128)(2,1)S(1)}, bf16[64,2944]{1,0:T(8,128)(2,1)S(1)}, u32[]{:S(2)}, u32[]{:S(2)}) collective-permute-start(bf16[64,2944]{1,0:T(8,128)(2,1)S(1)} %collective-permute-done.14), channel_id=1, source_target_pairs={{0,2},{1,5},{2,0},{3,7},{4,6},{5,1},{6,4},{7,3},{8,10},{9,13},{10,... | collective-permute-start | bytes 1130504 | tf_op jit(solution)/shard_map/ppermute | solution.py:62
  35.5 14.7 %collective-permute-start.23 = (bf16[64,2944]{1,0:T(8,128)(2,1)S(1)}, bf16[64,2944]{1,0:T(8,128)(2,1)S(1)}, u32[]{:S(2)}, u32[]{:S(2)}) collective-permute-start(bf16[64,2944]{1,0:T(8,128)(2,1)S(1)} %collective-permute-done.22), channel_id=1, source_target_pairs={{0,2},{1,5},{2,0},{3,7},{4,6},{5,1},{6,4},{7,3},{8,10},{9,13},{10,... | collective-permute-start | bytes 1130504 | tf_op jit(solution)/shard_map/ppermute | solution.py:62
  37.2 21.0 %collective-permute-start.7 = (bf16[64,2944]{1,0:T(8,128)(2,1)S(1)}, bf16[64,2944]{1,0:T(8,128)(2,1)S(1)}, u32[]{:S(2)}, u32[]{:S(2)}) collective-permute-start(bf16[64,2944]{1,0:T(8,128)(2,1)S(1)} %collective-permute-done.6), channel_id=1, source_target_pairs={{0,2},{1,5},{2,0},{3,7},{4,6},{5,1},{6,4},{7,3},{8,10},{9,13},{10,... | collective-permute-start | bytes 1130504 | tf_op jit(solution)/shard_map/ppermute | solution.py:62
  42.7 20.8 %collective-permute-start.16 = (bf16[128,2944]{1,0:T(8,128)(2,1)S(1)}, bf16[128,2944]{1,0:T(8,128)(2,1)S(1)}, u32[]{:S(2)}, u32[]{:S(2)}) collective-permute-start(bf16[128,2944]{1,0:T(8,128)(2,1)S(1)} %pad_maximum_fusion.3), channel_id=1, source_target_pairs={{0,4},{1,3},{2,6},{3,1},{4,0},{5,7},{6,2},{7,5},{8,12},{9,11},{10,... | collective-permute-start | bytes 2261000 | tf_op jit(solution)/shard_map/ppermute | solution.py:62
  50.2 13.5 %collective-permute-start.24 = (bf16[128,2944]{1,0:T(8,128)(2,1)S(1)}, bf16[128,2944]{1,0:T(8,128)(2,1)S(1)}, u32[]{:S(2)}, u32[]{:S(2)}) collective-permute-start(bf16[128,2944]{1,0:T(8,128)(2,1)S(1)} %pad_maximum_fusion.4), channel_id=1, source_target_pairs={{0,4},{1,3},{2,6},{3,1},{4,0},{5,7},{6,2},{7,5},{8,12},{9,11},{10,... | collective-permute-start | bytes 2261000 | tf_op jit(solution)/shard_map/ppermute | solution.py:62
  58.3 13.5 %collective-permute-start.8 = (bf16[128,2944]{1,0:T(8,128)(2,1)S(1)}, bf16[128,2944]{1,0:T(8,128)(2,1)S(1)}, u32[]{:S(2)}, u32[]{:S(2)}) collective-permute-start(bf16[128,2944]{1,0:T(8,128)(2,1)S(1)} %pad_maximum_fusion.2), channel_id=1, source_target_pairs={{0,4},{1,3},{2,6},{3,1},{4,0},{5,7},{6,2},{7,5},{8,12},{9,11},{10,... | collective-permute-start | bytes 2261000 | tf_op jit(solution)/shard_map/ppermute | solution.py:62
  59.2 2.0 copy-start.9
  59.4 21.4 %collective-permute-start.2 = (bf16[256,2944]{1,0:T(8,128)(2,1)S(1)}, bf16[256,2944]{1,0:T(8,128)(2,1)S(1)}, u32[]{:S(2)}, u32[]{:S(2)}) collective-permute-start(bf16[256,2944]{1,0:T(8,128)(2,1)S(1)} %pad_maximum_fusion), channel_id=1, source_target_pairs={{0,1},{1,0},{2,3},{3,2},{4,5},{5,4},{6,7},{7,6},{8,9},{9,8},{10,11... | collective-permute-start | bytes 4521992 | tf_op jit(solution)/shard_map/ppermute | solution.py:62
  63.6 21.7 %copy-start.2 = (bf16[256,2944]{1,0:T(8,128)(2,1)}, bf16[256,2944]{1,0:T(8,128)(2,1)S(1)}, u32[]{:S(2)}) copy-start(bf16[256,2944]{1,0:T(8,128)(2,1)S(1)} %constant_dynamic-update-slice_fusion.3) | copy-start | bytes 4521988
  63.6 21.7 %collective-permute-start.17 = (bf16[256,2944]{1,0:T(8,128)(2,1)S(1)}, bf16[256,2944]{1,0:T(8,128)(2,1)S(1)}, u32[]{:S(2)}, u32[]{:S(2)}) collective-permute-start(bf16[256,2944]{1,0:T(8,128)(2,1)S(1)} %constant_dynamic-update-slice_fusion.3), channel_id=1, source_target_pairs={{0,1},{1,0},{2,3},{3,2},{4,5},{5,4},{6,7},{7,6},{8,9},{9,8},{10,11... | collective-permute-start | bytes 4521992 | tf_op jit(solution)/shard_map/ppermute | solution.py:62
  63.8 21.5 %copy-start.3 = (bf16[256,2944]{1,0:T(8,128)(2,1)}, bf16[256,2944]{1,0:T(8,128)(2,1)S(1)}, u32[]{:S(2)}) copy-start(bf16[256,2944]{1,0:T(8,128)(2,1)S(1)} %constant_dynamic-update-slice_fusion.6) | copy-start | bytes 4521988
  63.8 21.5 %collective-permute-start.25 = (bf16[256,2944]{1,0:T(8,128)(2,1)S(1)}, bf16[256,2944]{1,0:T(8,128)(2,1)S(1)}, u32[]{:S(2)}, u32[]{:S(2)}) collective-permute-start(bf16[256,2944]{1,0:T(8,128)(2,1)S(1)} %constant_dynamic-update-slice_fusion.6), channel_id=1, source_target_pairs={{0,1},{1,0},{2,3},{3,2},{4,5},{5,4},{6,7},{7,6},{8,9},{9,8},{10,11... | collective-permute-start | bytes 4521992 | tf_op jit(solution)/shard_map/ppermute | solution.py:62
  71.8 13.5 %copy-start.4 = (bf16[256,2944]{1,0:T(8,128)(2,1)}, bf16[256,2944]{1,0:T(8,128)(2,1)S(1)}, u32[]{:S(2)}) copy-start(bf16[256,2944]{1,0:T(8,128)(2,1)S(1)} %constant_dynamic-update-slice_fusion) | copy-start | bytes 4521988
  71.8 11.2 %collective-permute-start.9 = (bf16[256,2944]{1,0:T(8,128)(2,1)S(1)}, bf16[256,2944]{1,0:T(8,128)(2,1)S(1)}, u32[]{:S(2)}, u32[]{:S(2)}) collective-permute-start(bf16[256,2944]{1,0:T(8,128)(2,1)S(1)} %constant_dynamic-update-slice_fusion), channel_id=1, source_target_pairs={{0,1},{1,0},{2,3},{3,2},{4,5},{5,4},{6,7},{7,6},{8,9},{9,8},{10,11... | collective-permute-start | bytes 4521992 | tf_op jit(solution)/shard_map/ppermute | solution.py:62
  80.7 4.6 %copy-start.5 = (bf16[256,2944]{1,0:T(8,128)(2,1)}, bf16[256,2944]{1,0:T(8,128)(2,1)S(1)}, u32[]{:S(2)}) copy-start(bf16[256,2944]{1,0:T(8,128)(2,1)S(1)} %collective-permute-done.2) | copy-start | bytes 4521988
  83.0 2.3 copy-start.8
  85.3 1.2 copy-start.6
  85.3 1.6 copy-start.7
  94.5 32.0 %collective-permute-start.10 = (bf16[256,2880]{0,1:T(8,128)(2,1)}, bf16[256,2880]{0,1:T(8,128)(2,1)}, u32[]{:S(2)}, u32[]{:S(2)}) collective-permute-start(bf16[256,2880]{0,1:T(8,128)(2,1)} %multiply_convert_fusion.2), channel_id=1, source_target_pairs={{0,1},{1,0},{2,3},{3,2},{4,5},{5,4},{6,7},{7,6},{8,9},{9,8},{10,11... | collective-permute-start | bytes 4423688 | tf_op jit(solution)/shard_map/ppermute | solution.py:62
  105.9 33.8 %collective-permute-start.18 = (bf16[256,2880]{0,1:T(8,128)(2,1)}, bf16[256,2880]{0,1:T(8,128)(2,1)}, u32[]{:S(2)}, u32[]{:S(2)}) collective-permute-start(bf16[256,2880]{0,1:T(8,128)(2,1)} %multiply_convert_fusion.1), channel_id=1, source_target_pairs={{0,1},{1,0},{2,3},{3,2},{4,5},{5,4},{6,7},{7,6},{8,9},{9,8},{10,11... | collective-permute-start | bytes 4423688 | tf_op jit(solution)/shard_map/ppermute | solution.py:62
  111.1 7.6 %copy-start.13 = (f32[256,640]{1,0:T(8,128)S(1)}, f32[256,640]{1,0:T(8,128)}, u32[]{:S(2)}) copy-start(f32[256,640]{1,0:T(8,128)} %fusion.24) | copy-start | bytes 1966084
  118.6 36.1 %collective-permute-start.26 = (bf16[256,2880]{0,1:T(8,128)(2,1)}, bf16[256,2880]{0,1:T(8,128)(2,1)}, u32[]{:S(2)}, u32[]{:S(2)}) collective-permute-start(bf16[256,2880]{0,1:T(8,128)(2,1)} %multiply_convert_fusion), channel_id=1, source_target_pairs={{0,1},{1,0},{2,3},{3,2},{4,5},{5,4},{6,7},{7,6},{8,9},{9,8},{10,11... | collective-permute-start | bytes 4423688 | tf_op jit(solution)/shard_map/ppermute | solution.py:62
  126.0 42.6 %collective-permute-start.3 = (bf16[256,2880]{0,1:T(8,128)(2,1)}, bf16[256,2880]{0,1:T(8,128)(2,1)}, u32[]{:S(2)}, u32[]{:S(2)}) collective-permute-start(bf16[256,2880]{0,1:T(8,128)(2,1)} %multiply_convert_fusion.3), channel_id=1, source_target_pairs={{0,1},{1,0},{2,3},{3,2},{4,5},{5,4},{6,7},{7,6},{8,9},{9,8},{10,11... | collective-permute-start | bytes 4423688 | tf_op jit(solution)/shard_map/ppermute | solution.py:62
  139.1 3.2 %copy-start.12 = (f32[256,640]{1,0:T(8,128)S(1)}, f32[256,640]{1,0:T(8,128)}, u32[]{:S(2)}) copy-start(f32[256,640]{1,0:T(8,128)} %fusion.18) | copy-start | bytes 1966084
  139.1 44.0 %collective-permute-start.11 = (bf16[128,2880]{0,1:T(8,128)(2,1)S(1)}, bf16[128,2880]{0,1:T(8,128)(2,1)}, u32[]{:S(2)}, u32[]{:S(2)}) collective-permute-start(bf16[128,2880]{0,1:T(8,128)(2,1)S(1)} %copy.66), channel_id=1, source_target_pairs={{0,4},{1,3},{2,6},{3,1},{4,0},{5,7},{6,2},{7,5},{8,12},{9,11},{10,... | collective-permute-start | bytes 2211848 | tf_op jit(solution)/shard_map/ppermute | solution.py:62
  153.2 4.1 %copy-start.11 = (f32[256,640]{1,0:T(8,128)S(1)}, f32[256,640]{1,0:T(8,128)}, u32[]{:S(2)}) copy-start(f32[256,640]{1,0:T(8,128)} %fusion.14) | copy-start | bytes 1966084
  153.2 34.1 %collective-permute-start.19 = (bf16[128,2880]{0,1:T(8,128)(2,1)}, bf16[128,2880]{0,1:T(8,128)(2,1)}, u32[]{:S(2)}, u32[]{:S(2)}) collective-permute-start(bf16[128,2880]{0,1:T(8,128)(2,1)} %copy.70), channel_id=1, source_target_pairs={{0,4},{1,3},{2,6},{3,1},{4,0},{5,7},{6,2},{7,5},{8,12},{9,11},{10,... | collective-permute-start | bytes 2211848 | tf_op jit(solution)/shard_map/ppermute | solution.py:62
  168.1 3.1 %copy-start.10 = (f32[256,640]{1,0:T(8,128)S(1)}, f32[256,640]{1,0:T(8,128)}, u32[]{:S(2)}) copy-start(f32[256,640]{1,0:T(8,128)} %fusion.26) | copy-start | bytes 1966084
  168.1 25.6 %collective-permute-start.27 = (bf16[128,2880]{0,1:T(8,128)(2,1)}, bf16[128,2880]{0,1:T(8,128)(2,1)}, u32[]{:S(2)}, u32[]{:S(2)}) collective-permute-start(bf16[128,2880]{0,1:T(8,128)(2,1)} %copy.74), channel_id=1, source_target_pairs={{0,4},{1,3},{2,6},{3,1},{4,0},{5,7},{6,2},{7,5},{8,12},{9,11},{10,... | collective-permute-start | bytes 2211848 | tf_op jit(solution)/shard_map/ppermute | solution.py:62
  181.6 18.4 %collective-permute-start.4 = (bf16[128,2880]{0,1:T(8,128)(2,1)}, bf16[128,2880]{0,1:T(8,128)(2,1)}, u32[]{:S(2)}, u32[]{:S(2)}) collective-permute-start(bf16[128,2880]{0,1:T(8,128)(2,1)} %copy.62), channel_id=1, source_target_pairs={{0,4},{1,3},{2,6},{3,1},{4,0},{5,7},{6,2},{7,5},{8,12},{9,11},{10,... | collective-permute-start | bytes 2211848 | tf_op jit(solution)/shard_map/ppermute | solution.py:62
  186.8 18.9 %collective-permute-start.12 = (bf16[64,2880]{1,0:T(8,128)(2,1)}, bf16[64,2880]{1,0:T(8,128)(2,1)S(1)}, u32[]{:S(2)}, u32[]{:S(2)}) collective-permute-start(bf16[64,2880]{1,0:T(8,128)(2,1)} %slice.284), channel_id=1, source_target_pairs={{0,2},{1,5},{2,0},{3,7},{4,6},{5,1},{6,4},{7,3},{8,10},{9,13},{10,... | collective-permute-start | bytes 1105928 | tf_op jit(solution)/shard_map/ppermute | solution.py:62
  192.1 17.3 %collective-permute-start.20 = (bf16[64,2880]{1,0:T(8,128)(2,1)}, bf16[64,2880]{1,0:T(8,128)(2,1)}, u32[]{:S(2)}, u32[]{:S(2)}) collective-permute-start(bf16[64,2880]{1,0:T(8,128)(2,1)} %slice.283), channel_id=1, source_target_pairs={{0,2},{1,5},{2,0},{3,7},{4,6},{5,1},{6,4},{7,3},{8,10},{9,13},{10,... | collective-permute-start | bytes 1105928 | tf_op jit(solution)/shard_map/ppermute | solution.py:62
  197.7 1.1 copy-start
  199.6 12.9 %collective-permute-start.28 = (bf16[64,2880]{1,0:T(8,128)(2,1)}, bf16[64,2880]{1,0:T(8,128)(2,1)}, u32[]{:S(2)}, u32[]{:S(2)}) collective-permute-start(bf16[64,2880]{1,0:T(8,128)(2,1)} %slice.282), channel_id=1, source_target_pairs={{0,2},{1,5},{2,0},{3,7},{4,6},{5,1},{6,4},{7,3},{8,10},{9,13},{10,... | collective-permute-start | bytes 1105928 | tf_op jit(solution)/shard_map/ppermute | solution.py:62
  204.0 8.4 %copy-start.1 = (f32[128,2880]{1,0:T(8,128)S(1)}, f32[128,2880]{1,0:T(8,128)}, u32[]{:S(2)}) copy-start(f32[128,2880]{1,0:T(8,128)} %copy-done) | copy-start | bytes 4423684
  204.0 11.0 %collective-permute-start.5 = (bf16[64,2880]{1,0:T(8,128)(2,1)S(1)}, bf16[64,2880]{1,0:T(8,128)(2,1)S(1)}, u32[]{:S(2)}, u32[]{:S(2)}) collective-permute-start(bf16[64,2880]{1,0:T(8,128)(2,1)S(1)} %slice.285), channel_id=1, source_target_pairs={{0,2},{1,5},{2,0},{3,7},{4,6},{5,1},{6,4},{7,3},{8,10},{9,13},{10,... | collective-permute-start | bytes 1105928 | tf_op jit(solution)/shard_map/ppermute | solution.py:62
  205.8 16.8 %collective-permute-start.13 = (bf16[64,2880]{1,0:T(8,128)(2,1)S(1)}, bf16[64,2880]{1,0:T(8,128)(2,1)S(1)}, u32[]{:S(2)}, u32[]{:S(2)}) collective-permute-start(bf16[64,2880]{1,0:T(8,128)(2,1)S(1)} %fusion.65), channel_id=1, source_target_pairs={{0,8},{1,9},{2,10},{3,11},{4,12},{5,13},{6,14},{7,15},{8,0},{9,1},... | collective-permute-start | bytes 1105928 | tf_op jit(solution)/shard_map/ppermute | solution.py:62
  210.5 28.8 %collective-permute-start.21 = (bf16[64,2880]{1,0:T(8,128)(2,1)S(1)}, bf16[64,2880]{1,0:T(8,128)(2,1)S(1)}, u32[]{:S(2)}, u32[]{:S(2)}) collective-permute-start(bf16[64,2880]{1,0:T(8,128)(2,1)S(1)} %fusion.64), channel_id=1, source_target_pairs={{0,16},{1,17},{2,18},{3,19},{4,20},{5,21},{6,22},{7,23},{8,24},{9,... | collective-permute-start | bytes 1105928 | tf_op jit(solution)/shard_map/ppermute | solution.py:62
  213.5 25.8 %collective-permute-start.29 = (bf16[64,2880]{1,0:T(8,128)(2,1)S(1)}, bf16[64,2880]{1,0:T(8,128)(2,1)S(1)}, u32[]{:S(2)}, u32[]{:S(2)}) collective-permute-start(bf16[64,2880]{1,0:T(8,128)(2,1)S(1)} %fusion.63), channel_id=1, source_target_pairs={{0,24},{1,25},{2,26},{3,27},{4,28},{5,29},{6,30},{7,31},{8,16},{9,... | collective-permute-start | bytes 1105928 | tf_op jit(solution)/shard_map/ppermute | solution.py:62

commit v2 on v1

--- a/solution.py
+++ b/solution.py
@@ -1,6 +1,10 @@
+import functools
+
 import jax
 import jax.numpy as jnp
 from jax import lax
+from jax.experimental import pallas as pl
+from jax.experimental.pallas import tpu as pltpu
 from jax.sharding import PartitionSpec as P
 
 SLICES = 4
@@ -51,6 +55,97 @@
     return mixed.astype(BF16)
 
 
+def pieces(extent, size):
+    return [(at, min(size, extent - at)) for at in range(0, extent, size)]
+
+
+def load_kernel(*refs):
+    count = len(refs) // 3
+    copies = [
+        pltpu.make_async_copy(refs[n].at[0], refs[count + n], refs[2 * count + n]) for n in range(count)
+    ]
+    for copy in copies:
+        copy.start()
+    for copy in copies:
+        copy.wait()
+
+
+def load_call(*arrays):
+    count = len(arrays)
+    return pl.pallas_call(
+        load_kernel,
+        out_shape=tuple(pltpu.VMEM(a.shape[1:], a.dtype) for a in arrays),
+        in_specs=[pl.BlockSpec(memory_space=pl.ANY)] * count,
+        out_specs=(pl.BlockSpec(memory_space=pltpu.VMEM),) * count,
+        scratch_shapes=[pltpu.SemaphoreType.DMA] * count,
+        compiler_params=pltpu.CompilerParams(vmem_limit_bytes=16 * 2**20),
+    )(*arrays)
+
+
+def rows_kernel(experts, tokens_ref, gain_ref, ids_ref, weights_ref, rows_ref):
+    tok_rows, features = tokens_ref.shape
+    values = tokens_ref[...].astype(F32)
+    mean_sq = jnp.sum(values * values, axis=-1, keepdims=True) * (1.0 / features)
+    rows_ref[:, :features] = (values * lax.rsqrt(mean_sq + 1e-05) * gain_ref[...]).astype(BF16)
+    lane = lax.broadcasted_iota(jnp.int32, (tok_rows, rows_ref.shape[1] - features), 1)
+    expert = lax.rem(lane, experts)
+    ids, chosen = ids_ref[...], weights_ref[...]
+    dense = jnp.zeros(lane.shape, F32)
+    for j in range(ids.shape[1]):
+        dense += jnp.where(expert == ids[:, j : j + 1], chosen[:, j : j + 1], 0.0)
+    high = dense.astype(BF16).astype(F32)
+    middle = (dense - high).astype(BF16).astype(F32)
+    low = dense - high - middle
+    term = jnp.where(lane < experts, high, jnp.where(lane < 2 * experts, middle, low))
+    rows_ref[:, features:] = jnp.where(lane < 3 * experts, term, 0.0).astype(BF16)
+
+
+def rows_call(tokens, norm_gain, expert_ids, gate_weights, experts, width):
+    return pl.pallas_call(
+        functools.partial(rows_kernel, experts),
+        out_shape=jax.ShapeDtypeStruct((tokens.shape[0], width), BF16),
+        in_specs=[pl.BlockSpec(memory_space=pltpu.VMEM)] * 4,
+        out_specs=pl.BlockSpec(memory_space=pltpu.VMEM),
+        compiler_params=pltpu.CompilerParams(vmem_limit_bytes=16 * 2**20),
+    )(tokens, norm_gain[None, :], expert_ids, gate_weights)
+
+
+def expert_kernel(x_ref, mask_ref, gate_ref, up_ref, down_ref, y_ref, hidden_ref):
+    features, hidden = gate_ref.shape
+    for at, size in pieces(hidden, 2 * LANES):
+        gate = jnp.dot(x_ref[:, :features], gate_ref[:, at : at + size], preferred_element_type=F32)
+        up = jnp.dot(x_ref[:, :features], up_ref[:, at : at + size], preferred_element_type=F32)
+        hidden_ref[:, at : at + size] = (gate * jax.nn.sigmoid(gate) * up).astype(BF16)
+    tail = features // LANES * LANES
+    parts = x_ref[:, tail : tail + LANES].astype(F32)
+    weight = jnp.sum(jnp.where(mask_ref[...] > 0.0, parts, 0.0), axis=1, keepdims=True)
+    for at, size in pieces(features, 6 * LANES):
+        y = lax.dot_general(
+            hidden_ref[...],
+            down_ref[at : at + size, :],
+            (((1,), (1,)), ((), ())),
+            preferred_element_type=F32,
+        )
+        y_ref[:, at : at + size] = (y * weight).astype(BF16)
+    y_ref[:, features:] = jnp.zeros((y_ref.shape[0], y_ref.shape[1] - features), BF16)
+
+
+def expert_call(x, mask, gate_w, up_w, down_t):
+    rows = x.shape[0]
+    features, hidden = gate_w.shape
+    return pl.pallas_call(
+        expert_kernel,
+        out_shape=jax.ShapeDtypeStruct(x.shape, BF16),
+        in_specs=[pl.BlockSpec(memory_space=pltpu.VMEM)] * 5,
+        out_specs=pl.BlockSpec(memory_space=pltpu.VMEM),
+        scratch_shapes=[pltpu.VMEM((rows, hidden), BF16)],
+        compiler_params=pltpu.CompilerParams(vmem_limit_bytes=16 * 2**20),
+        cost_estimate=pl.CostEstimate(
+            flops=6 * rows * features * hidden, bytes_accessed=4 * rows * features, transcendentals=0
+        ),
+    )(x, mask, gate_w, up_w, down_t)
+
+
 def local_cube(tokens, norm_gain, expert_ids, gate_weights, gate_proj, up_proj, down_proj):
     tok_rows, features = tokens.shape
     devices = lax.axis_size("ex")
@@ -73,39 +168,98 @@
     def slice_bits(j):
         return lambda i: i ^ (j * experts)
 
-    normed = normalise(tokens, norm_gain)
-    picked = expert_ids[:, :, None] == jnp.arange(experts, dtype=jnp.int32)[None, None, :]
-    dense = jnp.sum(jnp.where(picked, gate_weights[:, :, None], 0.0), axis=1)
-    high = lax.reduce_precision(dense, 8, 7)
-    rest = dense - high
-    middle = lax.reduce_precision(rest, 8, 7)
-    low = rest - middle
-    extra = [part.astype(BF16) for part in (high, middle, low)]
-    fill = jnp.zeros((tok_rows, width - features - 3 * experts), BF16)
-    rows = jnp.concatenate([normed, *extra, fill], axis=1)
-
-    def partial(block):
-        produced = expert_rows(block[:, :features], gate_proj[0], up_proj[0], down_proj[0])
-        parts = block[:, features : features + 3 * experts].astype(F32)
-        column = jnp.arange(3 * experts, dtype=jnp.int32) % experts == mine
-        weight = jnp.sum(jnp.where(column[None, :], parts, 0.0), axis=1, keepdims=True)
-        return produced * weight
-
-    blocks = [rows] + [swap(rows, slice_bits(j)) for j in range(1, SLICES)]
-    total = None
-    for j, block in enumerate(blocks):
-        half = jnp.concatenate([block, swap(block, first)], axis=0)
-        full = jnp.concatenate([half, swap(half, second)], axis=0)
-        other = swap(full, core)
-        back = swap(partial(other).astype(BF16), core)
-        sums = partial(full) + back.astype(F32)
-        cut = 2 * tok_rows
-        sums = sums[:cut] + swap(sums[cut:].astype(BF16), second).astype(F32)
-        sums = sums[:tok_rows] + swap(sums[tok_rows:].astype(BF16), first).astype(F32)
-        if j:
-            sums = swap(sums.astype(BF16), slice_bits(j)).astype(F32)
-        total = sums if total is None else total + sums
-    return total.astype(BF16)
+    rows = rows_call(tokens, norm_gain, expert_ids, gate_weights, experts, width)
+    lane = jnp.arange(LANES, dtype=jnp.int32)[None, :] - features % LANES
+    mask = ((lane >= 0) & (lane < 3 * experts) & (lane % experts == mine)).astype(F32)
+    stored = (gate_proj, up_proj, jnp.swapaxes(down_proj, 1, 2))
+    loaded = load_call(*(pltpu.with_memory_space_constraint(w, pltpu.HBM) for w in stored))
+    weights = [pltpu.with_memory_space_constraint(w, pltpu.VMEM) for w in loaded]
+
+    last = [mask]
+
+    def order(value):
+        value = lax.optimization_barrier((value, last[0]))[0]
+        last[0] = value
+        return value
+
+    def expert(x):
+        y = expert_call(x, mask, *weights)
+        last[0] = y
+        return y
+
+    def add(a, b):
+        return (a.astype(F32) + b.astype(F32)).astype(BF16)
+
+    cut = 2 * tok_rows
+    p1, p2, half, full, c, own, back, q2, q1, z, zb = ([None] * SLICES for _ in range(11))
+
+    def gather_half(j, block):
+        half[j] = jnp.concatenate([block, order(p1[j])], axis=0)
+        p2[j] = swap(half[j], second)
+
+    def gather_full(j):
+        full[j] = jnp.concatenate([half[j], order(p2[j])], axis=0)
+        c[j] = swap(full[j], core)
+
+    def run_own(j):
+        own[j] = expert(order(full[j]))
+
+    def run_other(j):
+        back[j] = swap(expert(order(c[j])), core)
+
+    def reduce_core(j):
+        arrived = order(back[j])
+        q2[j] = swap(add(own[j][cut:], arrived[cut:]), second)
+        own[j] = add(own[j][:cut], arrived[:cut])
+
+    def reduce_second(j):
+        arrived = order(q2[j])
+        q1[j] = swap(add(own[j][tok_rows:], arrived[tok_rows:]), first)
+        own[j] = add(own[j][:tok_rows], arrived[:tok_rows])
+
+    def reduce_first(j):
+        sums = add(own[j], order(q1[j]))
+        zb[j] = swap(sums, slice_bits(j)) if j else sums
+
+    p1[0] = swap(rows, first)
+    z[1] = order(swap(rows, slice_bits(1)))
+    gather_half(0, rows)
+    z[2] = swap(order(rows), slice_bits(2))
+    p1[1] = swap(z[1], first)
+    gather_full(0)
+    gather_half(1, z[1])
+    run_own(0)
+    z[2] = order(z[2])
+    p1[2] = swap(z[2], first)
+    z[3] = swap(order(rows), slice_bits(3))
+    run_other(0)
+    gather_full(1)
+    gather_half(2, z[2])
+    run_own(1)
+    run_other(1)
+    reduce_core(0)
+    gather_full(2)
+    z[3] = order(z[3])
+    p1[3] = swap(z[3], first)
+    run_own(2)
+    run_other(2)
+    gather_half(3, z[3])
+    reduce_core(1)
+    reduce_second(0)
+    gather_full(3)
+    run_own(3)
+    run_other(3)
+    reduce_core(2)
+    reduce_second(1)
+    reduce_core(3)
+    reduce_first(1)
+    reduce_second(2)
+    reduce_first(2)
+    reduce_second(3)
+    reduce_first(3)
+    reduce_first(0)
+    total = sum(order(zb[j]).astype(F32) for j in range(SLICES))
+    return total[:, :features].astype(BF16)
 
 
 def solution(mesh):

time: 244 us -> 197 us (0.81)
  the two profiles are of different devices: /device:TPU:0 before, /device:TPU:16 now
where the time goes in v2:
time: 197 us
  waiting for transfers between devices  128 us (65%)
  Pallas kernels  36 us (18%)
  starting transfers between devices  25.1 us (13%)
  other arithmetic  3.73 us (2%)
  local copies, waits for them, and re-layouts  3.68 us (2%)
    ppermute x30, waiting for transfers between devices, swap(): return lax.ppermute(array, 'ex', [(i, partner(i)) for i in range(devices)])  128 us
    pallas_call x8, Pallas kernels, expert_call(): pl.pallas_call(expert_kernel, out_shape=jax.ShapeDtypeStruct(x.shape, BF1...  31.4 us
    ppermute x30, starting transfers between devices, swap(): return lax.ppermute(array, 'ex', [(i, partner(i)) for i in range(devices)])  25.1 us
    pallas_call x1, Pallas kernels, load_call(): pl.pallas_call(load_kernel, out_shape=tuple((pltpu.VMEM(a.shape[1:], a.dt...  4.24 us
  transfers between devices with their start and end apart: 30, of which 18 were waited for; matrix products, arithmetic and copies ran while one was open for 1% of the time, Pallas kernels for 18%

profile of v2, /device:TPU:16, one launch (start us, length us, event | category | flops | bytes accessed | tf_op | source)
XLA Modules:
  0.0 196.9 jit_solution(2732893741965712403)
XLA Ops:
  0.0 0.7 broadcast_in_dim.4.gain_ref
  0.7 0.8 copy.8.ids_ref
  1.5 0.8 copy.9.weights_ref
  2.3 1.0 copy-done
  3.6 1.6 collective-permute-start.1
  5.2 1.5 collective-permute-start
  6.7 7.4 %collective-permute-done.1 = bf16[64,2944]{1,0:T(8,128)(2,1)S(1)} collective-permute-done((bf16[64,2944]{1,0:T(8,128)(2,1)S(1)}, bf16[64,2944]{1,0:T(8,128)(2,1)S(1)}, u32[]{:S(2)}, u32[]{:S(2)}) %collective-permute-start.1) | collective-permute-done | bytes 376864 | tf_op jit(solution)/shard_map/ppermute | solution.py:157
  14.2 1.6 collective-permute-start.2
  15.8 10.1 %collective-permute-done.2 = bf16[128,2944]{1,0:T(8,128)(2,1)S(1)} collective-permute-done((bf16[128,2944]{1,0:T(8,128)(2,1)S(1)}, bf16[128,2944]{1,0:T(8,128)(2,1)S(1)}, u32[]{:S(2)}, u32[]{:S(2)}) %collective-permute-start.2) | collective-permute-done | bytes 753696 | tf_op jit(solution)/shard_map/ppermute | solution.py:157
  26.1 1.6 collective-permute-start.3
  27.6 4.2 %shard_map.74 = (bf16[2880,640]{1,0:T(8,128)(2,1)S(1)}, bf16[2880,640]{1,0:T(8,128)(2,1)S(1)}, bf16[2880,640]{1,0:T(8,128)(2,1)S(1)}) custom-call(bf16[1,2880,640]{2,1,0:T(8,128)(2,1)} %refs_0_.1, bf16[1,2880,640]{2,1,0:T(8,128)(2,1)} %refs_1_.1, bf16[1,2880,640]{2,1,0:T(8,128)(2,1)} %bitcast.1), custom_call_target="tpu_custom_call" | custom-call | tf_op jit(solution)/shard_map/pallas_call | solution.py:75
  32.3 1.4 collective-permute-done.3
  33.8 1.6 collective-permute-start.7
  35.4 3.8 %shard_map.75 = bf16[256,2944]{1,0:T(8,128)(2,1)S(1)} custom-call(bf16[256,2944]{1,0:T(8,128)(2,1)S(1)} %pad_maximum_fusion.x_ref, f32[1,128]{1,0:T(1,128)S(1)} %and_convert_fusion.mask_ref, bf16[2880,640]{1,0:T(8,128)(2,1)S(1)} %get-tuple-element.51.gate_ref, bf16[2880,640]{1,0:T(8,128)(2,1)S(1)} %get-tuple-element.52.up_ref, ...), custom_call_target="tpu_custom_call" | custom-call | flops 2831155200 | bytes 2949120 | tf_op jit(solution)/shard_map/pallas_call | solution.py:136
  39.2 9.5 %collective-permute-done.5 = bf16[64,2944]{1,0:T(8,128)(2,1)S(1)} collective-permute-done((bf16[64,2944]{1,0:T(8,128)(2,1)S(1)}, bf16[64,2944]{1,0:T(8,128)(2,1)S(1)}, u32[]{:S(2)}, u32[]{:S(2)}) %collective-permute-start.5) | collective-permute-done | bytes 376864 | tf_op jit(solution)/shard_map/ppermute | solution.py:157
  48.8 3.9 %shard_map.76 = bf16[256,2944]{1,0:T(8,128)(2,1)S(1)} custom-call(bf16[256,2944]{1,0:T(8,128)(2,1)S(1)} %collective-permute-done.4.x_ref, f32[1,128]{1,0:T(1,128)S(1)} %and_convert_fusion.mask_ref, bf16[2880,640]{1,0:T(8,128)(2,1)S(1)} %get-tuple-element.51.gate_ref, bf16[2880,640]{1,0:T(8,128)(2,1)S(1)} %get-tuple-element.52.up_ref, ...), custom_call_target="tpu_custom_call" | custom-call | flops 2831155200 | bytes 2949120 | tf_op jit(solution)/shard_map/pallas_call | solution.py:136
  52.9 1.3 collective-permute-start.9
  54.2 6.4 %collective-permute-done.9 = bf16[64,2944]{1,0:T(8,128)(2,1)S(1)} collective-permute-done((bf16[64,2944]{1,0:T(8,128)(2,1)S(1)}, bf16[64,2944]{1,0:T(8,128)(2,1)S(1)}, u32[]{:S(2)}, u32[]{:S(2)}) %collective-permute-start.9) | collective-permute-done | bytes 376864 | tf_op jit(solution)/shard_map/ppermute | solution.py:157
  60.6 0.5 collective-permute-start.13
  61.1 3.9 %shard_map.77 = bf16[256,2944]{1,0:T(8,128)(2,1)S(1)} custom-call(bf16[256,2944]{1,0:T(8,128)(2,1)S(1)} %constant_dynamic-update-slice_fusion.x_ref, f32[1,128]{1,0:T(1,128)S(1)} %and_convert_fusion.mask_ref, bf16[2880,640]{1,0:T(8,128)(2,1)S(1)} %get-tuple-element.51.gate_ref, bf16[2880,640]{1,0:T(8,128)(2,1)S(1)} %get-tuple-element.52.up_ref, ...), custom_call_target="tpu_custom_call" | custom-call | flops 2831155200 | bytes 2949120 | tf_op jit(solution)/shard_map/pallas_call | solution.py:136
  65.1 4.1 %shard_map.78 = bf16[256,2944]{1,0:T(8,128)(2,1)S(1)} custom-call(bf16[256,2944]{1,0:T(8,128)(2,1)S(1)} %collective-permute-done.8.x_ref, f32[1,128]{1,0:T(1,128)S(1)} %and_convert_fusion.mask_ref, bf16[2880,640]{1,0:T(8,128)(2,1)S(1)} %get-tuple-element.51.gate_ref, bf16[2880,640]{1,0:T(8,128)(2,1)S(1)} %get-tuple-element.52.up_ref, ...), custom_call_target="tpu_custom_call" | custom-call | flops 2831155200 | bytes 2949120 | tf_op jit(solution)/shard_map/pallas_call | solution.py:136
  69.2 3.1 %collective-permute-done.13 = bf16[128,2944]{1,0:T(8,128)(2,1)S(1)} collective-permute-done((bf16[128,2944]{1,0:T(8,128)(2,1)S(1)}, bf16[128,2944]{1,0:T(8,128)(2,1)S(1)}, u32[]{:S(2)}, u32[]{:S(2)}) %collective-permute-start.13) | collective-permute-done | bytes 753696 | tf_op jit(solution)/shard_map/ppermute | solution.py:157
  72.5 2.7 %collective-permute-start.12 = (bf16[64,2944]{1,0:T(8,128)(2,1)S(1)}, bf16[64,2944]{1,0:T(8,128)(2,1)S(1)}, u32[]{:S(2)}, u32[]{:S(2)}) collective-permute-start(bf16[64,2944]{1,0:T(8,128)(2,1)S(1)} %shard_map.73), channel_id=1, source_target_pairs={{0,24},{1,25},{2,26},{3,27},{4,28},{5,29},{6,30},{7,31},{8,16},{9,... | collective-permute-start | bytes 1130504 | tf_op jit(solution)/shard_map/ppermute | solution.py:157
  75.7 16.9 %collective-permute-done.12 = bf16[64,2944]{1,0:T(8,128)(2,1)S(1)} collective-permute-done((bf16[64,2944]{1,0:T(8,128)(2,1)S(1)}, bf16[64,2944]{1,0:T(8,128)(2,1)S(1)}, u32[]{:S(2)}, u32[]{:S(2)}) %collective-permute-start.12) | collective-permute-done | bytes 376864 | tf_op jit(solution)/shard_map/ppermute | solution.py:157
  92.6 1.4 collective-permute-start.14
  93.9 0.6 collective-permute-start.10
  94.5 3.9 %shard_map.79 = bf16[256,2944]{1,0:T(8,128)(2,1)S(1)} custom-call(bf16[256,2944]{1,0:T(8,128)(2,1)S(1)} %constant_dynamic-update-slice_fusion.3.x_ref, f32[1,128]{1,0:T(1,128)S(1)} %and_convert_fusion.mask_ref, bf16[2880,640]{1,0:T(8,128)(2,1)S(1)} %get-tuple-element.51.gate_ref, bf16[2880,640]{1,0:T(8,128)(2,1)S(1)} %get-tuple-element.52.up_ref, ...), custom_call_target="tpu_custom_call" | custom-call | flops 2831155200 | bytes 2949120 | tf_op jit(solution)/shard_map/pallas_call | solution.py:136
  98.5 3.8 %shard_map.80 = bf16[256,2944]{1,0:T(8,128)(2,1)S(1)} custom-call(bf16[256,2944]{1,0:T(8,128)(2,1)S(1)} %collective-permute-done.15.x_ref, f32[1,128]{1,0:T(1,128)S(1)} %and_convert_fusion.mask_ref, bf16[2880,640]{1,0:T(8,128)(2,1)S(1)} %get-tuple-element.51.gate_ref, bf16[2880,640]{1,0:T(8,128)(2,1)S(1)} %get-tuple-element.52.up_ref, ...), custom_call_target="tpu_custom_call" | custom-call | flops 2831155200 | bytes 2949120 | tf_op jit(solution)/shard_map/pallas_call | solution.py:136
  102.3 1.9 collective-permute-done.14
  104.7 2.4 %collective-permute-done.10 = bf16[128,2944]{1,0:T(8,128)(2,1)S(1)} collective-permute-done((bf16[128,2944]{1,0:T(8,128)(2,1)S(1)}, bf16[128,2944]{1,0:T(8,128)(2,1)S(1)}, u32[]{:S(2)}, u32[]{:S(2)}) %collective-permute-start.10) | collective-permute-done | bytes 753696 | tf_op jit(solution)/shard_map/ppermute | solution.py:157
  107.1 8.8 %collective-permute-done.17 = bf16[128,2944]{1,0:T(8,128)(2,1)S(1)} collective-permute-done((bf16[128,2944]{1,0:T(8,128)(2,1)S(1)}, bf16[128,2944]{1,0:T(8,128)(2,1)S(1)}, u32[]{:S(2)}, u32[]{:S(2)}) %collective-permute-start.17) | collective-permute-done | bytes 753696 | tf_op jit(solution)/shard_map/ppermute | solution.py:157
  116.1 0.5 collective-permute-start.21
  117.4 4.1 %shard_map.81 = bf16[256,2944]{1,0:T(8,128)(2,1)S(1)} custom-call(bf16[256,2944]{1,0:T(8,128)(2,1)S(1)} %constant_dynamic-update-slice_fusion.6.x_ref, f32[1,128]{1,0:T(1,128)S(1)} %and_convert_fusion.mask_ref, bf16[2880,640]{1,0:T(8,128)(2,1)S(1)} %get-tuple-element.51.gate_ref, bf16[2880,640]{1,0:T(8,128)(2,1)S(1)} %get-tuple-element.52.up_ref, ...), custom_call_target="tpu_custom_call" | custom-call | flops 2831155200 | bytes 2949120 | tf_op jit(solution)/shard_map/pallas_call | solution.py:136
  121.5 3.9 %shard_map.82 = bf16[256,2944]{1,0:T(8,128)(2,1)S(1)} custom-call(bf16[256,2944]{1,0:T(8,128)(2,1)S(1)} %collective-permute-done.18.x_ref, f32[1,128]{1,0:T(1,128)S(1)} %and_convert_fusion.mask_ref, bf16[2880,640]{1,0:T(8,128)(2,1)S(1)} %get-tuple-element.51.gate_ref, bf16[2880,640]{1,0:T(8,128)(2,1)S(1)} %get-tuple-element.52.up_ref, ...), custom_call_target="tpu_custom_call" | custom-call | flops 2831155200 | bytes 2949120 | tf_op jit(solution)/shard_map/pallas_call | solution.py:136
  125.4 0.8 collective-permute-start.19
  126.3 2.4 %collective-permute-done.20 = bf16[128,2944]{1,0:T(8,128)(2,1)S(1)} collective-permute-done((bf16[128,2944]{1,0:T(8,128)(2,1)S(1)}, bf16[128,2944]{1,0:T(8,128)(2,1)S(1)}, u32[]{:S(2)}, u32[]{:S(2)}) %collective-permute-start.20) | collective-permute-done | bytes 753696 | tf_op jit(solution)/shard_map/ppermute | solution.py:157
  128.8 1.4 collective-permute-start.24
  130.6 0.7 collective-permute-start.23
  131.9 8.6 %collective-permute-done.24 = bf16[64,2944]{1,0:T(8,128)(2,1)S(1)} collective-permute-done((bf16[64,2944]{1,0:T(8,128)(2,1)S(1)}, bf16[64,2944]{1,0:T(8,128)(2,1)S(1)}, u32[]{:S(2)}, u32[]{:S(2)}) %collective-permute-start.24) | collective-permute-done | bytes 376864 | tf_op jit(solution)/shard_map/ppermute | solution.py:157
  141.2 5.6 %collective-permute-done.23 = bf16[128,2944]{1,0:T(8,128)(2,1)S(1)} collective-permute-done((bf16[128,2944]{1,0:T(8,128)(2,1)S(1)}, bf16[128,2944]{1,0:T(8,128)(2,1)S(1)}, u32[]{:S(2)}, u32[]{:S(2)}) %collective-permute-start.23) | collective-permute-done | bytes 753696 | tf_op jit(solution)/shard_map/ppermute | solution.py:157
  146.9 1.4 collective-permute-start.25
  148.6 10.1 %collective-permute-done.25 = bf16[64,2944]{1,0:T(8,128)(2,1)S(1)} collective-permute-done((bf16[64,2944]{1,0:T(8,128)(2,1)S(1)}, bf16[64,2944]{1,0:T(8,128)(2,1)S(1)}, u32[]{:S(2)}, u32[]{:S(2)}) %collective-permute-start.25) | collective-permute-done | bytes 376864 | tf_op jit(solution)/shard_map/ppermute | solution.py:157
  159.0 1.4 collective-permute-start.26
  160.7 6.0 %collective-permute-done.26 = bf16[64,2944]{1,0:T(8,128)(2,1)S(1)} collective-permute-done((bf16[64,2944]{1,0:T(8,128)(2,1)S(1)}, bf16[64,2944]{1,0:T(8,128)(2,1)S(1)}, u32[]{:S(2)}, u32[]{:S(2)}) %collective-permute-start.26) | collective-permute-done | bytes 376864 | tf_op jit(solution)/shard_map/ppermute | solution.py:157
  166.9 1.9 collective-permute-start.29
  168.9 17.0 %collective-permute-done.28 = bf16[64,2944]{1,0:T(8,128)(2,1)S(1)} collective-permute-done((bf16[64,2944]{1,0:T(8,128)(2,1)S(1)}, bf16[64,2944]{1,0:T(8,128)(2,1)S(1)}, u32[]{:S(2)}, u32[]{:S(2)}) %collective-permute-start.28) | collective-permute-done | bytes 376864 | tf_op jit(solution)/shard_map/ppermute | solution.py:157
  185.9 10.1 %collective-permute-done.29 = bf16[64,2944]{1,0:T(8,128)(2,1)S(1)} collective-permute-done((bf16[64,2944]{1,0:T(8,128)(2,1)S(1)}, bf16[64,2944]{1,0:T(8,128)(2,1)S(1)}, u32[]{:S(2)}, u32[]{:S(2)}) %collective-permute-start.29) | collective-permute-done | bytes 376864 | tf_op jit(solution)/shard_map/ppermute | solution.py:157
  196.0 0.9 add_convert_fusion.8
  (55 shorter events, 6.6 us)
Async XLA Ops:
  2.3 1.0 copy-start
  3.6 10.5 %collective-permute-start.1 = (bf16[64,2944]{1,0:T(8,128)(2,1)S(1)}, bf16[64,2944]{1,0:T(8,128)(2,1)S(1)}, u32[]{:S(2)}, u32[]{:S(2)}) collective-permute-start(bf16[64,2944]{1,0:T(8,128)(2,1)S(1)} %shard_map.73), channel_id=1, source_target_pairs={{0,8},{1,9},{2,10},{3,11},{4,12},{5,13},{6,14},{7,15},{8,0},{9,1},... | collective-permute-start | bytes 1130504 | tf_op jit(solution)/shard_map/ppermute | solution.py:157
  5.2 8.9 %collective-permute-start = (bf16[64,2944]{1,0:T(8,128)(2,1)S(1)}, bf16[64,2944]{1,0:T(8,128)(2,1)S(1)}, u32[]{:S(2)}, u32[]{:S(2)}) collective-permute-start(bf16[64,2944]{1,0:T(8,128)(2,1)S(1)} %shard_map.73), channel_id=1, source_target_pairs={{0,2},{1,5},{2,0},{3,7},{4,6},{5,1},{6,4},{7,3},{8,10},{9,13},{10,... | collective-permute-start | bytes 1130504 | tf_op jit(solution)/shard_map/ppermute | solution.py:157
  14.2 11.7 %collective-permute-start.2 = (bf16[128,2944]{1,0:T(8,128)(2,1)S(1)}, bf16[128,2944]{1,0:T(8,128)(2,1)S(1)}, u32[]{:S(2)}, u32[]{:S(2)}) collective-permute-start(bf16[128,2944]{1,0:T(8,128)(2,1)S(1)} %pad_maximum_fusion.1), channel_id=1, source_target_pairs={{0,4},{1,3},{2,6},{3,1},{4,0},{5,7},{6,2},{7,5},{8,12},{9,11},{10,... | collective-permute-start | bytes 2261000 | tf_op jit(solution)/shard_map/ppermute | solution.py:157
  26.0 22.8 %collective-permute-start.4 = (bf16[256,2944]{1,0:T(8,128)(2,1)S(1)}, bf16[256,2944]{1,0:T(8,128)(2,1)S(1)}, u32[]{:S(2)}, u32[]{:S(2)}) collective-permute-start(bf16[256,2944]{1,0:T(8,128)(2,1)S(1)} %pad_maximum_fusion.x_ref), channel_id=1, source_target_pairs={{0,1},{1,0},{2,3},{3,2},{4,5},{5,4},{6,7},{7,6},{8,9},{9,8},{10,11... | collective-permute-start | bytes 4521992 | tf_op jit(solution)/shard_map/ppermute | solution.py:157
  26.1 7.7 %collective-permute-start.3 = (bf16[64,2944]{1,0:T(8,128)(2,1)S(1)}, bf16[64,2944]{1,0:T(8,128)(2,1)S(1)}, u32[]{:S(2)}, u32[]{:S(2)}) collective-permute-start(bf16[64,2944]{1,0:T(8,128)(2,1)S(1)} %collective-permute-done.1), channel_id=1, source_target_pairs={{0,2},{1,5},{2,0},{3,7},{4,6},{5,1},{6,4},{7,3},{8,10},{9,13},{10,... | collective-permute-start | bytes 1130504 | tf_op jit(solution)/shard_map/ppermute | solution.py:157
  31.9 16.8 %collective-permute-start.5 = (bf16[64,2944]{1,0:T(8,128)(2,1)S(1)}, bf16[64,2944]{1,0:T(8,128)(2,1)S(1)}, u32[]{:S(2)}, u32[]{:S(2)}) collective-permute-start(bf16[64,2944]{1,0:T(8,128)(2,1)S(1)} %shard_map.73), channel_id=1, source_target_pairs={{0,16},{1,17},{2,18},{3,19},{4,20},{5,21},{6,22},{7,23},{8,24},{9,... | collective-permute-start | bytes 1130504 | tf_op jit(solution)/shard_map/ppermute | solution.py:157
  33.8 18.9 %collective-permute-start.7 = (bf16[128,2944]{1,0:T(8,128)(2,1)S(1)}, bf16[128,2944]{1,0:T(8,128)(2,1)S(1)}, u32[]{:S(2)}, u32[]{:S(2)}) collective-permute-start(bf16[128,2944]{1,0:T(8,128)(2,1)S(1)} %pad_maximum_fusion.2), channel_id=1, source_target_pairs={{0,4},{1,3},{2,6},{3,1},{4,0},{5,7},{6,2},{7,5},{8,12},{9,11},{10,... | collective-permute-start | bytes 2261000 | tf_op jit(solution)/shard_map/ppermute | solution.py:157
  52.8 12.3 %collective-permute-start.8 = (bf16[256,2944]{1,0:T(8,128)(2,1)S(1)}, bf16[256,2944]{1,0:T(8,128)(2,1)S(1)}, u32[]{:S(2)}, u32[]{:S(2)}) collective-permute-start(bf16[256,2944]{1,0:T(8,128)(2,1)S(1)} %constant_dynamic-update-slice_fusion.x_ref), channel_id=1, source_target_pairs={{0,1},{1,0},{2,3},{3,2},{4,5},{5,4},{6,7},{7,6},{8,9},{9,8},{10,11... | collective-permute-start | bytes 4521992 | tf_op jit(solution)/shard_map/ppermute | solution.py:157
  52.9 7.7 %collective-permute-start.9 = (bf16[64,2944]{1,0:T(8,128)(2,1)S(1)}, bf16[64,2944]{1,0:T(8,128)(2,1)S(1)}, u32[]{:S(2)}, u32[]{:S(2)}) collective-permute-start(bf16[64,2944]{1,0:T(8,128)(2,1)S(1)} %collective-permute-done.5), channel_id=1, source_target_pairs={{0,2},{1,5},{2,0},{3,7},{4,6},{5,1},{6,4},{7,3},{8,10},{9,13},{10,... | collective-permute-start | bytes 1130504 | tf_op jit(solution)/shard_map/ppermute | solution.py:157
  54.1 15.0 %collective-permute-start.6 = (bf16[256,2944]{1,0:T(8,128)(2,1)S(1)}, bf16[256,2944]{1,0:T(8,128)(2,1)S(1)}, u32[]{:S(2)}, u32[]{:S(2)}) collective-permute-start(bf16[256,2944]{1,0:T(8,128)(2,1)S(1)} %shard_map.76), channel_id=1, source_target_pairs={{0,1},{1,0},{2,3},{3,2},{4,5},{5,4},{6,7},{7,6},{8,9},{9,8},{10,11... | collective-permute-start | bytes 4521992 | tf_op jit(solution)/shard_map/ppermute | solution.py:157
  60.6 11.7 %collective-permute-start.13 = (bf16[128,2944]{1,0:T(8,128)(2,1)S(1)}, bf16[128,2944]{1,0:T(8,128)(2,1)S(1)}, u32[]{:S(2)}, u32[]{:S(2)}) collective-permute-start(bf16[128,2944]{1,0:T(8,128)(2,1)S(1)} %pad_maximum_fusion.3), channel_id=1, source_target_pairs={{0,4},{1,3},{2,6},{3,1},{4,0},{5,7},{6,2},{7,5},{8,12},{9,11},{10,... | collective-permute-start | bytes 2261000 | tf_op jit(solution)/shard_map/ppermute | solution.py:157
  72.4 26.1 %collective-permute-start.15 = (bf16[256,2944]{1,0:T(8,128)(2,1)S(1)}, bf16[256,2944]{1,0:T(8,128)(2,1)S(1)}, u32[]{:S(2)}, u32[]{:S(2)}) collective-permute-start(bf16[256,2944]{1,0:T(8,128)(2,1)S(1)} %constant_dynamic-update-slice_fusion.3.x_ref), channel_id=1, source_target_pairs={{0,1},{1,0},{2,3},{3,2},{4,5},{5,4},{6,7},{7,6},{8,9},{9,8},{10,11... | collective-permute-start | bytes 4521992 | tf_op jit(solution)/shard_map/ppermute | solution.py:157
  72.5 20.1 %collective-permute-start.12 = (bf16[64,2944]{1,0:T(8,128)(2,1)S(1)}, bf16[64,2944]{1,0:T(8,128)(2,1)S(1)}, u32[]{:S(2)}, u32[]{:S(2)}) collective-permute-start(bf16[64,2944]{1,0:T(8,128)(2,1)S(1)} %shard_map.73), channel_id=1, source_target_pairs={{0,24},{1,25},{2,26},{3,27},{4,28},{5,29},{6,30},{7,31},{8,16},{9,... | collective-permute-start | bytes 1130504 | tf_op jit(solution)/shard_map/ppermute | solution.py:157
  75.1 29.6 %collective-permute-start.11 = (bf16[256,2944]{1,0:T(8,128)(2,1)S(1)}, bf16[256,2944]{1,0:T(8,128)(2,1)S(1)}, u32[]{:S(2)}, u32[]{:S(2)}) collective-permute-start(bf16[256,2944]{1,0:T(8,128)(2,1)S(1)} %shard_map.78), channel_id=1, source_target_pairs={{0,1},{1,0},{2,3},{3,2},{4,5},{5,4},{6,7},{7,6},{8,9},{9,8},{10,11... | collective-permute-start | bytes 4521992 | tf_op jit(solution)/shard_map/ppermute | solution.py:157
  92.6 11.6 %collective-permute-start.14 = (bf16[64,2944]{1,0:T(8,128)(2,1)S(1)}, bf16[64,2944]{1,0:T(8,128)(2,1)S(1)}, u32[]{:S(2)}, u32[]{:S(2)}) collective-permute-start(bf16[64,2944]{1,0:T(8,128)(2,1)S(1)} %collective-permute-done.12), channel_id=1, source_target_pairs={{0,2},{1,5},{2,0},{3,7},{4,6},{5,1},{6,4},{7,3},{8,10},{9,13},{10,... | collective-permute-start | bytes 1130504 | tf_op jit(solution)/shard_map/ppermute | solution.py:157
  93.9 13.2 %collective-permute-start.10 = (bf16[128,2944]{1,0:T(8,128)(2,1)S(1)}, bf16[128,2944]{1,0:T(8,128)(2,1)S(1)}, u32[]{:S(2)}, u32[]{:S(2)}) collective-permute-start(bf16[128,2944]{1,0:T(8,128)(2,1)S(1)} %get-tuple-element.86), channel_id=1, source_target_pairs={{0,4},{1,3},{2,6},{3,1},{4,0},{5,7},{6,2},{7,5},{8,12},{9,11},{10,... | collective-permute-start | bytes 2261000 | tf_op jit(solution)/shard_map/ppermute | solution.py:157
  104.2 11.7 %collective-permute-start.17 = (bf16[128,2944]{1,0:T(8,128)(2,1)S(1)}, bf16[128,2944]{1,0:T(8,128)(2,1)S(1)}, u32[]{:S(2)}, u32[]{:S(2)}) collective-permute-start(bf16[128,2944]{1,0:T(8,128)(2,1)S(1)} %pad_maximum_fusion.4), channel_id=1, source_target_pairs={{0,4},{1,3},{2,6},{3,1},{4,0},{5,7},{6,2},{7,5},{8,12},{9,11},{10,... | collective-permute-start | bytes 2261000 | tf_op jit(solution)/shard_map/ppermute | solution.py:157
  116.0 5.5 %collective-permute-start.18 = (bf16[256,2944]{1,0:T(8,128)(2,1)S(1)}, bf16[256,2944]{1,0:T(8,128)(2,1)S(1)}, u32[]{:S(2)}, u32[]{:S(2)}) collective-permute-start(bf16[256,2944]{1,0:T(8,128)(2,1)S(1)} %constant_dynamic-update-slice_fusion.6.x_ref), channel_id=1, source_target_pairs={{0,1},{1,0},{2,3},{3,2},{4,5},{5,4},{6,7},{7,6},{8,9},{9,8},{10,11... | collective-permute-start | bytes 4521992 | tf_op jit(solution)/shard_map/ppermute | solution.py:157
  116.1 10.2 %collective-permute-start.21 = (bf16[256,2944]{1,0:T(8,128)(2,1)S(1)}, bf16[256,2944]{1,0:T(8,128)(2,1)S(1)}, u32[]{:S(2)}, u32[]{:S(2)}) collective-permute-start(bf16[256,2944]{1,0:T(8,128)(2,1)S(1)} %shard_map.80), channel_id=1, source_target_pairs={{0,1},{1,0},{2,3},{3,2},{4,5},{5,4},{6,7},{7,6},{8,9},{9,8},{10,11... | collective-permute-start | bytes 4521992 | tf_op jit(solution)/shard_map/ppermute | solution.py:157
  117.0 11.7 %collective-permute-start.20 = (bf16[128,2944]{1,0:T(8,128)(2,1)S(1)}, bf16[128,2944]{1,0:T(8,128)(2,1)S(1)}, u32[]{:S(2)}, u32[]{:S(2)}) collective-permute-start(bf16[128,2944]{1,0:T(8,128)(2,1)S(1)} %get-tuple-element.88), channel_id=1, source_target_pairs={{0,4},{1,3},{2,6},{3,1},{4,0},{5,7},{6,2},{7,5},{8,12},{9,11},{10,... | collective-permute-start | bytes 2261000 | tf_op jit(solution)/shard_map/ppermute | solution.py:157
  125.4 6.5 %collective-permute-start.19 = (bf16[256,2944]{1,0:T(8,128)(2,1)S(1)}, bf16[256,2944]{1,0:T(8,128)(2,1)S(1)}, u32[]{:S(2)}, u32[]{:S(2)}) collective-permute-start(bf16[256,2944]{1,0:T(8,128)(2,1)S(1)} %shard_map.82), channel_id=1, source_target_pairs={{0,1},{1,0},{2,3},{3,2},{4,5},{5,4},{6,7},{7,6},{8,9},{9,8},{10,11... | collective-permute-start | bytes 4521992 | tf_op jit(solution)/shard_map/ppermute | solution.py:157
  128.8 11.7 %collective-permute-start.24 = (bf16[64,2944]{1,0:T(8,128)(2,1)S(1)}, bf16[64,2944]{1,0:T(8,128)(2,1)S(1)}, u32[]{:S(2)}, u32[]{:S(2)}) collective-permute-start(bf16[64,2944]{1,0:T(8,128)(2,1)S(1)} %add_convert_fusion.18), channel_id=1, source_target_pairs={{0,2},{1,5},{2,0},{3,7},{4,6},{5,1},{6,4},{7,3},{8,10},{9,13},{10,... | collective-permute-start | bytes 1130504 | tf_op jit(solution)/shard_map/ppermute | solution.py:157
  130.6 16.2 %collective-permute-start.23 = (bf16[128,2944]{1,0:T(8,128)(2,1)S(1)}, bf16[128,2944]{1,0:T(8,128)(2,1)S(1)}, u32[]{:S(2)}, u32[]{:S(2)}) collective-permute-start(bf16[128,2944]{1,0:T(8,128)(2,1)S(1)} %get-tuple-element.89), channel_id=1, source_target_pairs={{0,4},{1,3},{2,6},{3,1},{4,0},{5,7},{6,2},{7,5},{8,12},{9,11},{10,... | collective-permute-start | bytes 2261000 | tf_op jit(solution)/shard_map/ppermute | solution.py:157
  131.4 35.4 %collective-permute-start.16 = (bf16[64,2944]{1,0:T(8,128)(2,1)S(1)}, bf16[64,2944]{1,0:T(8,128)(2,1)S(1)}, u32[]{:S(2)}, u32[]{:S(2)}) collective-permute-start(bf16[64,2944]{1,0:T(8,128)(2,1)S(1)} %add_convert_fusion.19), channel_id=1, source_target_pairs={{0,2},{1,5},{2,0},{3,7},{4,6},{5,1},{6,4},{7,3},{8,10},{9,13},{10,... | collective-permute-start | bytes 1130504 | tf_op jit(solution)/shard_map/ppermute | solution.py:157
  140.8 18.1 %collective-permute-start.22 = (bf16[128,2944]{1,0:T(8,128)(2,1)S(1)}, bf16[128,2944]{1,0:T(8,128)(2,1)S(1)}, u32[]{:S(2)}, u32[]{:S(2)}) collective-permute-start(bf16[128,2944]{1,0:T(8,128)(2,1)S(1)} %get-tuple-element.91), channel_id=1, source_target_pairs={{0,4},{1,3},{2,6},{3,1},{4,0},{5,7},{6,2},{7,5},{8,12},{9,11},{10,... | collective-permute-start | bytes 2261000 | tf_op jit(solution)/shard_map/ppermute | solution.py:157
  146.9 11.8 %collective-permute-start.25 = (bf16[64,2944]{1,0:T(8,128)(2,1)S(1)}, bf16[64,2944]{1,0:T(8,128)(2,1)S(1)}, u32[]{:S(2)}, u32[]{:S(2)}) collective-permute-start(bf16[64,2944]{1,0:T(8,128)(2,1)S(1)} %add_convert_fusion.17), channel_id=1, source_target_pairs={{0,2},{1,5},{2,0},{3,7},{4,6},{5,1},{6,4},{7,3},{8,10},{9,13},{10,... | collective-permute-start | bytes 1130504 | tf_op jit(solution)/shard_map/ppermute | solution.py:157
  148.5 20.4 %collective-permute-start.27 = (bf16[64,2944]{1,0:T(8,128)(2,1)S(1)}, bf16[64,2944]{1,0:T(8,128)(2,1)S(1)}, u32[]{:S(2)}, u32[]{:S(2)}) collective-permute-start(bf16[64,2944]{1,0:T(8,128)(2,1)S(1)} %add_convert_fusion.13), channel_id=1, source_target_pairs={{0,8},{1,9},{2,10},{3,11},{4,12},{5,13},{6,14},{7,15},{8,0},{9,1},... | collective-permute-start | bytes 1130504 | tf_op jit(solution)/shard_map/ppermute | solution.py:157
  159.0 7.7 %collective-permute-start.26 = (bf16[64,2944]{1,0:T(8,128)(2,1)S(1)}, bf16[64,2944]{1,0:T(8,128)(2,1)S(1)}, u32[]{:S(2)}, u32[]{:S(2)}) collective-permute-start(bf16[64,2944]{1,0:T(8,128)(2,1)S(1)} %add_convert_fusion.16), channel_id=1, source_target_pairs={{0,2},{1,5},{2,0},{3,7},{4,6},{5,1},{6,4},{7,3},{8,10},{9,13},{10,... | collective-permute-start | bytes 1130504 | tf_op jit(solution)/shard_map/ppermute | solution.py:157
  160.6 25.3 %collective-permute-start.28 = (bf16[64,2944]{1,0:T(8,128)(2,1)S(1)}, bf16[64,2944]{1,0:T(8,128)(2,1)S(1)}, u32[]{:S(2)}, u32[]{:S(2)}) collective-permute-start(bf16[64,2944]{1,0:T(8,128)(2,1)S(1)} %add_convert_fusion.11), channel_id=1, source_target_pairs={{0,16},{1,17},{2,18},{3,19},{4,20},{5,21},{6,22},{7,23},{8,24},{9,... | collective-permute-start | bytes 1130504 | tf_op jit(solution)/shard_map/ppermute | solution.py:157
  166.9 29.1 %collective-permute-start.29 = (bf16[64,2944]{1,0:T(8,128)(2,1)S(1)}, bf16[64,2944]{1,0:T(8,128)(2,1)S(1)}, u32[]{:S(2)}, u32[]{:S(2)}) collective-permute-start(bf16[64,2944]{1,0:T(8,128)(2,1)S(1)} %add_convert_fusion.9), channel_id=1, source_target_pairs={{0,24},{1,25},{2,26},{3,27},{4,28},{5,29},{6,30},{7,31},{8,16},{9,... | collective-permute-start | bytes 1130504 | tf_op jit(solution)/shard_map/ppermute | solution.py:157

commit v3 on v2

v3 whole, which is shorter than its diff:
```python
import functools

import jax
import jax.numpy as jnp
from jax import lax
from jax.experimental import pallas as pl
from jax.experimental.pallas import tpu as pltpu
from jax.sharding import PartitionSpec as P

SLICES = 4
LANES = 128
UNITS = 2 * LANES
COLUMNS = 6 * LANES
BF16 = jnp.bfloat16
F32 = jnp.float32


def normalise(tokens, norm_gain):
    values = tokens.astype(F32)
    mean_sq = jnp.mean(values * values, axis=-1, keepdims=True)
    return (values * lax.rsqrt(mean_sq + 1e-05) * norm_gain).astype(BF16)


def expert_rows(flat_rows, gate_w, up_w, down_w):
    gate_act = jnp.dot(flat_rows, gate_w, preferred_element_type=F32)
    up_act = jnp.dot(flat_rows, up_w, preferred_element_type=F32)
    hidden = (jax.nn.silu(gate_act) * up_act).astype(BF16)
    return jnp.dot(hidden, down_w, preferred_element_type=F32)


def local_general(tokens, norm_gain, expert_ids, gate_weights, gate_proj, up_proj, down_proj):
    tok_rows, features = tokens.shape
    picks = expert_ids.shape[1]
    devices = lax.axis_size("ex")
    experts = devices // SLICES
    capacity = min(tok_rows, 4 * ((3 * tok_rows * picks + 8 * experts - 1) // (8 * experts)))
    normed = normalise(tokens, norm_gain)
    padded = jnp.concatenate([normed, jnp.zeros((1, features), normed.dtype)], axis=0)
    flat_expert = expert_ids.reshape(-1)
    onehot = (flat_expert[:, None] == jnp.arange(experts, dtype=jnp.int32)[None, :]).astype(
        jnp.int32
    )
    before = jnp.cumsum(onehot, axis=0) - onehot
    rank_in = jnp.sum(before * onehot, axis=1)
    token_index = jnp.arange(tok_rows * picks, dtype=jnp.int32) // picks
    slot_index = flat_expert * capacity + rank_in
    table = jnp.full((experts * capacity,), tok_rows, jnp.int32).at[slot_index].set(token_index)
    buffer = padded[table].reshape(experts, capacity, features)
    outgoing = jnp.tile(buffer, (SLICES, 1, 1))
    arrived = lax.all_to_all(outgoing, "ex", split_axis=0, concat_axis=0, tiled=True)
    partials = expert_rows(arrived.reshape(-1, features), gate_proj[0], up_proj[0], down_proj[0])
    partials = partials.reshape(devices, capacity, features)
    returned = lax.all_to_all(partials, "ex", split_axis=0, concat_axis=0, tiled=True)
    summed = jnp.sum(returned.reshape(SLICES, experts * capacity, features), axis=0)
    gathered = summed[slot_index].reshape(tok_rows, picks, features)
    mixed = jnp.sum(gathered * gate_weights[:, :, None], axis=1)
    return mixed.astype(BF16)


def pieces(extent, size):
    return [(at, min(size, extent - at)) for at in range(0, extent, size)]


def rows_kernel(
    experts, tokens_any, gain_any, ids_any, weights_any, rows_ref, tokens_ref, gain_ref, ids_ref, weights_ref, sems
):
    copies = [
        pltpu.make_async_copy(tokens_any, tokens_ref, sems.at[0]),
        pltpu.make_async_copy(gain_any, gain_ref, sems.at[1]),
        pltpu.make_async_copy(ids_any, ids_ref, sems.at[2]),
        pltpu.make_async_copy(weights_any, weights_ref, sems.at[3]),
    ]
    for copy in copies:
        copy.start()
    for copy in copies:
        copy.wait()
    tok_rows, features = tokens_ref.shape
    extra = rows_ref.shape[1] - features
    values = tokens_ref[...].astype(F32)
    mean_sq = jnp.sum(values * values, axis=-1, keepdims=True) * (1.0 / features)
    rows_ref[:, :features] = (values * lax.rsqrt(mean_sq + 1e-05) * gain_ref[...][None, :]).astype(BF16)
    place = lax.broadcasted_iota(jnp.int32, (extra, tok_rows), 0)
    expert = lax.rem(place, experts)
    dense = jnp.zeros((extra, tok_rows), F32)
    for j in range(ids_ref.shape[0]):
        dense += jnp.where(expert == ids_ref[j : j + 1, :], weights_ref[j : j + 1, :], 0.0)
    high = dense.astype(BF16).astype(F32)
    middle = (dense - high).astype(BF16).astype(F32)
    low = dense - high - middle
    term = jnp.where(place < experts, high, jnp.where(place < 2 * experts, middle, low))
    term = jnp.where(place < 3 * experts, term, 0.0).astype(BF16)
    row = lax.broadcasted_iota(jnp.int32, (extra, extra), 0)
    column = lax.broadcasted_iota(jnp.int32, (extra, extra), 1)
    unit = jnp.where(row == column, 1.0, 0.0).astype(BF16)
    turned = lax.dot_general(term, unit, (((0,), (0,)), ((), ())), preferred_element_type=F32)
    rows_ref[:, features:] = turned.astype(BF16)


def rows_call(tokens, norm_gain, expert_ids, gate_weights, experts, width):
    arrays = (tokens, norm_gain, jnp.swapaxes(expert_ids, 0, 1), jnp.swapaxes(gate_weights, 0, 1))
    return pl.pallas_call(
        functools.partial(rows_kernel, experts),
        out_shape=jax.ShapeDtypeStruct((tokens.shape[0], width), BF16),
        in_specs=[pl.BlockSpec(memory_space=pl.ANY)] * 4,
        out_specs=pl.BlockSpec(memory_space=pltpu.VMEM),
        scratch_shapes=[pltpu.VMEM(a.shape, a.dtype) for a in arrays] + [pltpu.SemaphoreType.DMA((4,))],
        compiler_params=pltpu.CompilerParams(vmem_limit_bytes=16 * 2**20),
    )(*(pltpu.with_memory_space_constraint(a, pltpu.HBM) for a in arrays))


def expert_body(xa_ref, xb_ref, mask_ref, gate_ref, up_ref, down_ref, ya_ref, yb_ref, x_ref, hidden_ref, ready):
    features, hidden = gate_ref.shape
    rows = xa_ref.shape[0]
    x_ref[:rows, :] = xa_ref[...]
    x_ref[rows:, :] = xb_ref[...]
    for n, (at, size) in enumerate(pieces(hidden, UNITS)):
        ready(0, n)
        gate = jnp.dot(x_ref[:, :features], gate_ref[:, at : at + size], preferred_element_type=F32)
        up = jnp.dot(x_ref[:, :features], up_ref[:, at : at + size], preferred_element_type=F32)
        hidden_ref[:, at : at + size] = (gate * jax.nn.sigmoid(gate) * up).astype(BF16)
    tail = features // LANES * LANES
    parts = x_ref[:, tail : tail + LANES].astype(F32)
    weight = jnp.sum(jnp.where(mask_ref[...] > 0.0, parts, 0.0), axis=1, keepdims=True)
    for n, (at, size) in enumerate(pieces(features, COLUMNS)):
        ready(1, n)
        y = lax.dot_general(
            hidden_ref[...],
            down_ref[at : at + size, :],
            (((1,), (1,)), ((), ())),
            preferred_element_type=F32,
        )
        y = (y * weight).astype(BF16)
        ya_ref[:, at : at + size] = y[:rows]
        yb_ref[:, at : at + size] = y[rows:]
    blank = jnp.zeros((rows, ya_ref.shape[1] - features), BF16)
    ya_ref[:, features:] = blank
    yb_ref[:, features:] = blank


def expert_kernel(xa, xb, mask, gate, up, down, ya, yb, x, hidden):
    expert_body(xa, xb, mask, gate, up, down, ya, yb, x, hidden, lambda part, n: None)


def first_kernel(xa, xb, mask, gate_any, up_any, down_any, ya, yb, gate, up, down, x, hidden, sems_wide, sems_down):
    wide = []
    for n, (at, size) in enumerate(pieces(gate.shape[1], UNITS)):
        cut = pl.ds(at, size)
        wide.append(
            [
                pltpu.make_async_copy(gate_any.at[0, :, cut], gate.at[:, cut], sems_wide.at[2 * n]),
                pltpu.make_async_copy(up_any.at[0, :, cut], up.at[:, cut], sems_wide.at[2 * n + 1]),
            ]
        )
    tall = []
    for n, (at, size) in enumerate(pieces(down.shape[0], COLUMNS)):
        cut = pl.ds(at, size)
        tall.append([pltpu.make_async_copy(down_any.at[0, cut, :], down.at[cut, :], sems_down.at[n])])
    for copies in wide + tall:
        for copy in copies:
            copy.start()

    def ready(part, n):
        for copy in (wide, tall)[part][n]:
            copy.wait()

    expert_body(xa, xb, mask, gate, up, down, ya, yb, x, hidden, ready)


def expert_call(xa, xb, mask, weights, first=False):
    rows, width = xa.shape
    shapes = [w.shape[-2:] for w in weights]
    hidden, features = shapes[0][1], shapes[2][0]
    out = jax.ShapeDtypeStruct((rows, width), BF16)
    kept = tuple(pltpu.VMEM(shape, BF16) for shape in shapes) if first else ()
    place = pl.BlockSpec(memory_space=pltpu.VMEM)
    scratch = [pltpu.VMEM((2 * rows, width), BF16), pltpu.VMEM((2 * rows, hidden), BF16)]
    if first:
        scratch += [
            pltpu.SemaphoreType.DMA((2 * len(pieces(hidden, UNITS)),)),
            pltpu.SemaphoreType.DMA((len(pieces(features, COLUMNS)),)),
        ]
    weights = [pltpu.with_memory_space_constraint(w, pltpu.HBM if first else pltpu.VMEM) for w in weights]
    return pl.pallas_call(
        first_kernel if first else expert_kernel,
        out_shape=(out, out, *kept),
        in_specs=[place] * 3 + [pl.BlockSpec(memory_space=pl.ANY) if first else place] * 3,
        out_specs=(place,) * (2 + len(kept)),
        scratch_shapes=scratch,
        compiler_params=pltpu.CompilerParams(vmem_limit_bytes=16 * 2**20),
        cost_estimate=pl.CostEstimate(flops=0, bytes_accessed=0, transcendentals=0),
    )(xa, xb, mask, *weights)


def local_cube(tokens, norm_gain, expert_ids, gate_weights, gate_proj, up_proj, down_proj):
    tok_rows, features = tokens.shape
    devices = lax.axis_size("ex")
    experts = devices // SLICES
    mine = lax.axis_index("ex") % experts
    width = -(-(features + 3 * experts) // LANES) * LANES

    def swap(array, partner):
        return lax.ppermute(array, "ex", [(i, partner(i)) for i in range(devices)])

    def first(i):
        return i ^ (2 if i % 2 == 0 else 4)

    def second(i):
        return i ^ (4 if i % 2 == 0 else 2)

    def core(i):
        return i ^ 1

    def slice_bits(j):
        return lambda i: i ^ (j * experts)

    rows = rows_call(tokens, norm_gain, expert_ids, gate_weights, experts, width)
    lane = jnp.arange(LANES, dtype=jnp.int32)[None, :] - features % LANES
    ours = (lane >= 0) & (lane < 3 * experts) & (lane % experts == mine)
    mask = ours.astype(F32)
    weights = [gate_proj, up_proj, jnp.swapaxes(down_proj, 1, 2)]
    last = [mask]

    def order(value):
        value = lax.optimization_barrier((value, last[0]))[0]
        last[0] = value
        return value

    def expert(xa, xb):
        first_time = len(weights[0].shape) == 3
        parts = expert_call(xa, xb, mask, weights, first_time)
        if first_time:
            weights[:] = parts[2:]
        last[0] = parts[0]
        return parts[:2]

    def add(a, b):
        return (a.astype(F32) + b.astype(F32)).astype(BF16)

    p1, p2, half, ch, cp, near, far, back, q2, q1, z, zb = ([None] * SLICES for _ in range(12))

    def gather_half(j, block):
        half[j] = jnp.concatenate([block, order(p1[j])], axis=0)
        p2[j] = swap(half[j], second)
        ch[j] = swap(half[j], core)

    def gather_full(j):
        p2[j] = order(p2[j])
        cp[j] = swap(p2[j], core)

    def run_own(j):
        near[j], far[j] = expert(order(half[j]), p2[j])

    def run_other(j):
        mine_half = order(ch[j])
        back[j] = [swap(part, core) for part in expert(mine_half, order(cp[j]))]

    def reduce_core(j):
        q2[j] = swap(add(far[j], order(back[j][1])), second)

    def reduce_second(j):
        arrived = order(q2[j])
        near[j] = (near[j], order(back[j][0]), arrived)
        q1[j] = swap(total_of([a[tok_rows:] for a in near[j]]), first)

    def reduce_first(j):
        sums = total_of([a[:tok_rows] for a in near[j]] + [order(q1[j])])
        zb[j] = swap(sums, slice_bits(j)) if j else sums

    def total_of(arrays):
        return sum(a.astype(F32) for a in arrays).astype(BF16)

    p1[0] = order(swap(rows, first))
    z[1] = order(swap(rows, slice_bits(1)))
    z[2] = swap(order(rows), slice_bits(2))
    gather_half(0, rows)
    p1[1] = swap(z[1], first)
    gather_half(1, z[1])
    gather_full(0)
    run_own(0)
    z[2] = order(z[2])
    p1[2] = swap(z[2], first)
    z[3] = swap(order(rows), slice_bits(3))
    run_other(0)
    gather_half(2, z[2])
    gather_full(1)
    run_own(1)
    z[3] = order(z[3])
    p1[3] = swap(z[3], first)
    run_other(1)
    gather_half(3, z[3])
    gather_full(2)
    run_own(2)
    run_other(2)
    gather_full(3)
    reduce_core(1)
    reduce_core(2)
    run_own(3)
    run_other(3)
    reduce_second(1)
    reduce_second(2)
    reduce_core(3)
    reduce_first(1)
    reduce_first(2)
    reduce_core(0)
    reduce_second(3)
    zb[2] = order(zb[2])
    reduce_first(3)
    reduce_second(0)
    reduce_first(0)
    total = sum(order(zb[j]).astype(F32) for j in (2, 3, 1, 0))
    return total[:, :features].astype(BF16)


def solution(mesh):
    in_specs = (
        P(("groups", "ex"), None),
        P(),
        P(("groups", "ex"), None),
        P(("groups", "ex"), None),
        P("ex", None, None),
        P("ex", None, None),
        P("ex", None, None),
    )
    out_specs = P(("groups", "ex"), None)
    local = local_cube if mesh.shape["ex"] == 8 * SLICES else local_general
    return jax.shard_map(local, mesh=mesh, in_specs=in_specs, out_specs=out_specs, check_vma=False)
```

time: 197 us -> 152 us (0.77)
  the two profiles are of different devices: /device:TPU:16 before, /device:TPU:0 now
where the time goes in v3:
time: 152 us
  waiting for transfers between devices  69.2 us (46%)
  starting transfers between devices  42.5 us (28%)
  Pallas kernels  36.6 us (24%)
  other arithmetic  3.08 us (2%)
    ppermute x38, waiting for transfers between devices, swap(): return lax.ppermute(array, 'ex', [(i, partner(i)) for i in range(devices)])  69.2 us
    ppermute x38, starting transfers between devices, swap(): return lax.ppermute(array, 'ex', [(i, partner(i)) for i in range(devices)])  42.5 us
    pallas_call x8, Pallas kernels, expert_call(): pl.pallas_call(first_kernel if first else expert_kernel, out_shape=(out,...  35.4 us
  transfers between devices with their start and end apart: 38, of which 15 were waited for; matrix products, arithmetic and copies ran while one was open for 1% of the time, Pallas kernels for 23%

profile of v3, /device:TPU:0, one launch (start us, length us, event | category | flops | bytes accessed | tf_op | source)
XLA Modules:
  0.0 151.8 jit_solution(11866065778329589085)
XLA Ops:
  0.0 1.3 shard_map.73
  1.3 3.0 %collective-permute-start.1 = (bf16[64,2944]{1,0:T(8,128)(2,1)S(1)}, bf16[64,2944]{1,0:T(8,128)(2,1)S(1)}, u32[]{:S(2)}, u32[]{:S(2)}) collective-permute-start(bf16[64,2944]{1,0:T(8,128)(2,1)S(1)} %shard_map.73), channel_id=1, source_target_pairs={{0,2},{1,5},{2,0},{3,7},{4,6},{5,1},{6,4},{7,3},{8,10},{9,13},{10,... | collective-permute-start | bytes 1130504 | tf_op jit(solution)/shard_map/ppermute | solution.py:202
  4.3 1.6 %collective-permute-start = (bf16[64,2944]{1,0:T(8,128)(2,1)S(1)}, bf16[64,2944]{1,0:T(8,128)(2,1)S(1)}, u32[]{:S(2)}, u32[]{:S(2)}) collective-permute-start(bf16[64,2944]{1,0:T(8,128)(2,1)S(1)} %shard_map.73), channel_id=1, source_target_pairs={{0,8},{1,9},{2,10},{3,11},{4,12},{5,13},{6,14},{7,15},{8,0},{9,1},... | collective-permute-start | bytes 1130504 | tf_op jit(solution)/shard_map/ppermute | solution.py:202
  5.9 4.0 %collective-permute-done.1 = bf16[64,2944]{1,0:T(8,128)(2,1)S(1)} collective-permute-done((bf16[64,2944]{1,0:T(8,128)(2,1)S(1)}, bf16[64,2944]{1,0:T(8,128)(2,1)S(1)}, u32[]{:S(2)}, u32[]{:S(2)}) %collective-permute-start.1) | collective-permute-done | bytes 376864 | tf_op jit(solution)/shard_map/ppermute | solution.py:202
  9.9 4.7 %collective-permute-done = bf16[64,2944]{1,0:T(8,128)(2,1)S(1)} collective-permute-done((bf16[64,2944]{1,0:T(8,128)(2,1)S(1)}, bf16[64,2944]{1,0:T(8,128)(2,1)S(1)}, u32[]{:S(2)}, u32[]{:S(2)}) %collective-permute-start) | collective-permute-done | bytes 376864 | tf_op jit(solution)/shard_map/ppermute | solution.py:202
  14.6 0.4 collective-permute-start.3
  15.0 1.6 %collective-permute-start.4 = (bf16[64,2944]{1,0:T(8,128)(2,1)S(1)}, bf16[64,2944]{1,0:T(8,128)(2,1)S(1)}, u32[]{:S(2)}, u32[]{:S(2)}) collective-permute-start(bf16[64,2944]{1,0:T(8,128)(2,1)S(1)} %collective-permute-done), channel_id=1, source_target_pairs={{0,2},{1,5},{2,0},{3,7},{4,6},{5,1},{6,4},{7,3},{8,10},{9,13},{10,... | collective-permute-start | bytes 1130504 | tf_op jit(solution)/shard_map/ppermute | solution.py:202
  16.7 2.6 %collective-permute-start.2 = (bf16[64,2944]{1,0:T(8,128)(2,1)S(1)}, bf16[64,2944]{1,0:T(8,128)(2,1)S(1)}, u32[]{:S(2)}, u32[]{:S(2)}) collective-permute-start(bf16[64,2944]{1,0:T(8,128)(2,1)S(1)} %shard_map.73), channel_id=1, source_target_pairs={{0,16},{1,17},{2,18},{3,19},{4,20},{5,21},{6,22},{7,23},{8,24},{9,... | collective-permute-start | bytes 1130504 | tf_op jit(solution)/shard_map/ppermute | solution.py:202
  19.3 7.4 %collective-permute-done.4 = bf16[64,2944]{1,0:T(8,128)(2,1)S(1)} collective-permute-done((bf16[64,2944]{1,0:T(8,128)(2,1)S(1)}, bf16[64,2944]{1,0:T(8,128)(2,1)S(1)}, u32[]{:S(2)}, u32[]{:S(2)}) %collective-permute-start.4) | collective-permute-done | bytes 376864 | tf_op jit(solution)/shard_map/ppermute | solution.py:202
  26.7 3.6 %collective-permute-done.3.xb = bf16[128,2944]{1,0:T(8,128)(2,1)S(1)} collective-permute-done((bf16[128,2944]{1,0:T(8,128)(2,1)S(1)}, bf16[128,2944]{1,0:T(8,128)(2,1)S(1)}, u32[]{:S(2)}, u32[]{:S(2)}) %collective-permute-start.3) | collective-permute-done | bytes 753696 | tf_op jit(solution)/shard_map/ppermute | solution.py:202
  30.4 0.4 collective-permute-start.10
  30.8 7.8 %shard_map.74 = (bf16[128,2944]{1,0:T(8,128)(2,1)S(1)}, bf16[128,2944]{1,0:T(8,128)(2,1)S(1)}, bf16[2880,640]{1,0:T(8,128)(2,1)S(1)}, bf16[2880,640]{1,0:T(8,128)(2,1)S(1)}, bf16[2880,640]{1,0:T(8,128)(2,1)S(1)}) custom-call(bf16[128,2944]{1,0:T(8,128)(2,1)S(1)} %pad_maximum_fusion.xa, bf16[128,2944]{1,0:T(8,128)(2,1)S(1)} %collective-permute-done.3.xb, ...), custom_call_target="tpu_custom_call" | custom-call | tf_op jit(solution)/shard_map/pallas_call | solution.py:183
  38.6 0.7 collective-permute-start.5
  39.3 3.3 %collective-permute-start.9 = (bf16[64,2944]{1,0:T(8,128)(2,1)S(1)}, bf16[64,2944]{1,0:T(8,128)(2,1)S(1)}, u32[]{:S(2)}, u32[]{:S(2)}) collective-permute-start(bf16[64,2944]{1,0:T(8,128)(2,1)S(1)} %shard_map.73), channel_id=1, source_target_pairs={{0,24},{1,25},{2,26},{3,27},{4,28},{5,29},{6,30},{7,31},{8,16},{9,... | collective-permute-start | bytes 1130504 | tf_op jit(solution)/shard_map/ppermute | solution.py:202
  42.6 3.9 %shard_map.75 = (bf16[128,2944]{1,0:T(8,128)(2,1)S(1)}, bf16[128,2944]{1,0:T(8,128)(2,1)S(1)}) custom-call(bf16[128,2944]{1,0:T(8,128)(2,1)S(1)} %collective-permute-done.6.xa, bf16[128,2944]{1,0:T(8,128)(2,1)S(1)} %collective-permute-done.7.xb, f32[1,128]{1,0:T(1,128)S(1)} %and_convert_fusion.mask, bf16[2880,640]{1,0:T(8,128)(2,1)S(1)} %get-tuple-element.83.gate, ...), custom_call_target="tpu_custom_call" | custom-call | tf_op jit(solution)/shard_map/pallas_call | solution.py:183
  46.9 1.8 %collective-permute-start.8 = (bf16[128,2944]{1,0:T(8,128)(2,1)S(1)}, bf16[128,2944]{1,0:T(8,128)(2,1)S(1)}, u32[]{:S(2)}, u32[]{:S(2)}) collective-permute-start(bf16[128,2944]{1,0:T(8,128)(2,1)S(1)} %constant_dynamic-update-slice_fusion.xa), channel_id=1, source_target_pairs={{0,4},{1,3},{2,6},{3,1},{4,0},{5,7},{6,2},{7,5},{8,12},{9,11},{10,... | collective-permute-start | bytes 2261000 | tf_op jit(solution)/shard_map/ppermute | solution.py:202
  48.7 3.9 %shard_map.76 = (bf16[128,2944]{1,0:T(8,128)(2,1)S(1)}, bf16[128,2944]{1,0:T(8,128)(2,1)S(1)}) custom-call(bf16[128,2944]{1,0:T(8,128)(2,1)S(1)} %constant_dynamic-update-slice_fusion.2.xa, bf16[128,2944]{1,0:T(8,128)(2,1)S(1)} %collective-permute-done.10.xb, f32[1,128]{1,0:T(1,128)S(1)} %and_convert_fusion.mask, ...), custom_call_target="tpu_custom_call" | custom-call | tf_op jit(solution)/shard_map/pallas_call | solution.py:183
  52.6 1.7 %collective-permute-start.11 = (bf16[64,2944]{1,0:T(8,128)(2,1)S(1)}, bf16[64,2944]{1,0:T(8,128)(2,1)S(1)}, u32[]{:S(2)}, u32[]{:S(2)}) collective-permute-start(bf16[64,2944]{1,0:T(8,128)(2,1)S(1)} %collective-permute-done.9), channel_id=1, source_target_pairs={{0,2},{1,5},{2,0},{3,7},{4,6},{5,1},{6,4},{7,3},{8,10},{9,13},{10,... | collective-permute-start | bytes 1130504 | tf_op jit(solution)/shard_map/ppermute | solution.py:202
  54.3 4.1 %shard_map.77 = (bf16[128,2944]{1,0:T(8,128)(2,1)S(1)}, bf16[128,2944]{1,0:T(8,128)(2,1)S(1)}) custom-call(bf16[128,2944]{1,0:T(8,128)(2,1)S(1)} %collective-permute-done.12.xa, bf16[128,2944]{1,0:T(8,128)(2,1)S(1)} %collective-permute-done.13.xb, f32[1,128]{1,0:T(1,128)S(1)} %and_convert_fusion.mask, bf16[2880,640]{1,0:T(8,128)(2,1)S(1)} %get-tuple-element.83.gate, ...), custom_call_target="tpu_custom_call" | custom-call | tf_op jit(solution)/shard_map/pallas_call | solution.py:183
  58.4 3.5 %collective-permute-done.11 = bf16[64,2944]{1,0:T(8,128)(2,1)S(1)} collective-permute-done((bf16[64,2944]{1,0:T(8,128)(2,1)S(1)}, bf16[64,2944]{1,0:T(8,128)(2,1)S(1)}, u32[]{:S(2)}, u32[]{:S(2)}) %collective-permute-start.11) | collective-permute-done | bytes 376864 | tf_op jit(solution)/shard_map/ppermute | solution.py:202
  61.9 0.5 collective-permute-start.15
  62.5 1.8 %collective-permute-start.19 = (bf16[128,2944]{1,0:T(8,128)(2,1)S(1)}, bf16[128,2944]{1,0:T(8,128)(2,1)S(1)}, u32[]{:S(2)}, u32[]{:S(2)}) collective-permute-start(bf16[128,2944]{1,0:T(8,128)(2,1)S(1)} %constant_dynamic-update-slice_fusion.4.xa), channel_id=1, source_target_pairs={{0,4},{1,3},{2,6},{3,1},{4,0},{5,7},{6,2},{7,5},{8,12},{9,11},{10,... | collective-permute-start | bytes 2261000 | tf_op jit(solution)/shard_map/ppermute | solution.py:202
  64.6 3.9 %shard_map.78 = (bf16[128,2944]{1,0:T(8,128)(2,1)S(1)}, bf16[128,2944]{1,0:T(8,128)(2,1)S(1)}) custom-call(bf16[128,2944]{1,0:T(8,128)(2,1)S(1)} %constant_dynamic-update-slice_fusion.xa, bf16[128,2944]{1,0:T(8,128)(2,1)S(1)} %collective-permute-done.8.xb, f32[1,128]{1,0:T(1,128)S(1)} %and_convert_fusion.mask, bf16[2880,640]{1,0:T(8,128)(2,1)S(1)} %get-tuple-element.83.gate, ...), custom_call_target="tpu_custom_call" | custom-call | tf_op jit(solution)/shard_map/pallas_call | solution.py:183
  68.5 3.9 %shard_map.79 = (bf16[128,2944]{1,0:T(8,128)(2,1)S(1)}, bf16[128,2944]{1,0:T(8,128)(2,1)S(1)}) custom-call(bf16[128,2944]{1,0:T(8,128)(2,1)S(1)} %collective-permute-done.14.xa, bf16[128,2944]{1,0:T(8,128)(2,1)S(1)} %collective-permute-done.15.xb, f32[1,128]{1,0:T(1,128)S(1)} %and_convert_fusion.mask, bf16[2880,640]{1,0:T(8,128)(2,1)S(1)} %get-tuple-element.83.gate, ...), custom_call_target="tpu_custom_call" | custom-call | tf_op jit(solution)/shard_map/pallas_call | solution.py:183
  73.2 1.0 collective-permute-done.19.xb
  74.4 1.8 %collective-permute-start.22 = (bf16[128,2944]{1,0:T(8,128)(2,1)S(1)}, bf16[128,2944]{1,0:T(8,128)(2,1)S(1)}, u32[]{:S(2)}, u32[]{:S(2)}) collective-permute-start(bf16[128,2944]{1,0:T(8,128)(2,1)S(1)} %add_convert_fusion.2), channel_id=1, source_target_pairs={{0,4},{1,3},{2,6},{3,1},{4,0},{5,7},{6,2},{7,5},{8,12},{9,11},{10,... | collective-permute-start | bytes 2261000 | tf_op jit(solution)/shard_map/ppermute | solution.py:202
  76.4 0.3 collective-permute-start.20
  77.1 4.1 %shard_map.80 = (bf16[128,2944]{1,0:T(8,128)(2,1)S(1)}, bf16[128,2944]{1,0:T(8,128)(2,1)S(1)}) custom-call(bf16[128,2944]{1,0:T(8,128)(2,1)S(1)} %constant_dynamic-update-slice_fusion.4.xa, bf16[128,2944]{1,0:T(8,128)(2,1)S(1)} %collective-permute-done.19.xb, f32[1,128]{1,0:T(1,128)S(1)} %and_convert_fusion.mask, ...), custom_call_target="tpu_custom_call" | custom-call | tf_op jit(solution)/shard_map/pallas_call | solution.py:183
  81.2 0.4 collective-permute-start.31
  81.6 3.9 %shard_map.81 = (bf16[128,2944]{1,0:T(8,128)(2,1)S(1)}, bf16[128,2944]{1,0:T(8,128)(2,1)S(1)}) custom-call(bf16[128,2944]{1,0:T(8,128)(2,1)S(1)} %collective-permute-done.23.xa, bf16[128,2944]{1,0:T(8,128)(2,1)S(1)} %collective-permute-done.24.xb, f32[1,128]{1,0:T(1,128)S(1)} %and_convert_fusion.mask, bf16[2880,640]{1,0:T(8,128)(2,1)S(1)} %get-tuple-element.83.gate, ...), custom_call_target="tpu_custom_call" | custom-call | tf_op jit(solution)/shard_map/pallas_call | solution.py:183
  85.4 0.6 collective-permute-done.22
  86.1 0.5 collective-permute-start.27
  86.7 7.4 %collective-permute-done.20 = bf16[128,2944]{1,0:T(8,128)(2,1)S(1)} collective-permute-done((bf16[128,2944]{1,0:T(8,128)(2,1)S(1)}, bf16[128,2944]{1,0:T(8,128)(2,1)S(1)}, u32[]{:S(2)}, u32[]{:S(2)}) %collective-permute-start.20) | collective-permute-done | bytes 753696 | tf_op jit(solution)/shard_map/ppermute | solution.py:202
  94.1 2.0 %collective-permute-start.26 = (bf16[64,2944]{1,0:T(8,128)(2,1)S(1)}, bf16[64,2944]{1,0:T(8,128)(2,1)S(1)}, u32[]{:S(2)}, u32[]{:S(2)}) collective-permute-start(bf16[64,2944]{1,0:T(8,128)(2,1)S(1)} %add_convert_fusion.11), channel_id=1, source_target_pairs={{0,2},{1,5},{2,0},{3,7},{4,6},{5,1},{6,4},{7,3},{8,10},{9,13},{10,... | collective-permute-start | bytes 1130504 | tf_op jit(solution)/shard_map/ppermute | solution.py:202
  96.4 5.4 %collective-permute-done.26 = bf16[64,2944]{1,0:T(8,128)(2,1)S(1)} collective-permute-done((bf16[64,2944]{1,0:T(8,128)(2,1)S(1)}, bf16[64,2944]{1,0:T(8,128)(2,1)S(1)}, u32[]{:S(2)}, u32[]{:S(2)}) %collective-permute-start.26) | collective-permute-done | bytes 376864 | tf_op jit(solution)/shard_map/ppermute | solution.py:202
  101.9 1.8 %collective-permute-start.30 = (bf16[128,2944]{1,0:T(8,128)(2,1)S(1)}, bf16[128,2944]{1,0:T(8,128)(2,1)S(1)}, u32[]{:S(2)}, u32[]{:S(2)}) collective-permute-start(bf16[128,2944]{1,0:T(8,128)(2,1)S(1)} %add_convert_fusion.1), channel_id=1, source_target_pairs={{0,4},{1,3},{2,6},{3,1},{4,0},{5,7},{6,2},{7,5},{8,12},{9,11},{10,... | collective-permute-start | bytes 2261000 | tf_op jit(solution)/shard_map/ppermute | solution.py:202
  103.8 4.1 %collective-permute-done.25 = bf16[64,2944]{1,0:T(8,128)(2,1)S(1)} collective-permute-done((bf16[64,2944]{1,0:T(8,128)(2,1)S(1)}, bf16[64,2944]{1,0:T(8,128)(2,1)S(1)}, u32[]{:S(2)}, u32[]{:S(2)}) %collective-permute-start.25) | collective-permute-done | bytes 376864 | tf_op jit(solution)/shard_map/ppermute | solution.py:202
  108.1 1.9 %collective-permute-start.33 = (bf16[128,2944]{1,0:T(8,128)(2,1)S(1)}, bf16[128,2944]{1,0:T(8,128)(2,1)S(1)}, u32[]{:S(2)}, u32[]{:S(2)}) collective-permute-start(bf16[128,2944]{1,0:T(8,128)(2,1)S(1)} %add_convert_fusion), channel_id=1, source_target_pairs={{0,4},{1,3},{2,6},{3,1},{4,0},{5,7},{6,2},{7,5},{8,12},{9,11},{10,... | collective-permute-start | bytes 2261000 | tf_op jit(solution)/shard_map/ppermute | solution.py:202
  110.2 6.3 %collective-permute-start.28 = (bf16[64,2944]{1,0:T(8,128)(2,1)S(1)}, bf16[64,2944]{1,0:T(8,128)(2,1)S(1)}, u32[]{:S(2)}, u32[]{:S(2)}) collective-permute-start(bf16[64,2944]{1,0:T(8,128)(2,1)S(1)} %add_convert_fusion.10), channel_id=1, source_target_pairs={{0,16},{1,17},{2,18},{3,19},{4,20},{5,21},{6,22},{7,23},{8,24},{9,... | collective-permute-start | bytes 1130504 | tf_op jit(solution)/shard_map/ppermute | solution.py:202
  116.6 1.7 %collective-permute-start.34 = (bf16[64,2944]{1,0:T(8,128)(2,1)S(1)}, bf16[64,2944]{1,0:T(8,128)(2,1)S(1)}, u32[]{:S(2)}, u32[]{:S(2)}) collective-permute-start(bf16[64,2944]{1,0:T(8,128)(2,1)S(1)} %add_convert_fusion.9), channel_id=1, source_target_pairs={{0,2},{1,5},{2,0},{3,7},{4,6},{5,1},{6,4},{7,3},{8,10},{9,13},{10,... | collective-permute-start | bytes 1130504 | tf_op jit(solution)/shard_map/ppermute | solution.py:202
  118.3 11.2 %collective-permute-done.28 = bf16[64,2944]{1,0:T(8,128)(2,1)S(1)} collective-permute-done((bf16[64,2944]{1,0:T(8,128)(2,1)S(1)}, bf16[64,2944]{1,0:T(8,128)(2,1)S(1)}, u32[]{:S(2)}, u32[]{:S(2)}) %collective-permute-start.28) | collective-permute-done | bytes 376864 | tf_op jit(solution)/shard_map/ppermute | solution.py:202
  129.9 0.5 collective-permute-start.35
  130.3 1.3 collective-permute-start.36
  131.9 2.8 %collective-permute-start.37 = (bf16[64,2944]{1,0:T(8,128)(2,1)S(1)}, bf16[64,2944]{1,0:T(8,128)(2,1)S(1)}, u32[]{:S(2)}, u32[]{:S(2)}) collective-permute-start(bf16[64,2944]{1,0:T(8,128)(2,1)S(1)} %add_convert_fusion.6), channel_id=1, source_target_pairs={{0,8},{1,9},{2,10},{3,11},{4,12},{5,13},{6,14},{7,15},{8,0},{9,1},... | collective-permute-start | bytes 1130504 | tf_op jit(solution)/shard_map/ppermute | solution.py:202
  134.7 2.9 %collective-permute-done.35 = bf16[64,2944]{1,0:T(8,128)(2,1)S(1)} collective-permute-done((bf16[64,2944]{1,0:T(8,128)(2,1)S(1)}, bf16[64,2944]{1,0:T(8,128)(2,1)S(1)}, u32[]{:S(2)}, u32[]{:S(2)}) %collective-permute-start.35) | collective-permute-done | bytes 376864 | tf_op jit(solution)/shard_map/ppermute | solution.py:202
  137.5 6.3 %collective-permute-done.36 = bf16[64,2944]{1,0:T(8,128)(2,1)S(1)} collective-permute-done((bf16[64,2944]{1,0:T(8,128)(2,1)S(1)}, bf16[64,2944]{1,0:T(8,128)(2,1)S(1)}, u32[]{:S(2)}, u32[]{:S(2)}) %collective-permute-start.36) | collective-permute-done | bytes 376864 | tf_op jit(solution)/shard_map/ppermute | solution.py:202
  144.0 6.8 %collective-permute-done.37 = bf16[64,2944]{1,0:T(8,128)(2,1)S(1)} collective-permute-done((bf16[64,2944]{1,0:T(8,128)(2,1)S(1)}, bf16[64,2944]{1,0:T(8,128)(2,1)S(1)}, u32[]{:S(2)}, u32[]{:S(2)}) %collective-permute-start.37) | collective-permute-done | bytes 376864 | tf_op jit(solution)/shard_map/ppermute | solution.py:202
  150.8 1.0 add_convert_fusion.4
  (58 shorter events, 4.3 us)
Async XLA Ops:
  1.3 8.6 %collective-permute-start.1 = (bf16[64,2944]{1,0:T(8,128)(2,1)S(1)}, bf16[64,2944]{1,0:T(8,128)(2,1)S(1)}, u32[]{:S(2)}, u32[]{:S(2)}) collective-permute-start(bf16[64,2944]{1,0:T(8,128)(2,1)S(1)} %shard_map.73), channel_id=1, source_target_pairs={{0,2},{1,5},{2,0},{3,7},{4,6},{5,1},{6,4},{7,3},{8,10},{9,13},{10,... | collective-permute-start | bytes 1130504 | tf_op jit(solution)/shard_map/ppermute | solution.py:202
  4.3 10.3 %collective-permute-start = (bf16[64,2944]{1,0:T(8,128)(2,1)S(1)}, bf16[64,2944]{1,0:T(8,128)(2,1)S(1)}, u32[]{:S(2)}, u32[]{:S(2)}) collective-permute-start(bf16[64,2944]{1,0:T(8,128)(2,1)S(1)} %shard_map.73), channel_id=1, source_target_pairs={{0,8},{1,9},{2,10},{3,11},{4,12},{5,13},{6,14},{7,15},{8,0},{9,1},... | collective-permute-start | bytes 1130504 | tf_op jit(solution)/shard_map/ppermute | solution.py:202
  14.6 15.7 %collective-permute-start.3 = (bf16[128,2944]{1,0:T(8,128)(2,1)S(1)}, bf16[128,2944]{1,0:T(8,128)(2,1)S(1)}, u32[]{:S(2)}, u32[]{:S(2)}) collective-permute-start(bf16[128,2944]{1,0:T(8,128)(2,1)S(1)} %pad_maximum_fusion.xa), channel_id=1, source_target_pairs={{0,4},{1,3},{2,6},{3,1},{4,0},{5,7},{6,2},{7,5},{8,12},{9,11},{10,... | collective-permute-start | bytes 2261000 | tf_op jit(solution)/shard_map/ppermute | solution.py:202
  15.0 11.7 %collective-permute-start.4 = (bf16[64,2944]{1,0:T(8,128)(2,1)S(1)}, bf16[64,2944]{1,0:T(8,128)(2,1)S(1)}, u32[]{:S(2)}, u32[]{:S(2)}) collective-permute-start(bf16[64,2944]{1,0:T(8,128)(2,1)S(1)} %collective-permute-done), channel_id=1, source_target_pairs={{0,2},{1,5},{2,0},{3,7},{4,6},{5,1},{6,4},{7,3},{8,10},{9,13},{10,... | collective-permute-start | bytes 1130504 | tf_op jit(solution)/shard_map/ppermute | solution.py:202
  16.7 22.6 %collective-permute-start.6 = (bf16[128,2944]{1,0:T(8,128)(2,1)S(1)}, bf16[128,2944]{1,0:T(8,128)(2,1)S(1)}, u32[]{:S(2)}, u32[]{:S(2)}) collective-permute-start(bf16[128,2944]{1,0:T(8,128)(2,1)S(1)} %pad_maximum_fusion.xa), channel_id=1, source_target_pairs={{0,1},{1,0},{2,3},{3,2},{4,5},{5,4},{6,7},{7,6},{8,9},{9,8},{10,11... | collective-permute-start | bytes 2261000 | tf_op jit(solution)/shard_map/ppermute | solution.py:202
  16.7 21.9 %collective-permute-start.2 = (bf16[64,2944]{1,0:T(8,128)(2,1)S(1)}, bf16[64,2944]{1,0:T(8,128)(2,1)S(1)}, u32[]{:S(2)}, u32[]{:S(2)}) collective-permute-start(bf16[64,2944]{1,0:T(8,128)(2,1)S(1)} %shard_map.73), channel_id=1, source_target_pairs={{0,16},{1,17},{2,18},{3,19},{4,20},{5,21},{6,22},{7,23},{8,24},{9,... | collective-permute-start | bytes 1130504 | tf_op jit(solution)/shard_map/ppermute | solution.py:202
  30.4 12.3 %collective-permute-start.7 = (bf16[128,2944]{1,0:T(8,128)(2,1)S(1)}, bf16[128,2944]{1,0:T(8,128)(2,1)S(1)}, u32[]{:S(2)}, u32[]{:S(2)}) collective-permute-start(bf16[128,2944]{1,0:T(8,128)(2,1)S(1)} %collective-permute-done.3.xb), channel_id=1, source_target_pairs={{0,1},{1,0},{2,3},{3,2},{4,5},{5,4},{6,7},{7,6},{8,9},{9,8},{10,11... | collective-permute-start | bytes 2261000 | tf_op jit(solution)/shard_map/ppermute | solution.py:202
  30.4 16.2 %collective-permute-start.10 = (bf16[128,2944]{1,0:T(8,128)(2,1)S(1)}, bf16[128,2944]{1,0:T(8,128)(2,1)S(1)}, u32[]{:S(2)}, u32[]{:S(2)}) collective-permute-start(bf16[128,2944]{1,0:T(8,128)(2,1)S(1)} %constant_dynamic-update-slice_fusion.2.xa), channel_id=1, source_target_pairs={{0,4},{1,3},{2,6},{3,1},{4,0},{5,7},{6,2},{7,5},{8,12},{9,11},{10,... | collective-permute-start | bytes 2261000 | tf_op jit(solution)/shard_map/ppermute | solution.py:202
  38.6 7.9 %collective-permute-start.5 = (bf16[64,2944]{1,0:T(8,128)(2,1)S(1)}, bf16[64,2944]{1,0:T(8,128)(2,1)S(1)}, u32[]{:S(2)}, u32[]{:S(2)}) collective-permute-start(bf16[64,2944]{1,0:T(8,128)(2,1)S(1)} %collective-permute-done.2), channel_id=1, source_target_pairs={{0,2},{1,5},{2,0},{3,7},{4,6},{5,1},{6,4},{7,3},{8,10},{9,13},{10,... | collective-permute-start | bytes 1130504 | tf_op jit(solution)/shard_map/ppermute | solution.py:202
  39.3 15.0 %collective-permute-start.12 = (bf16[128,2944]{1,0:T(8,128)(2,1)S(1)}, bf16[128,2944]{1,0:T(8,128)(2,1)S(1)}, u32[]{:S(2)}, u32[]{:S(2)}) collective-permute-start(bf16[128,2944]{1,0:T(8,128)(2,1)S(1)} %constant_dynamic-update-slice_fusion.2.xa), channel_id=1, source_target_pairs={{0,1},{1,0},{2,3},{3,2},{4,5},{5,4},{6,7},{7,6},{8,9},{9,8},{10,11... | collective-permute-start | bytes 2261000 | tf_op jit(solution)/shard_map/ppermute | solution.py:202
  39.3 13.3 %collective-permute-start.9 = (bf16[64,2944]{1,0:T(8,128)(2,1)S(1)}, bf16[64,2944]{1,0:T(8,128)(2,1)S(1)}, u32[]{:S(2)}, u32[]{:S(2)}) collective-permute-start(bf16[64,2944]{1,0:T(8,128)(2,1)S(1)} %shard_map.73), channel_id=1, source_target_pairs={{0,24},{1,25},{2,26},{3,27},{4,28},{5,29},{6,30},{7,31},{8,16},{9,... | collective-permute-start | bytes 1130504 | tf_op jit(solution)/shard_map/ppermute | solution.py:202
  46.6 7.8 %collective-permute-start.13 = (bf16[128,2944]{1,0:T(8,128)(2,1)S(1)}, bf16[128,2944]{1,0:T(8,128)(2,1)S(1)}, u32[]{:S(2)}, u32[]{:S(2)}) collective-permute-start(bf16[128,2944]{1,0:T(8,128)(2,1)S(1)} %collective-permute-done.10.xb), channel_id=1, source_target_pairs={{0,1},{1,0},{2,3},{3,2},{4,5},{5,4},{6,7},{7,6},{8,9},{9,8},{10,11... | collective-permute-start | bytes 2261000 | tf_op jit(solution)/shard_map/ppermute | solution.py:202
  46.9 15.1 %collective-permute-start.8 = (bf16[128,2944]{1,0:T(8,128)(2,1)S(1)}, bf16[128,2944]{1,0:T(8,128)(2,1)S(1)}, u32[]{:S(2)}, u32[]{:S(2)}) collective-permute-start(bf16[128,2944]{1,0:T(8,128)(2,1)S(1)} %constant_dynamic-update-slice_fusion.xa), channel_id=1, source_target_pairs={{0,4},{1,3},{2,6},{3,1},{4,0},{5,7},{6,2},{7,5},{8,12},{9,11},{10,... | collective-permute-start | bytes 2261000 | tf_op jit(solution)/shard_map/ppermute | solution.py:202
  52.6 9.3 %collective-permute-start.11 = (bf16[64,2944]{1,0:T(8,128)(2,1)S(1)}, bf16[64,2944]{1,0:T(8,128)(2,1)S(1)}, u32[]{:S(2)}, u32[]{:S(2)}) collective-permute-start(bf16[64,2944]{1,0:T(8,128)(2,1)S(1)} %collective-permute-done.9), channel_id=1, source_target_pairs={{0,2},{1,5},{2,0},{3,7},{4,6},{5,1},{6,4},{7,3},{8,10},{9,13},{10,... | collective-permute-start | bytes 1130504 | tf_op jit(solution)/shard_map/ppermute | solution.py:202
  54.3 14.2 %collective-permute-start.14 = (bf16[128,2944]{1,0:T(8,128)(2,1)S(1)}, bf16[128,2944]{1,0:T(8,128)(2,1)S(1)}, u32[]{:S(2)}, u32[]{:S(2)}) collective-permute-start(bf16[128,2944]{1,0:T(8,128)(2,1)S(1)} %constant_dynamic-update-slice_fusion.xa), channel_id=1, source_target_pairs={{0,1},{1,0},{2,3},{3,2},{4,5},{5,4},{6,7},{7,6},{8,9},{9,8},{10,11... | collective-permute-start | bytes 2261000 | tf_op jit(solution)/shard_map/ppermute | solution.py:202
  61.9 6.6 %collective-permute-start.15 = (bf16[128,2944]{1,0:T(8,128)(2,1)S(1)}, bf16[128,2944]{1,0:T(8,128)(2,1)S(1)}, u32[]{:S(2)}, u32[]{:S(2)}) collective-permute-start(bf16[128,2944]{1,0:T(8,128)(2,1)S(1)} %collective-permute-done.8.xb), channel_id=1, source_target_pairs={{0,1},{1,0},{2,3},{3,2},{4,5},{5,4},{6,7},{7,6},{8,9},{9,8},{10,11... | collective-permute-start | bytes 2261000 | tf_op jit(solution)/shard_map/ppermute | solution.py:202
  62.5 11.7 %collective-permute-start.19 = (bf16[128,2944]{1,0:T(8,128)(2,1)S(1)}, bf16[128,2944]{1,0:T(8,128)(2,1)S(1)}, u32[]{:S(2)}, u32[]{:S(2)}) collective-permute-start(bf16[128,2944]{1,0:T(8,128)(2,1)S(1)} %constant_dynamic-update-slice_fusion.4.xa), channel_id=1, source_target_pairs={{0,4},{1,3},{2,6},{3,1},{4,0},{5,7},{6,2},{7,5},{8,12},{9,11},{10,... | collective-permute-start | bytes 2261000 | tf_op jit(solution)/shard_map/ppermute | solution.py:202
  64.3 9.9 %collective-permute-start.18 = (bf16[128,2944]{1,0:T(8,128)(2,1)S(1)}, bf16[128,2944]{1,0:T(8,128)(2,1)S(1)}, u32[]{:S(2)}, u32[]{:S(2)}) collective-permute-start(bf16[128,2944]{1,0:T(8,128)(2,1)S(1)} %get-tuple-element.104), channel_id=1, source_target_pairs={{0,1},{1,0},{2,3},{3,2},{4,5},{5,4},{6,7},{7,6},{8,9},{9,8},{10,11... | collective-permute-start | bytes 2261000 | tf_op jit(solution)/shard_map/ppermute | solution.py:202
  72.4 3.8 %collective-permute-start.17 = (bf16[128,2944]{1,0:T(8,128)(2,1)S(1)}, bf16[128,2944]{1,0:T(8,128)(2,1)S(1)}, u32[]{:S(2)}, u32[]{:S(2)}) collective-permute-start(bf16[128,2944]{1,0:T(8,128)(2,1)S(1)} %get-tuple-element.103), channel_id=1, source_target_pairs={{0,1},{1,0},{2,3},{3,2},{4,5},{5,4},{6,7},{7,6},{8,9},{9,8},{10,11... | collective-permute-start | bytes 2261000 | tf_op jit(solution)/shard_map/ppermute | solution.py:202
  72.7 13.4 %collective-permute-start.21 = (bf16[128,2944]{1,0:T(8,128)(2,1)S(1)}, bf16[128,2944]{1,0:T(8,128)(2,1)S(1)}, u32[]{:S(2)}, u32[]{:S(2)}) collective-permute-start(bf16[128,2944]{1,0:T(8,128)(2,1)S(1)} %get-tuple-element.94), channel_id=1, source_target_pairs={{0,1},{1,0},{2,3},{3,2},{4,5},{5,4},{6,7},{7,6},{8,9},{9,8},{10,11... | collective-permute-start | bytes 2261000 | tf_op jit(solution)/shard_map/ppermute | solution.py:202
  73.0 3.9 %collective-permute-start.23 = (bf16[128,2944]{1,0:T(8,128)(2,1)S(1)}, bf16[128,2944]{1,0:T(8,128)(2,1)S(1)}, u32[]{:S(2)}, u32[]{:S(2)}) collective-permute-start(bf16[128,2944]{1,0:T(8,128)(2,1)S(1)} %constant_dynamic-update-slice_fusion.4.xa), channel_id=1, source_target_pairs={{0,1},{1,0},{2,3},{3,2},{4,5},{5,4},{6,7},{7,6},{8,9},{9,8},{10,11... | collective-permute-start | bytes 2261000 | tf_op jit(solution)/shard_map/ppermute | solution.py:202
  74.2 7.0 %collective-permute-start.24 = (bf16[128,2944]{1,0:T(8,128)(2,1)S(1)}, bf16[128,2944]{1,0:T(8,128)(2,1)S(1)}, u32[]{:S(2)}, u32[]{:S(2)}) collective-permute-start(bf16[128,2944]{1,0:T(8,128)(2,1)S(1)} %collective-permute-done.19.xb), channel_id=1, source_target_pairs={{0,1},{1,0},{2,3},{3,2},{4,5},{5,4},{6,7},{7,6},{8,9},{9,8},{10,11... | collective-permute-start | bytes 2261000 | tf_op jit(solution)/shard_map/ppermute | solution.py:202
  74.4 11.7 %collective-permute-start.22 = (bf16[128,2944]{1,0:T(8,128)(2,1)S(1)}, bf16[128,2944]{1,0:T(8,128)(2,1)S(1)}, u32[]{:S(2)}, u32[]{:S(2)}) collective-permute-start(bf16[128,2944]{1,0:T(8,128)(2,1)S(1)} %add_convert_fusion.2), channel_id=1, source_target_pairs={{0,4},{1,3},{2,6},{3,1},{4,0},{5,7},{6,2},{7,5},{8,12},{9,11},{10,... | collective-permute-start | bytes 2261000 | tf_op jit(solution)/shard_map/ppermute | solution.py:202
  76.4 17.8 %collective-permute-start.20 = (bf16[128,2944]{1,0:T(8,128)(2,1)S(1)}, bf16[128,2944]{1,0:T(8,128)(2,1)S(1)}, u32[]{:S(2)}, u32[]{:S(2)}) collective-permute-start(bf16[128,2944]{1,0:T(8,128)(2,1)S(1)} %add_convert_fusion.3), channel_id=1, source_target_pairs={{0,4},{1,3},{2,6},{3,1},{4,0},{5,7},{6,2},{7,5},{8,12},{9,11},{10,... | collective-permute-start | bytes 2261000 | tf_op jit(solution)/shard_map/ppermute | solution.py:202
  76.9 19.2 %collective-permute-start.16 = (bf16[128,2944]{1,0:T(8,128)(2,1)S(1)}, bf16[128,2944]{1,0:T(8,128)(2,1)S(1)}, u32[]{:S(2)}, u32[]{:S(2)}) collective-permute-start(bf16[128,2944]{1,0:T(8,128)(2,1)S(1)} %get-tuple-element.101), channel_id=1, source_target_pairs={{0,1},{1,0},{2,3},{3,2},{4,5},{5,4},{6,7},{7,6},{8,9},{9,8},{10,11... | collective-permute-start | bytes 2261000 | tf_op jit(solution)/shard_map/ppermute | solution.py:202
  81.2 26.7 %collective-permute-start.31 = (bf16[128,2944]{1,0:T(8,128)(2,1)S(1)}, bf16[128,2944]{1,0:T(8,128)(2,1)S(1)}, u32[]{:S(2)}, u32[]{:S(2)}) collective-permute-start(bf16[128,2944]{1,0:T(8,128)(2,1)S(1)} %get-tuple-element.123), channel_id=1, source_target_pairs={{0,1},{1,0},{2,3},{3,2},{4,5},{5,4},{6,7},{7,6},{8,9},{9,8},{10,11... | collective-permute-start | bytes 2261000 | tf_op jit(solution)/shard_map/ppermute | solution.py:202
  86.1 30.4 %collective-permute-start.29 = (bf16[128,2944]{1,0:T(8,128)(2,1)S(1)}, bf16[128,2944]{1,0:T(8,128)(2,1)S(1)}, u32[]{:S(2)}, u32[]{:S(2)}) collective-permute-start(bf16[128,2944]{1,0:T(8,128)(2,1)S(1)} %get-tuple-element.113), channel_id=1, source_target_pairs={{0,1},{1,0},{2,3},{3,2},{4,5},{5,4},{6,7},{7,6},{8,9},{9,8},{10,11... | collective-permute-start | bytes 2261000 | tf_op jit(solution)/shard_map/ppermute | solution.py:202
  86.1 10.3 %collective-permute-start.27 = (bf16[128,2944]{1,0:T(8,128)(2,1)S(1)}, bf16[128,2944]{1,0:T(8,128)(2,1)S(1)}, u32[]{:S(2)}, u32[]{:S(2)}) collective-permute-start(bf16[128,2944]{1,0:T(8,128)(2,1)S(1)} %get-tuple-element.118), channel_id=1, source_target_pairs={{0,1},{1,0},{2,3},{3,2},{4,5},{5,4},{6,7},{7,6},{8,9},{9,8},{10,11... | collective-permute-start | bytes 2261000 | tf_op jit(solution)/shard_map/ppermute | solution.py:202
  94.1 7.6 %collective-permute-start.26 = (bf16[64,2944]{1,0:T(8,128)(2,1)S(1)}, bf16[64,2944]{1,0:T(8,128)(2,1)S(1)}, u32[]{:S(2)}, u32[]{:S(2)}) collective-permute-start(bf16[64,2944]{1,0:T(8,128)(2,1)S(1)} %add_convert_fusion.11), channel_id=1, source_target_pairs={{0,2},{1,5},{2,0},{3,7},{4,6},{5,1},{6,4},{7,3},{8,10},{9,13},{10,... | collective-permute-start | bytes 1130504 | tf_op jit(solution)/shard_map/ppermute | solution.py:202
  96.2 11.7 %collective-permute-start.25 = (bf16[64,2944]{1,0:T(8,128)(2,1)S(1)}, bf16[64,2944]{1,0:T(8,128)(2,1)S(1)}, u32[]{:S(2)}, u32[]{:S(2)}) collective-permute-start(bf16[64,2944]{1,0:T(8,128)(2,1)S(1)} %add_convert_fusion.12), channel_id=1, source_target_pairs={{0,2},{1,5},{2,0},{3,7},{4,6},{5,1},{6,4},{7,3},{8,10},{9,13},{10,... | collective-permute-start | bytes 1130504 | tf_op jit(solution)/shard_map/ppermute | solution.py:202
  101.9 14.5 %collective-permute-start.30 = (bf16[128,2944]{1,0:T(8,128)(2,1)S(1)}, bf16[128,2944]{1,0:T(8,128)(2,1)S(1)}, u32[]{:S(2)}, u32[]{:S(2)}) collective-permute-start(bf16[128,2944]{1,0:T(8,128)(2,1)S(1)} %add_convert_fusion.1), channel_id=1, source_target_pairs={{0,4},{1,3},{2,6},{3,1},{4,0},{5,7},{6,2},{7,5},{8,12},{9,11},{10,... | collective-permute-start | bytes 2261000 | tf_op jit(solution)/shard_map/ppermute | solution.py:202
  108.1 21.4 %collective-permute-start.33 = (bf16[128,2944]{1,0:T(8,128)(2,1)S(1)}, bf16[128,2944]{1,0:T(8,128)(2,1)S(1)}, u32[]{:S(2)}, u32[]{:S(2)}) collective-permute-start(bf16[128,2944]{1,0:T(8,128)(2,1)S(1)} %add_convert_fusion), channel_id=1, source_target_pairs={{0,4},{1,3},{2,6},{3,1},{4,0},{5,7},{6,2},{7,5},{8,12},{9,11},{10,... | collective-permute-start | bytes 2261000 | tf_op jit(solution)/shard_map/ppermute | solution.py:202
  110.2 19.3 %collective-permute-start.28 = (bf16[64,2944]{1,0:T(8,128)(2,1)S(1)}, bf16[64,2944]{1,0:T(8,128)(2,1)S(1)}, u32[]{:S(2)}, u32[]{:S(2)}) collective-permute-start(bf16[64,2944]{1,0:T(8,128)(2,1)S(1)} %add_convert_fusion.10), channel_id=1, source_target_pairs={{0,16},{1,17},{2,18},{3,19},{4,20},{5,21},{6,22},{7,23},{8,24},{9,... | collective-permute-start | bytes 1130504 | tf_op jit(solution)/shard_map/ppermute | solution.py:202
  116.6 12.9 %collective-permute-start.34 = (bf16[64,2944]{1,0:T(8,128)(2,1)S(1)}, bf16[64,2944]{1,0:T(8,128)(2,1)S(1)}, u32[]{:S(2)}, u32[]{:S(2)}) collective-permute-start(bf16[64,2944]{1,0:T(8,128)(2,1)S(1)} %add_convert_fusion.9), channel_id=1, source_target_pairs={{0,2},{1,5},{2,0},{3,7},{4,6},{5,1},{6,4},{7,3},{8,10},{9,13},{10,... | collective-permute-start | bytes 1130504 | tf_op jit(solution)/shard_map/ppermute | solution.py:202
  118.3 11.4 %collective-permute-start.32 = (bf16[128,2944]{1,0:T(8,128)(2,1)S(1)}, bf16[128,2944]{1,0:T(8,128)(2,1)S(1)}, u32[]{:S(2)}, u32[]{:S(2)}) collective-permute-start(bf16[128,2944]{1,0:T(8,128)(2,1)S(1)} %get-tuple-element.86), channel_id=1, source_target_pairs={{0,1},{1,0},{2,3},{3,2},{4,5},{5,4},{6,7},{7,6},{8,9},{9,8},{10,11... | collective-permute-start | bytes 2261000 | tf_op jit(solution)/shard_map/ppermute | solution.py:202
  129.9 7.7 %collective-permute-start.35 = (bf16[64,2944]{1,0:T(8,128)(2,1)S(1)}, bf16[64,2944]{1,0:T(8,128)(2,1)S(1)}, u32[]{:S(2)}, u32[]{:S(2)}) collective-permute-start(bf16[64,2944]{1,0:T(8,128)(2,1)S(1)} %add_convert_fusion.8), channel_id=1, source_target_pairs={{0,2},{1,5},{2,0},{3,7},{4,6},{5,1},{6,4},{7,3},{8,10},{9,13},{10,... | collective-permute-start | bytes 1130504 | tf_op jit(solution)/shard_map/ppermute | solution.py:202
  130.3 13.5 %collective-permute-start.36 = (bf16[64,2944]{1,0:T(8,128)(2,1)S(1)}, bf16[64,2944]{1,0:T(8,128)(2,1)S(1)}, u32[]{:S(2)}, u32[]{:S(2)}) collective-permute-start(bf16[64,2944]{1,0:T(8,128)(2,1)S(1)} %add_convert_fusion.7), channel_id=1, source_target_pairs={{0,24},{1,25},{2,26},{3,27},{4,28},{5,29},{6,30},{7,31},{8,16},{9,... | collective-permute-start | bytes 1130504 | tf_op jit(solution)/shard_map/ppermute | solution.py:202
  131.9 19.0 %collective-permute-start.37 = (bf16[64,2944]{1,0:T(8,128)(2,1)S(1)}, bf16[64,2944]{1,0:T(8,128)(2,1)S(1)}, u32[]{:S(2)}, u32[]{:S(2)}) collective-permute-start(bf16[64,2944]{1,0:T(8,128)(2,1)S(1)} %add_convert_fusion.6), channel_id=1, source_target_pairs={{0,8},{1,9},{2,10},{3,11},{4,12},{5,13},{6,14},{7,15},{8,0},{9,1},... | collective-permute-start | bytes 1130504 | tf_op jit(solution)/shard_map/ppermute | solution.py:202

commit v4 on v3

--- a/solution.py
+++ b/solution.py
@@ -108,15 +108,17 @@
     )(*(pltpu.with_memory_space_constraint(a, pltpu.HBM) for a in arrays))
 
 
-def expert_body(xa_ref, xb_ref, mask_ref, gate_ref, up_ref, down_ref, ya_ref, yb_ref, x_ref, hidden_ref, ready):
-    features, hidden = gate_ref.shape
-    rows = xa_ref.shape[0]
-    x_ref[:rows, :] = xa_ref[...]
-    x_ref[rows:, :] = xb_ref[...]
+def expert_body(xs, mask_ref, both_ref, down_ref, ys, x_ref, hidden_ref, ready):
+    features, hidden = down_ref.shape
+    at = 0
+    for ref in xs:
+        x_ref[at : at + ref.shape[0], :] = ref[...]
+        at += ref.shape[0]
     for n, (at, size) in enumerate(pieces(hidden, UNITS)):
         ready(0, n)
-        gate = jnp.dot(x_ref[:, :features], gate_ref[:, at : at + size], preferred_element_type=F32)
-        up = jnp.dot(x_ref[:, :features], up_ref[:, at : at + size], preferred_element_type=F32)
+        x = x_ref[:, :features]
+        gate = jnp.dot(x, both_ref[:, 2 * at : 2 * at + size], preferred_element_type=F32)
+        up = jnp.dot(x, both_ref[:, 2 * at + size : 2 * (at + size)], preferred_element_type=F32)
         hidden_ref[:, at : at + size] = (gate * jax.nn.sigmoid(gate) * up).astype(BF16)
     tail = features // LANES * LANES
     parts = x_ref[:, tail : tail + LANES].astype(F32)
@@ -130,31 +132,37 @@
             preferred_element_type=F32,
         )
         y = (y * weight).astype(BF16)
-        ya_ref[:, at : at + size] = y[:rows]
-        yb_ref[:, at : at + size] = y[rows:]
-    blank = jnp.zeros((rows, ya_ref.shape[1] - features), BF16)
-    ya_ref[:, features:] = blank
-    yb_ref[:, features:] = blank
-
-
-def expert_kernel(xa, xb, mask, gate, up, down, ya, yb, x, hidden):
-    expert_body(xa, xb, mask, gate, up, down, ya, yb, x, hidden, lambda part, n: None)
-
-
-def first_kernel(xa, xb, mask, gate_any, up_any, down_any, ya, yb, gate, up, down, x, hidden, sems_wide, sems_down):
+        top = 0
+        for ref in ys:
+            ref[:, at : at + size] = y[top : top + ref.shape[0]]
+            top += ref.shape[0]
+    for ref in ys:
+        ref[:, features:] = jnp.zeros((ref.shape[0], ref.shape[1] - features), BF16)
+
+
+def expert_kernel(inputs, outputs, *refs):
+    xs, (mask, both, down), refs = refs[:inputs], refs[inputs : inputs + 3], refs[inputs + 3 :]
+    ys, (x, hidden) = refs[:outputs], refs[outputs:]
+    expert_body(xs, mask, both, down, ys, x, hidden, lambda part, n: None)
+
+
+def first_kernel(inputs, outputs, *refs):
+    xs, (mask, gate, up, stored), refs = refs[:inputs], refs[inputs : inputs + 4], refs[inputs + 4 :]
+    ys, (both, down, x, hidden, sems_wide, sems_down) = refs[:outputs], refs[outputs:]
     wide = []
-    for n, (at, size) in enumerate(pieces(gate.shape[1], UNITS)):
+    for n, (at, size) in enumerate(pieces(down.shape[1], UNITS)):
         cut = pl.ds(at, size)
+        left, right = pl.ds(2 * at, size), pl.ds(2 * at + size, size)
         wide.append(
             [
-                pltpu.make_async_copy(gate_any.at[0, :, cut], gate.at[:, cut], sems_wide.at[2 * n]),
-                pltpu.make_async_copy(up_any.at[0, :, cut], up.at[:, cut], sems_wide.at[2 * n + 1]),
+                pltpu.make_async_copy(gate.at[0, :, cut], both.at[:, left], sems_wide.at[2 * n]),
+                pltpu.make_async_copy(up.at[0, :, cut], both.at[:, right], sems_wide.at[2 * n + 1]),
             ]
         )
     tall = []
     for n, (at, size) in enumerate(pieces(down.shape[0], COLUMNS)):
         cut = pl.ds(at, size)
-        tall.append([pltpu.make_async_copy(down_any.at[0, cut, :], down.at[cut, :], sems_down.at[n])])
+        tall.append([pltpu.make_async_copy(stored.at[0, cut, :], down.at[cut, :], sems_down.at[n])])
     for copies in wide + tall:
         for copy in copies:
             copy.start()
@@ -163,32 +171,32 @@
         for copy in (wide, tall)[part][n]:
             copy.wait()
 
-    expert_body(xa, xb, mask, gate, up, down, ya, yb, x, hidden, ready)
-
-
-def expert_call(xa, xb, mask, weights, first=False):
-    rows, width = xa.shape
-    shapes = [w.shape[-2:] for w in weights]
-    hidden, features = shapes[0][1], shapes[2][0]
-    out = jax.ShapeDtypeStruct((rows, width), BF16)
-    kept = tuple(pltpu.VMEM(shape, BF16) for shape in shapes) if first else ()
+    expert_body(xs, mask, both, down, ys, x, hidden, ready)
+
+
+def expert_call(xs, mask, weights, splits, first=False):
+    rows, width = sum(splits), xs[0].shape[1]
+    features, hidden = weights[-1].shape[-2:]
+    outs = tuple(jax.ShapeDtypeStruct((split, width), BF16) for split in splits)
+    kept = (pltpu.VMEM((features, 2 * hidden), BF16), pltpu.VMEM((features, hidden), BF16)) if first else ()
     place = pl.BlockSpec(memory_space=pltpu.VMEM)
-    scratch = [pltpu.VMEM((2 * rows, width), BF16), pltpu.VMEM((2 * rows, hidden), BF16)]
+    scratch = [pltpu.VMEM((rows, width), BF16), pltpu.VMEM((rows, hidden), BF16)]
     if first:
         scratch += [
             pltpu.SemaphoreType.DMA((2 * len(pieces(hidden, UNITS)),)),
             pltpu.SemaphoreType.DMA((len(pieces(features, COLUMNS)),)),
         ]
     weights = [pltpu.with_memory_space_constraint(w, pltpu.HBM if first else pltpu.VMEM) for w in weights]
+    stay = pl.BlockSpec(memory_space=pl.ANY) if first else place
     return pl.pallas_call(
-        first_kernel if first else expert_kernel,
-        out_shape=(out, out, *kept),
-        in_specs=[place] * 3 + [pl.BlockSpec(memory_space=pl.ANY) if first else place] * 3,
-        out_specs=(place,) * (2 + len(kept)),
+        functools.partial(first_kernel if first else expert_kernel, len(xs), len(outs)),
+        out_shape=(*outs, *kept),
+        in_specs=[place] * (len(xs) + 1) + [stay] * len(weights),
+        out_specs=(place,) * (len(outs) + len(kept)),
         scratch_shapes=scratch,
         compiler_params=pltpu.CompilerParams(vmem_limit_bytes=16 * 2**20),
         cost_estimate=pl.CostEstimate(flops=0, bytes_accessed=0, transcendentals=0),
-    )(xa, xb, mask, *weights)
+    )(*xs, mask, *weights)
 
 
 def local_cube(tokens, norm_gain, expert_ids, gate_weights, gate_proj, up_proj, down_proj):
@@ -213,6 +221,11 @@
     def slice_bits(j):
         return lambda i: i ^ (j * experts)
 
+    def inner(array, outward):
+        low = [(i, i - experts if outward else i + experts) for i in range(experts, 2 * experts)]
+        high = [(i, i + experts if outward else i - experts) for i in range(2 * experts, 3 * experts)]
+        return lax.ppermute(array, "ex", low + high)
+
     rows = rows_call(tokens, norm_gain, expert_ids, gate_weights, experts, width)
     lane = jnp.arange(LANES, dtype=jnp.int32)[None, :] - features % LANES
     ours = (lane >= 0) & (lane < 3 * experts) & (lane % experts == mine)
@@ -225,21 +238,21 @@
         last[0] = value
         return value
 
-    def expert(xa, xb):
-        first_time = len(weights[0].shape) == 3
-        parts = expert_call(xa, xb, mask, weights, first_time)
+    def expert(xs, splits):
+        first_time = len(weights) == 3
+        parts = expert_call(xs, mask, weights, splits, first_time)
         if first_time:
-            weights[:] = parts[2:]
+            weights[:] = parts[len(splits) :]
         last[0] = parts[0]
-        return parts[:2]
-
-    def add(a, b):
-        return (a.astype(F32) + b.astype(F32)).astype(BF16)
+        return list(parts[: len(splits)])
 
     p1, p2, half, ch, cp, near, far, back, q2, q1, z, zb = ([None] * SLICES for _ in range(12))
 
+    one, two = tok_rows, 2 * tok_rows
+
     def gather_half(j, block):
-        half[j] = jnp.concatenate([block, order(p1[j])], axis=0)
+        p1[j] = order(p1[j])
+        half[j] = jnp.concatenate([block, p1[j]], axis=0)
         p2[j] = swap(half[j], second)
         ch[j] = swap(half[j], core)
 
@@ -247,23 +260,28 @@
         p2[j] = order(p2[j])
         cp[j] = swap(p2[j], core)
 
+    def run_early(j):
+        near[j] = expert([order(half[j])], [one, one])
+
+    def run_late(j):
+        far[j] = expert([order(p2[j])], [two])[0]
+
     def run_own(j):
-        near[j], far[j] = expert(order(half[j]), p2[j])
+        *near[j], far[j] = expert([order(half[j]), p2[j]], [one, one, two])
 
     def run_other(j):
         mine_half = order(ch[j])
-        back[j] = [swap(part, core) for part in expert(mine_half, order(cp[j]))]
+        back[j] = [swap(part, core) for part in expert([mine_half, order(cp[j])], [two, two])]
 
     def reduce_core(j):
-        q2[j] = swap(add(far[j], order(back[j][1])), second)
+        q2[j] = swap(total_of([far[j], order(back[j][1])]), second)
 
     def reduce_second(j):
-        arrived = order(q2[j])
-        near[j] = (near[j], order(back[j][0]), arrived)
-        q1[j] = swap(total_of([a[tok_rows:] for a in near[j]]), first)
+        q2[j], back[j] = order(q2[j]), order(back[j][0])
+        q1[j] = swap(total_of([near[j][1], back[j][one:], q2[j][one:]]), first)
 
     def reduce_first(j):
-        sums = total_of([a[:tok_rows] for a in near[j]] + [order(q1[j])])
+        sums = total_of([near[j][0], back[j][:one], q2[j][:one], order(q1[j])])
         zb[j] = swap(sums, slice_bits(j)) if j else sums
 
     def total_of(arrays):
@@ -271,20 +289,25 @@
 
     p1[0] = order(swap(rows, first))
     z[1] = order(swap(rows, slice_bits(1)))
-    z[2] = swap(order(rows), slice_bits(2))
+    z[3] = order(inner(rows, False))
+    z[2] = inner(z[1], False)
+    outward = inner(z[3], True)
     gather_half(0, rows)
     p1[1] = swap(z[1], first)
+    run_early(0)
     gather_half(1, z[1])
     gather_full(0)
-    run_own(0)
-    z[2] = order(z[2])
+    outward = order(outward)
+    crossed = order(z[2])
+    z[2] = crossed + outward
     p1[2] = swap(z[2], first)
-    z[3] = swap(order(rows), slice_bits(3))
-    run_other(0)
+    outward = inner(crossed, True)
+    run_late(0)
     gather_half(2, z[2])
     gather_full(1)
+    run_other(0)
     run_own(1)
-    z[3] = order(z[3])
+    z[3] = z[3] + order(outward)
     p1[3] = swap(z[3], first)
     run_other(1)
     gather_half(3, z[3])

time: 152 us -> 149 us (0.980)
  starting transfers between devices: 42.5 us -> 32.4 us
  waiting for transfers between devices: 69.2 us -> 74.7 us
    ppermute x38 -> x36, starting transfers between devices: 42.5 us -> 28.3 us  [swap(): return lax.ppermute(array, 'ex', [(i, partner(i)) for i in range(devices)])]
    ppermute x0 -> x4, waiting for transfers between devices: none -> 8.39 us  [inner(): return lax.ppermute(array, 'ex', low + high)]
    ppermute x0 -> x4, starting transfers between devices: none -> 4.11 us  [inner(): return lax.ppermute(array, 'ex', low + high)]
    ppermute x38 -> x36, waiting for transfers between devices: 69.2 us -> 66.3 us  [swap(): return lax.ppermute(array, 'ex', [(i, partner(i)) for i in range(devices)])]
    pallas_call x8 -> x9, Pallas kernels: 35.4 us -> 36.6 us  [expert_call(): pl.pallas_call(functools.partial(first_kernel if first else expert_kernel...]
  transfers between devices with their start and end apart: 38 -> 40, of which waited for: 15 -> 18; matrix products, arithmetic and copies ran while one was open for 1% -> 2% of each run, Pallas kernels for 23% -> 25%
where the time goes in v4:
time: 149 us
  waiting for transfers between devices  74.7 us (50%)
  Pallas kernels  37.9 us (25%)
  starting transfers between devices  32.4 us (22%)
  other arithmetic  3.3 us (2%)
    ppermute x36, waiting for transfers between devices, swap(): return lax.ppermute(array, 'ex', [(i, partner(i)) for i in range(devices)])  66.3 us
    pallas_call x9, Pallas kernels, expert_call(): pl.pallas_call(functools.partial(first_kernel if first else expert_kernel...  36.6 us
    ppermute x36, starting transfers between devices, swap(): return lax.ppermute(array, 'ex', [(i, partner(i)) for i in range(devices)])  28.3 us
    ppermute x4, waiting for transfers between devices, inner(): return lax.ppermute(array, 'ex', low + high)  8.39 us
    ppermute x4, starting transfers between devices, inner(): return lax.ppermute(array, 'ex', low + high)  4.11 us
  transfers between devices with their start and end apart: 40, of which 18 were waited for; matrix products, arithmetic and copies ran while one was open for 2% of the time, Pallas kernels for 25%

profile of v4, /device:TPU:0, one launch (start us, length us, event | category | flops | bytes accessed | tf_op | source)
XLA Modules:
  0.0 148.6 jit_solution(8686349272268136902)
XLA Ops:
  0.0 1.3 shard_map.73
  1.3 3.0 %collective-permute-start.1 = (bf16[64,2944]{1,0:T(8,128)(2,1)S(1)}, bf16[64,2944]{1,0:T(8,128)(2,1)S(1)}, u32[]{:S(2)}, u32[]{:S(2)}) collective-permute-start(bf16[64,2944]{1,0:T(8,128)(2,1)S(1)} %shard_map.73), channel_id=1, source_target_pairs={{0,2},{1,5},{2,0},{3,7},{4,6},{5,1},{6,4},{7,3},{8,10},{9,13},{10,... | collective-permute-start | bytes 1130504 | tf_op jit(solution)/shard_map/ppermute | solution.py:210
  4.3 1.6 %collective-permute-start = (bf16[64,2944]{1,0:T(8,128)(2,1)S(1)}, bf16[64,2944]{1,0:T(8,128)(2,1)S(1)}, u32[]{:S(2)}, u32[]{:S(2)}) collective-permute-start(bf16[64,2944]{1,0:T(8,128)(2,1)S(1)} %shard_map.73), channel_id=1, source_target_pairs={{0,8},{1,9},{2,10},{3,11},{4,12},{5,13},{6,14},{7,15},{8,0},{9,1},... | collective-permute-start | bytes 1130504 | tf_op jit(solution)/shard_map/ppermute | solution.py:210
  5.9 0.7 collective-permute-start.3
  6.6 3.3 %collective-permute-done.1 = bf16[64,2944]{1,0:T(8,128)(2,1)S(1)} collective-permute-done((bf16[64,2944]{1,0:T(8,128)(2,1)S(1)}, bf16[64,2944]{1,0:T(8,128)(2,1)S(1)}, u32[]{:S(2)}, u32[]{:S(2)}) %collective-permute-start.1) | collective-permute-done | bytes 376864 | tf_op jit(solution)/shard_map/ppermute | solution.py:210
  9.9 4.7 %collective-permute-done = bf16[64,2944]{1,0:T(8,128)(2,1)S(1)} collective-permute-done((bf16[64,2944]{1,0:T(8,128)(2,1)S(1)}, bf16[64,2944]{1,0:T(8,128)(2,1)S(1)}, u32[]{:S(2)}, u32[]{:S(2)}) %collective-permute-start) | collective-permute-done | bytes 376864 | tf_op jit(solution)/shard_map/ppermute | solution.py:210
  14.6 1.5 collective-permute-start.6
  16.1 0.6 collective-permute-start.5
  16.7 0.7 collective-permute-start.2
  17.4 1.3 collective-permute-start.4
  18.7 6.9 %shard_map.74 = (bf16[64,2944]{1,0:T(8,128)(2,1)S(1)}, bf16[64,2944]{1,0:T(8,128)(2,1)S(1)}, bf16[2880,1280]{1,0:T(8,128)(2,1)S(1)}, bf16[2880,640]{1,0:T(8,128)(2,1)S(1)}) custom-call(bf16[128,2944]{1,0:T(8,128)(2,1)S(1)} %pad_maximum_fusion.refs_0_, f32[1,128]{1,0:T(1,128)S(1)} %and_convert_fusion.refs_1_.refs_2_, bf16[1,2880,640]{2,1,0:T(8,128)(2,1)} %refs_2_.1, ...), custom_call_target="tpu_custom_call" | custom-call | tf_op jit(solution)/shard_map/pallas_call | solution.py:191
  25.6 0.6 collective-permute-done.6
  26.2 1.0 collective-permute-start.11
  27.2 0.7 collective-permute-done.5.refs_0_
  27.9 5.6 %collective-permute-done.4 = bf16[64,2944]{1,0:T(8,128)(2,1)S(1)} collective-permute-done((bf16[64,2944]{1,0:T(8,128)(2,1)S(1)}, bf16[64,2944]{1,0:T(8,128)(2,1)S(1)}, u32[]{:S(2)}, u32[]{:S(2)}) %collective-permute-start.4) | collective-permute-done | bytes 376864 | tf_op jit(solution)/shard_map/ppermute | solution.py:227
  34.5 2.5 %shard_map.75 = bf16[128,2944]{1,0:T(8,128)(2,1)S(1)} custom-call(bf16[128,2944]{1,0:T(8,128)(2,1)S(1)} %collective-permute-done.5.refs_0_, f32[1,128]{1,0:T(1,128)S(1)} %and_convert_fusion.refs_1_.refs_2_, bf16[2880,1280]{1,0:T(8,128)(2,1)S(1)} %get-tuple-element.85.refs_2_.refs_3_, bf16[2880,640]{1,0:T(8,128)(2,1)S(1)} %get-tuple-element.86.refs_3_.refs_4_), custom_call_target="tpu_custom_call" | custom-call | tf_op jit(solution)/shard_map/pallas_call | solution.py:191
  37.0 4.3 %collective-permute-done.7 = bf16[64,2944]{1,0:T(8,128)(2,1)S(1)} collective-permute-done((bf16[64,2944]{1,0:T(8,128)(2,1)S(1)}, bf16[64,2944]{1,0:T(8,128)(2,1)S(1)}, u32[]{:S(2)}, u32[]{:S(2)}) %collective-permute-start.7) | collective-permute-done | bytes 376864 | tf_op jit(solution)/shard_map/ppermute | solution.py:210
  41.3 1.5 collective-permute-start.9
  43.4 1.1 collective-permute-start.8
  44.5 3.9 %shard_map.76 = (bf16[128,2944]{1,0:T(8,128)(2,1)S(1)}, bf16[128,2944]{1,0:T(8,128)(2,1)S(1)}) custom-call(bf16[128,2944]{1,0:T(8,128)(2,1)S(1)} %collective-permute-done.10.refs_0_, bf16[128,2944]{1,0:T(8,128)(2,1)S(1)} %collective-permute-done.12.refs_1_, f32[1,128]{1,0:T(1,128)S(1)} %and_convert_fusion.refs_1_.refs_2_, ...), custom_call_target="tpu_custom_call" | custom-call | tf_op jit(solution)/shard_map/pallas_call | solution.py:191
  48.4 3.9 %shard_map.77 = (bf16[64,2944]{1,0:T(8,128)(2,1)S(1)}, bf16[64,2944]{1,0:T(8,128)(2,1)S(1)}, bf16[128,2944]{1,0:T(8,128)(2,1)S(1)}) custom-call(bf16[128,2944]{1,0:T(8,128)(2,1)S(1)} %constant_dynamic-update-slice_fusion.refs_0_, bf16[128,2944]{1,0:T(8,128)(2,1)S(1)} %collective-permute-done.11.refs_1_, f32[1,128]{1,0:T(1,128)S(1)} %and_convert_fusion.refs_1_.refs_2_, ...), custom_call_target="tpu_custom_call" | custom-call | tf_op jit(solution)/shard_map/pallas_call | solution.py:191
  52.2 2.8 %collective-permute-done.9 = bf16[64,2944]{1,0:T(8,128)(2,1)S(1)} collective-permute-done((bf16[64,2944]{1,0:T(8,128)(2,1)S(1)}, bf16[64,2944]{1,0:T(8,128)(2,1)S(1)}, u32[]{:S(2)}, u32[]{:S(2)}) %collective-permute-start.9) | collective-permute-done | bytes 376864 | tf_op jit(solution)/shard_map/ppermute | solution.py:227
  55.1 1.5 %collective-permute-start.13 = (bf16[64,2944]{1,0:T(8,128)(2,1)S(1)}, bf16[64,2944]{1,0:T(8,128)(2,1)S(1)}, u32[]{:S(2)}, u32[]{:S(2)}) collective-permute-start(bf16[64,2944]{1,0:T(8,128)(2,1)S(1)} %add.117), channel_id=1, source_target_pairs={{0,2},{1,5},{2,0},{3,7},{4,6},{5,1},{6,4},{7,3},{8,10},{9,13},{10,... | collective-permute-start | bytes 1130504 | tf_op jit(solution)/shard_map/ppermute | solution.py:210
  56.7 3.9 %shard_map.78 = (bf16[128,2944]{1,0:T(8,128)(2,1)S(1)}, bf16[128,2944]{1,0:T(8,128)(2,1)S(1)}) custom-call(bf16[128,2944]{1,0:T(8,128)(2,1)S(1)} %collective-permute-done.14.refs_0_, bf16[128,2944]{1,0:T(8,128)(2,1)S(1)} %collective-permute-done.15.refs_1_, f32[1,128]{1,0:T(1,128)S(1)} %and_convert_fusion.refs_1_.refs_2_, ...), custom_call_target="tpu_custom_call" | custom-call | tf_op jit(solution)/shard_map/pallas_call | solution.py:191
  60.5 2.2 %collective-permute-done.13 = bf16[64,2944]{1,0:T(8,128)(2,1)S(1)} collective-permute-done((bf16[64,2944]{1,0:T(8,128)(2,1)S(1)}, bf16[64,2944]{1,0:T(8,128)(2,1)S(1)}, u32[]{:S(2)}, u32[]{:S(2)}) %collective-permute-start.13) | collective-permute-done | bytes 376864 | tf_op jit(solution)/shard_map/ppermute | solution.py:210
  63.4 1.2 collective-permute-start.20
  64.6 4.1 %shard_map.79 = (bf16[64,2944]{1,0:T(8,128)(2,1)S(1)}, bf16[64,2944]{1,0:T(8,128)(2,1)S(1)}, bf16[128,2944]{1,0:T(8,128)(2,1)S(1)}) custom-call(bf16[128,2944]{1,0:T(8,128)(2,1)S(1)} %pad_maximum_fusion.1.refs_0_, bf16[128,2944]{1,0:T(8,128)(2,1)S(1)} %collective-permute-done.8.refs_1_, f32[1,128]{1,0:T(1,128)S(1)} %and_convert_fusion.refs_1_.refs_2_, ...), custom_call_target="tpu_custom_call" | custom-call | tf_op jit(solution)/shard_map/pallas_call | solution.py:191
  68.7 3.9 %shard_map.80 = (bf16[128,2944]{1,0:T(8,128)(2,1)S(1)}, bf16[128,2944]{1,0:T(8,128)(2,1)S(1)}) custom-call(bf16[128,2944]{1,0:T(8,128)(2,1)S(1)} %collective-permute-done.16.refs_0_, bf16[128,2944]{1,0:T(8,128)(2,1)S(1)} %collective-permute-done.17.refs_1_, f32[1,128]{1,0:T(1,128)S(1)} %and_convert_fusion.refs_1_.refs_2_, ...), custom_call_target="tpu_custom_call" | custom-call | tf_op jit(solution)/shard_map/pallas_call | solution.py:191
  73.2 1.3 collective-permute-done.21.refs_1_
  75.4 1.6 %collective-permute-start.22 = (bf16[128,2944]{1,0:T(8,128)(2,1)S(1)}, bf16[128,2944]{1,0:T(8,128)(2,1)S(1)}, u32[]{:S(2)}, u32[]{:S(2)}) collective-permute-start(bf16[128,2944]{1,0:T(8,128)(2,1)S(1)} %add_convert_fusion.3), channel_id=1, source_target_pairs={{0,4},{1,3},{2,6},{3,1},{4,0},{5,7},{6,2},{7,5},{8,12},{9,11},{10,... | collective-permute-start | bytes 2261000 | tf_op jit(solution)/shard_map/ppermute | solution.py:210
  77.2 3.8 %shard_map.81 = (bf16[64,2944]{1,0:T(8,128)(2,1)S(1)}, bf16[64,2944]{1,0:T(8,128)(2,1)S(1)}, bf16[128,2944]{1,0:T(8,128)(2,1)S(1)}) custom-call(bf16[128,2944]{1,0:T(8,128)(2,1)S(1)} %pad_maximum_fusion.2.refs_0_, bf16[128,2944]{1,0:T(8,128)(2,1)S(1)} %collective-permute-done.21.refs_1_, f32[1,128]{1,0:T(1,128)S(1)} %and_convert_fusion.refs_1_.refs_2_, ...), custom_call_target="tpu_custom_call" | custom-call | tf_op jit(solution)/shard_map/pallas_call | solution.py:191
  81.5 3.8 %shard_map.82 = (bf16[128,2944]{1,0:T(8,128)(2,1)S(1)}, bf16[128,2944]{1,0:T(8,128)(2,1)S(1)}) custom-call(bf16[128,2944]{1,0:T(8,128)(2,1)S(1)} %collective-permute-done.25.refs_0_, bf16[128,2944]{1,0:T(8,128)(2,1)S(1)} %collective-permute-done.26.refs_1_, f32[1,128]{1,0:T(1,128)S(1)} %and_convert_fusion.refs_1_.refs_2_, ...), custom_call_target="tpu_custom_call" | custom-call | tf_op jit(solution)/shard_map/pallas_call | solution.py:191
  85.4 1.1 collective-permute-done.24
  87.1 7.4 %collective-permute-done.22 = bf16[128,2944]{1,0:T(8,128)(2,1)S(1)} collective-permute-done((bf16[128,2944]{1,0:T(8,128)(2,1)S(1)}, bf16[128,2944]{1,0:T(8,128)(2,1)S(1)}, u32[]{:S(2)}, u32[]{:S(2)}) %collective-permute-start.22) | collective-permute-done | bytes 753696 | tf_op jit(solution)/shard_map/ppermute | solution.py:210
  94.5 1.5 collective-permute-start.28
  96.1 0.6 collective-permute-start.27
  96.7 5.4 %collective-permute-done.28 = bf16[64,2944]{1,0:T(8,128)(2,1)S(1)} collective-permute-done((bf16[64,2944]{1,0:T(8,128)(2,1)S(1)}, bf16[64,2944]{1,0:T(8,128)(2,1)S(1)}, u32[]{:S(2)}, u32[]{:S(2)}) %collective-permute-start.28) | collective-permute-done | bytes 376864 | tf_op jit(solution)/shard_map/ppermute | solution.py:210
  102.8 5.7 %collective-permute-done.27 = bf16[64,2944]{1,0:T(8,128)(2,1)S(1)} collective-permute-done((bf16[64,2944]{1,0:T(8,128)(2,1)S(1)}, bf16[64,2944]{1,0:T(8,128)(2,1)S(1)}, u32[]{:S(2)}, u32[]{:S(2)}) %collective-permute-start.27) | collective-permute-done | bytes 376864 | tf_op jit(solution)/shard_map/ppermute | solution.py:210
  109.4 2.7 %collective-permute-start.30 = (bf16[64,2944]{1,0:T(8,128)(2,1)S(1)}, bf16[64,2944]{1,0:T(8,128)(2,1)S(1)}, u32[]{:S(2)}, u32[]{:S(2)}) collective-permute-start(bf16[64,2944]{1,0:T(8,128)(2,1)S(1)} %add_convert_fusion.10), channel_id=1, source_target_pairs={{0,16},{1,17},{2,18},{3,19},{4,20},{5,21},{6,22},{7,23},{8,24},{9,... | collective-permute-start | bytes 1130504 | tf_op jit(solution)/shard_map/ppermute | solution.py:210
  112.1 1.9 %collective-permute-done.32 = bf16[128,2944]{1,0:T(8,128)(2,1)S(1)} collective-permute-done((bf16[128,2944]{1,0:T(8,128)(2,1)S(1)}, bf16[128,2944]{1,0:T(8,128)(2,1)S(1)}, u32[]{:S(2)}, u32[]{:S(2)}) %collective-permute-start.32) | collective-permute-done | bytes 753696 | tf_op jit(solution)/shard_map/ppermute | solution.py:210
  114.1 1.5 %collective-permute-start.36 = (bf16[64,2944]{1,0:T(8,128)(2,1)S(1)}, bf16[64,2944]{1,0:T(8,128)(2,1)S(1)}, u32[]{:S(2)}, u32[]{:S(2)}) collective-permute-start(bf16[64,2944]{1,0:T(8,128)(2,1)S(1)} %add_convert_fusion.9), channel_id=1, source_target_pairs={{0,2},{1,5},{2,0},{3,7},{4,6},{5,1},{6,4},{7,3},{8,10},{9,13},{10,... | collective-permute-start | bytes 1130504 | tf_op jit(solution)/shard_map/ppermute | solution.py:210
  115.7 10.6 %collective-permute-done.30 = bf16[64,2944]{1,0:T(8,128)(2,1)S(1)} collective-permute-done((bf16[64,2944]{1,0:T(8,128)(2,1)S(1)}, bf16[64,2944]{1,0:T(8,128)(2,1)S(1)}, u32[]{:S(2)}, u32[]{:S(2)}) %collective-permute-start.30) | collective-permute-done | bytes 376864 | tf_op jit(solution)/shard_map/ppermute | solution.py:210
  126.6 1.4 collective-permute-start.37
  128.0 2.0 %collective-permute-start.38 = (bf16[64,2944]{1,0:T(8,128)(2,1)S(1)}, bf16[64,2944]{1,0:T(8,128)(2,1)S(1)}, u32[]{:S(2)}, u32[]{:S(2)}) collective-permute-start(bf16[64,2944]{1,0:T(8,128)(2,1)S(1)} %add_convert_fusion.7), channel_id=1, source_target_pairs={{0,24},{1,25},{2,26},{3,27},{4,28},{5,29},{6,30},{7,31},{8,16},{9,... | collective-permute-start | bytes 1130504 | tf_op jit(solution)/shard_map/ppermute | solution.py:210
  130.4 3.9 %collective-permute-done.37 = bf16[64,2944]{1,0:T(8,128)(2,1)S(1)} collective-permute-done((bf16[64,2944]{1,0:T(8,128)(2,1)S(1)}, bf16[64,2944]{1,0:T(8,128)(2,1)S(1)}, u32[]{:S(2)}, u32[]{:S(2)}) %collective-permute-start.37) | collective-permute-done | bytes 376864 | tf_op jit(solution)/shard_map/ppermute | solution.py:210
  134.3 7.2 %collective-permute-done.38 = bf16[64,2944]{1,0:T(8,128)(2,1)S(1)} collective-permute-done((bf16[64,2944]{1,0:T(8,128)(2,1)S(1)}, bf16[64,2944]{1,0:T(8,128)(2,1)S(1)}, u32[]{:S(2)}, u32[]{:S(2)}) %collective-permute-start.38) | collective-permute-done | bytes 376864 | tf_op jit(solution)/shard_map/ppermute | solution.py:210
  141.7 5.9 %collective-permute-done.39 = bf16[64,2944]{1,0:T(8,128)(2,1)S(1)} collective-permute-done((bf16[64,2944]{1,0:T(8,128)(2,1)S(1)}, bf16[64,2944]{1,0:T(8,128)(2,1)S(1)}, u32[]{:S(2)}, u32[]{:S(2)}) %collective-permute-start.39) | collective-permute-done | bytes 376864 | tf_op jit(solution)/shard_map/ppermute | solution.py:210
  147.7 1.0 add_convert_fusion.4
  (63 shorter events, 7.9 us)
Async XLA Ops:
  1.3 8.6 %collective-permute-start.1 = (bf16[64,2944]{1,0:T(8,128)(2,1)S(1)}, bf16[64,2944]{1,0:T(8,128)(2,1)S(1)}, u32[]{:S(2)}, u32[]{:S(2)}) collective-permute-start(bf16[64,2944]{1,0:T(8,128)(2,1)S(1)} %shard_map.73), channel_id=1, source_target_pairs={{0,2},{1,5},{2,0},{3,7},{4,6},{5,1},{6,4},{7,3},{8,10},{9,13},{10,... | collective-permute-start | bytes 1130504 | tf_op jit(solution)/shard_map/ppermute | solution.py:210
  4.3 10.3 %collective-permute-start = (bf16[64,2944]{1,0:T(8,128)(2,1)S(1)}, bf16[64,2944]{1,0:T(8,128)(2,1)S(1)}, u32[]{:S(2)}, u32[]{:S(2)}) collective-permute-start(bf16[64,2944]{1,0:T(8,128)(2,1)S(1)} %shard_map.73), channel_id=1, source_target_pairs={{0,8},{1,9},{2,10},{3,11},{4,12},{5,13},{6,14},{7,15},{8,0},{9,1},... | collective-permute-start | bytes 1130504 | tf_op jit(solution)/shard_map/ppermute | solution.py:210
  5.9 10.1 %collective-permute-start.3 = (bf16[64,2944]{1,0:T(8,128)(2,1)S(1)}, bf16[64,2944]{1,0:T(8,128)(2,1)S(1)}, u32[]{:S(2)}, u32[]{:S(2)}) collective-permute-start(bf16[64,2944]{1,0:T(8,128)(2,1)S(1)} %shard_map.73), channel_id=1, source_target_pairs={{8,16},{9,17},{10,18},{11,19},{12,20},{13,21},{14,22},{15,23},{16,... | collective-permute-start | bytes 1130504 | tf_op jit(solution)/shard_map/ppermute | solution.py:227
  14.6 11.6 %collective-permute-start.6 = (bf16[64,2944]{1,0:T(8,128)(2,1)S(1)}, bf16[64,2944]{1,0:T(8,128)(2,1)S(1)}, u32[]{:S(2)}, u32[]{:S(2)}) collective-permute-start(bf16[64,2944]{1,0:T(8,128)(2,1)S(1)} %collective-permute-done), channel_id=1, source_target_pairs={{0,2},{1,5},{2,0},{3,7},{4,6},{5,1},{6,4},{7,3},{8,10},{9,13},{10,... | collective-permute-start | bytes 1130504 | tf_op jit(solution)/shard_map/ppermute | solution.py:210
  16.1 11.9 %collective-permute-start.5 = (bf16[128,2944]{1,0:T(8,128)(2,1)S(1)}, bf16[128,2944]{1,0:T(8,128)(2,1)S(1)}, u32[]{:S(2)}, u32[]{:S(2)}) collective-permute-start(bf16[128,2944]{1,0:T(8,128)(2,1)S(1)} %pad_maximum_fusion.refs_0_), channel_id=1, source_target_pairs={{0,4},{1,3},{2,6},{3,1},{4,0},{5,7},{6,2},{7,5},{8,12},{9,11},{10,... | collective-permute-start | bytes 2261000 | tf_op jit(solution)/shard_map/ppermute | solution.py:210
  16.7 16.8 %collective-permute-start.2 = (bf16[64,2944]{1,0:T(8,128)(2,1)S(1)}, bf16[64,2944]{1,0:T(8,128)(2,1)S(1)}, u32[]{:S(2)}, u32[]{:S(2)}) collective-permute-start(bf16[64,2944]{1,0:T(8,128)(2,1)S(1)} %collective-permute-done), channel_id=1, source_target_pairs={{8,16},{9,17},{10,18},{11,19},{12,20},{13,21},{14,22},{15,23},{16,... | collective-permute-start | bytes 1130504 | tf_op jit(solution)/shard_map/ppermute | solution.py:227
  17.4 16.1 %collective-permute-start.4 = (bf16[64,2944]{1,0:T(8,128)(2,1)S(1)}, bf16[64,2944]{1,0:T(8,128)(2,1)S(1)}, u32[]{:S(2)}, u32[]{:S(2)}) collective-permute-start(bf16[64,2944]{1,0:T(8,128)(2,1)S(1)} %collective-permute-done.3), channel_id=1, source_target_pairs={{8,0},{9,1},{10,2},{11,3},{12,4},{13,5},{14,6},{15,7},{16,24},{17,... | collective-permute-start | bytes 1130504 | tf_op jit(solution)/shard_map/ppermute | solution.py:227
  26.2 16.6 %collective-permute-start.11 = (bf16[128,2944]{1,0:T(8,128)(2,1)S(1)}, bf16[128,2944]{1,0:T(8,128)(2,1)S(1)}, u32[]{:S(2)}, u32[]{:S(2)}) collective-permute-start(bf16[128,2944]{1,0:T(8,128)(2,1)S(1)} %constant_dynamic-update-slice_fusion.refs_0_), channel_id=1, source_target_pairs={{0,4},{1,3},{2,6},{3,1},{4,0},{5,7},{6,2},{7,5},{8,12},{9,11},{10,... | collective-permute-start | bytes 2261000 | tf_op jit(solution)/shard_map/ppermute | solution.py:210
  27.2 16.2 %collective-permute-start.10 = (bf16[128,2944]{1,0:T(8,128)(2,1)S(1)}, bf16[128,2944]{1,0:T(8,128)(2,1)S(1)}, u32[]{:S(2)}, u32[]{:S(2)}) collective-permute-start(bf16[128,2944]{1,0:T(8,128)(2,1)S(1)} %pad_maximum_fusion.refs_0_), channel_id=1, source_target_pairs={{0,1},{1,0},{2,3},{3,2},{4,5},{5,4},{6,7},{7,6},{8,9},{9,8},{10,11... | collective-permute-start | bytes 2261000 | tf_op jit(solution)/shard_map/ppermute | solution.py:210
  33.6 7.7 %collective-permute-start.7 = (bf16[64,2944]{1,0:T(8,128)(2,1)S(1)}, bf16[64,2944]{1,0:T(8,128)(2,1)S(1)}, u32[]{:S(2)}, u32[]{:S(2)}) collective-permute-start(bf16[64,2944]{1,0:T(8,128)(2,1)S(1)} %add.116), channel_id=1, source_target_pairs={{0,2},{1,5},{2,0},{3,7},{4,6},{5,1},{6,4},{7,3},{8,10},{9,13},{10,... | collective-permute-start | bytes 1130504 | tf_op jit(solution)/shard_map/ppermute | solution.py:210
  34.0 10.5 %collective-permute-start.12 = (bf16[128,2944]{1,0:T(8,128)(2,1)S(1)}, bf16[128,2944]{1,0:T(8,128)(2,1)S(1)}, u32[]{:S(2)}, u32[]{:S(2)}) collective-permute-start(bf16[128,2944]{1,0:T(8,128)(2,1)S(1)} %collective-permute-done.5.refs_0_), channel_id=1, source_target_pairs={{0,1},{1,0},{2,3},{3,2},{4,5},{5,4},{6,7},{7,6},{8,9},{9,8},{10,11... | collective-permute-start | bytes 2261000 | tf_op jit(solution)/shard_map/ppermute | solution.py:210
  34.0 22.6 %collective-permute-start.14 = (bf16[128,2944]{1,0:T(8,128)(2,1)S(1)}, bf16[128,2944]{1,0:T(8,128)(2,1)S(1)}, u32[]{:S(2)}, u32[]{:S(2)}) collective-permute-start(bf16[128,2944]{1,0:T(8,128)(2,1)S(1)} %constant_dynamic-update-slice_fusion.refs_0_), channel_id=1, source_target_pairs={{0,1},{1,0},{2,3},{3,2},{4,5},{5,4},{6,7},{7,6},{8,9},{9,8},{10,11... | collective-permute-start | bytes 2261000 | tf_op jit(solution)/shard_map/ppermute | solution.py:210
  41.3 13.7 %collective-permute-start.9 = (bf16[64,2944]{1,0:T(8,128)(2,1)S(1)}, bf16[64,2944]{1,0:T(8,128)(2,1)S(1)}, u32[]{:S(2)}, u32[]{:S(2)}) collective-permute-start(bf16[64,2944]{1,0:T(8,128)(2,1)S(1)} %collective-permute-done.2), channel_id=1, source_target_pairs={{8,0},{9,1},{10,2},{11,3},{12,4},{13,5},{14,6},{15,7},{16,24},{17,... | collective-permute-start | bytes 1130504 | tf_op jit(solution)/shard_map/ppermute | solution.py:227
  42.8 13.8 %collective-permute-start.15 = (bf16[128,2944]{1,0:T(8,128)(2,1)S(1)}, bf16[128,2944]{1,0:T(8,128)(2,1)S(1)}, u32[]{:S(2)}, u32[]{:S(2)}) collective-permute-start(bf16[128,2944]{1,0:T(8,128)(2,1)S(1)} %collective-permute-done.11.refs_1_), channel_id=1, source_target_pairs={{0,1},{1,0},{2,3},{3,2},{4,5},{5,4},{6,7},{7,6},{8,9},{9,8},{10,11... | collective-permute-start | bytes 2261000 | tf_op jit(solution)/shard_map/ppermute | solution.py:210
  43.4 19.4 %collective-permute-start.8 = (bf16[128,2944]{1,0:T(8,128)(2,1)S(1)}, bf16[128,2944]{1,0:T(8,128)(2,1)S(1)}, u32[]{:S(2)}, u32[]{:S(2)}) collective-permute-start(bf16[128,2944]{1,0:T(8,128)(2,1)S(1)} %pad_maximum_fusion.1.refs_0_), channel_id=1, source_target_pairs={{0,4},{1,3},{2,6},{3,1},{4,0},{5,7},{6,2},{7,5},{8,12},{9,11},{10,... | collective-permute-start | bytes 2261000 | tf_op jit(solution)/shard_map/ppermute | solution.py:210
  55.1 7.7 %collective-permute-start.13 = (bf16[64,2944]{1,0:T(8,128)(2,1)S(1)}, bf16[64,2944]{1,0:T(8,128)(2,1)S(1)}, u32[]{:S(2)}, u32[]{:S(2)}) collective-permute-start(bf16[64,2944]{1,0:T(8,128)(2,1)S(1)} %add.117), channel_id=1, source_target_pairs={{0,2},{1,5},{2,0},{3,7},{4,6},{5,1},{6,4},{7,3},{8,10},{9,13},{10,... | collective-permute-start | bytes 1130504 | tf_op jit(solution)/shard_map/ppermute | solution.py:210
  56.6 12.0 %collective-permute-start.16 = (bf16[128,2944]{1,0:T(8,128)(2,1)S(1)}, bf16[128,2944]{1,0:T(8,128)(2,1)S(1)}, u32[]{:S(2)}, u32[]{:S(2)}) collective-permute-start(bf16[128,2944]{1,0:T(8,128)(2,1)S(1)} %pad_maximum_fusion.1.refs_0_), channel_id=1, source_target_pairs={{0,1},{1,0},{2,3},{3,2},{4,5},{5,4},{6,7},{7,6},{8,9},{9,8},{10,11... | collective-permute-start | bytes 2261000 | tf_op jit(solution)/shard_map/ppermute | solution.py:210
  62.8 5.9 %collective-permute-start.17 = (bf16[128,2944]{1,0:T(8,128)(2,1)S(1)}, bf16[128,2944]{1,0:T(8,128)(2,1)S(1)}, u32[]{:S(2)}, u32[]{:S(2)}) collective-permute-start(bf16[128,2944]{1,0:T(8,128)(2,1)S(1)} %collective-permute-done.8.refs_1_), channel_id=1, source_target_pairs={{0,1},{1,0},{2,3},{3,2},{4,5},{5,4},{6,7},{7,6},{8,9},{9,8},{10,11... | collective-permute-start | bytes 2261000 | tf_op jit(solution)/shard_map/ppermute | solution.py:210
  62.8 11.7 %collective-permute-start.21 = (bf16[128,2944]{1,0:T(8,128)(2,1)S(1)}, bf16[128,2944]{1,0:T(8,128)(2,1)S(1)}, u32[]{:S(2)}, u32[]{:S(2)}) collective-permute-start(bf16[128,2944]{1,0:T(8,128)(2,1)S(1)} %pad_maximum_fusion.2.refs_0_), channel_id=1, source_target_pairs={{0,4},{1,3},{2,6},{3,1},{4,0},{5,7},{6,2},{7,5},{8,12},{9,11},{10,... | collective-permute-start | bytes 2261000 | tf_op jit(solution)/shard_map/ppermute | solution.py:210
  63.4 11.2 %collective-permute-start.20 = (bf16[128,2944]{1,0:T(8,128)(2,1)S(1)}, bf16[128,2944]{1,0:T(8,128)(2,1)S(1)}, u32[]{:S(2)}, u32[]{:S(2)}) collective-permute-start(bf16[128,2944]{1,0:T(8,128)(2,1)S(1)} %get-tuple-element.107), channel_id=1, source_target_pairs={{0,1},{1,0},{2,3},{3,2},{4,5},{5,4},{6,7},{7,6},{8,9},{9,8},{10,11... | collective-permute-start | bytes 2261000 | tf_op jit(solution)/shard_map/ppermute | solution.py:210
  72.6 2.7 %collective-permute-start.19 = (bf16[128,2944]{1,0:T(8,128)(2,1)S(1)}, bf16[128,2944]{1,0:T(8,128)(2,1)S(1)}, u32[]{:S(2)}, u32[]{:S(2)}) collective-permute-start(bf16[128,2944]{1,0:T(8,128)(2,1)S(1)} %get-tuple-element.106), channel_id=1, source_target_pairs={{0,1},{1,0},{2,3},{3,2},{4,5},{5,4},{6,7},{7,6},{8,9},{9,8},{10,11... | collective-permute-start | bytes 2261000 | tf_op jit(solution)/shard_map/ppermute | solution.py:210
  72.6 13.8 %collective-permute-start.23 = (bf16[128,2944]{1,0:T(8,128)(2,1)S(1)}, bf16[128,2944]{1,0:T(8,128)(2,1)S(1)}, u32[]{:S(2)}, u32[]{:S(2)}) collective-permute-start(bf16[128,2944]{1,0:T(8,128)(2,1)S(1)} %get-tuple-element.97), channel_id=1, source_target_pairs={{0,1},{1,0},{2,3},{3,2},{4,5},{5,4},{6,7},{7,6},{8,9},{9,8},{10,11... | collective-permute-start | bytes 2261000 | tf_op jit(solution)/shard_map/ppermute | solution.py:210
  73.1 3.9 %collective-permute-start.25 = (bf16[128,2944]{1,0:T(8,128)(2,1)S(1)}, bf16[128,2944]{1,0:T(8,128)(2,1)S(1)}, u32[]{:S(2)}, u32[]{:S(2)}) collective-permute-start(bf16[128,2944]{1,0:T(8,128)(2,1)S(1)} %pad_maximum_fusion.2.refs_0_), channel_id=1, source_target_pairs={{0,1},{1,0},{2,3},{3,2},{4,5},{5,4},{6,7},{7,6},{8,9},{9,8},{10,11... | collective-permute-start | bytes 2261000 | tf_op jit(solution)/shard_map/ppermute | solution.py:210
  74.5 6.5 %collective-permute-start.26 = (bf16[128,2944]{1,0:T(8,128)(2,1)S(1)}, bf16[128,2944]{1,0:T(8,128)(2,1)S(1)}, u32[]{:S(2)}, u32[]{:S(2)}) collective-permute-start(bf16[128,2944]{1,0:T(8,128)(2,1)S(1)} %collective-permute-done.21.refs_1_), channel_id=1, source_target_pairs={{0,1},{1,0},{2,3},{3,2},{4,5},{5,4},{6,7},{7,6},{8,9},{9,8},{10,11... | collective-permute-start | bytes 2261000 | tf_op jit(solution)/shard_map/ppermute | solution.py:210
  74.7 11.7 %collective-permute-start.24 = (bf16[128,2944]{1,0:T(8,128)(2,1)S(1)}, bf16[128,2944]{1,0:T(8,128)(2,1)S(1)}, u32[]{:S(2)}, u32[]{:S(2)}) collective-permute-start(bf16[128,2944]{1,0:T(8,128)(2,1)S(1)} %add_convert_fusion.2), channel_id=1, source_target_pairs={{0,4},{1,3},{2,6},{3,1},{4,0},{5,7},{6,2},{7,5},{8,12},{9,11},{10,... | collective-permute-start | bytes 2261000 | tf_op jit(solution)/shard_map/ppermute | solution.py:210
  75.4 19.1 %collective-permute-start.22 = (bf16[128,2944]{1,0:T(8,128)(2,1)S(1)}, bf16[128,2944]{1,0:T(8,128)(2,1)S(1)}, u32[]{:S(2)}, u32[]{:S(2)}) collective-permute-start(bf16[128,2944]{1,0:T(8,128)(2,1)S(1)} %add_convert_fusion.3), channel_id=1, source_target_pairs={{0,4},{1,3},{2,6},{3,1},{4,0},{5,7},{6,2},{7,5},{8,12},{9,11},{10,... | collective-permute-start | bytes 2261000 | tf_op jit(solution)/shard_map/ppermute | solution.py:210
  77.1 18.9 %collective-permute-start.18 = (bf16[128,2944]{1,0:T(8,128)(2,1)S(1)}, bf16[128,2944]{1,0:T(8,128)(2,1)S(1)}, u32[]{:S(2)}, u32[]{:S(2)}) collective-permute-start(bf16[128,2944]{1,0:T(8,128)(2,1)S(1)} %get-tuple-element.104), channel_id=1, source_target_pairs={{0,1},{1,0},{2,3},{3,2},{4,5},{5,4},{6,7},{7,6},{8,9},{9,8},{10,11... | collective-permute-start | bytes 2261000 | tf_op jit(solution)/shard_map/ppermute | solution.py:210
  81.0 27.4 %collective-permute-start.33 = (bf16[128,2944]{1,0:T(8,128)(2,1)S(1)}, bf16[128,2944]{1,0:T(8,128)(2,1)S(1)}, u32[]{:S(2)}, u32[]{:S(2)}) collective-permute-start(bf16[128,2944]{1,0:T(8,128)(2,1)S(1)} %get-tuple-element.128), channel_id=1, source_target_pairs={{0,1},{1,0},{2,3},{3,2},{4,5},{5,4},{6,7},{7,6},{8,9},{9,8},{10,11... | collective-permute-start | bytes 2261000 | tf_op jit(solution)/shard_map/ppermute | solution.py:210
  86.4 27.6 %collective-permute-start.31 = (bf16[128,2944]{1,0:T(8,128)(2,1)S(1)}, bf16[128,2944]{1,0:T(8,128)(2,1)S(1)}, u32[]{:S(2)}, u32[]{:S(2)}) collective-permute-start(bf16[128,2944]{1,0:T(8,128)(2,1)S(1)} %get-tuple-element.116), channel_id=1, source_target_pairs={{0,1},{1,0},{2,3},{3,2},{4,5},{5,4},{6,7},{7,6},{8,9},{9,8},{10,11... | collective-permute-start | bytes 2261000 | tf_op jit(solution)/shard_map/ppermute | solution.py:210
  86.4 10.3 %collective-permute-start.29 = (bf16[128,2944]{1,0:T(8,128)(2,1)S(1)}, bf16[128,2944]{1,0:T(8,128)(2,1)S(1)}, u32[]{:S(2)}, u32[]{:S(2)}) collective-permute-start(bf16[128,2944]{1,0:T(8,128)(2,1)S(1)} %get-tuple-element.123), channel_id=1, source_target_pairs={{0,1},{1,0},{2,3},{3,2},{4,5},{5,4},{6,7},{7,6},{8,9},{9,8},{10,11... | collective-permute-start | bytes 2261000 | tf_op jit(solution)/shard_map/ppermute | solution.py:210
  94.5 7.6 %collective-permute-start.28 = (bf16[64,2944]{1,0:T(8,128)(2,1)S(1)}, bf16[64,2944]{1,0:T(8,128)(2,1)S(1)}, u32[]{:S(2)}, u32[]{:S(2)}) collective-permute-start(bf16[64,2944]{1,0:T(8,128)(2,1)S(1)} %add_convert_fusion.11), channel_id=1, source_target_pairs={{0,2},{1,5},{2,0},{3,7},{4,6},{5,1},{6,4},{7,3},{8,10},{9,13},{10,... | collective-permute-start | bytes 1130504 | tf_op jit(solution)/shard_map/ppermute | solution.py:210
  96.1 12.3 %collective-permute-start.27 = (bf16[64,2944]{1,0:T(8,128)(2,1)S(1)}, bf16[64,2944]{1,0:T(8,128)(2,1)S(1)}, u32[]{:S(2)}, u32[]{:S(2)}) collective-permute-start(bf16[64,2944]{1,0:T(8,128)(2,1)S(1)} %add_convert_fusion.12), channel_id=1, source_target_pairs={{0,2},{1,5},{2,0},{3,7},{4,6},{5,1},{6,4},{7,3},{8,10},{9,13},{10,... | collective-permute-start | bytes 1130504 | tf_op jit(solution)/shard_map/ppermute | solution.py:210
  102.3 11.7 %collective-permute-start.32 = (bf16[128,2944]{1,0:T(8,128)(2,1)S(1)}, bf16[128,2944]{1,0:T(8,128)(2,1)S(1)}, u32[]{:S(2)}, u32[]{:S(2)}) collective-permute-start(bf16[128,2944]{1,0:T(8,128)(2,1)S(1)} %add_convert_fusion.1), channel_id=1, source_target_pairs={{0,4},{1,3},{2,6},{3,1},{4,0},{5,7},{6,2},{7,5},{8,12},{9,11},{10,... | collective-permute-start | bytes 2261000 | tf_op jit(solution)/shard_map/ppermute | solution.py:210
  108.7 17.6 %collective-permute-start.35 = (bf16[128,2944]{1,0:T(8,128)(2,1)S(1)}, bf16[128,2944]{1,0:T(8,128)(2,1)S(1)}, u32[]{:S(2)}, u32[]{:S(2)}) collective-permute-start(bf16[128,2944]{1,0:T(8,128)(2,1)S(1)} %add_convert_fusion), channel_id=1, source_target_pairs={{0,4},{1,3},{2,6},{3,1},{4,0},{5,7},{6,2},{7,5},{8,12},{9,11},{10,... | collective-permute-start | bytes 2261000 | tf_op jit(solution)/shard_map/ppermute | solution.py:210
  109.4 16.9 %collective-permute-start.30 = (bf16[64,2944]{1,0:T(8,128)(2,1)S(1)}, bf16[64,2944]{1,0:T(8,128)(2,1)S(1)}, u32[]{:S(2)}, u32[]{:S(2)}) collective-permute-start(bf16[64,2944]{1,0:T(8,128)(2,1)S(1)} %add_convert_fusion.10), channel_id=1, source_target_pairs={{0,16},{1,17},{2,18},{3,19},{4,20},{5,21},{6,22},{7,23},{8,24},{9,... | collective-permute-start | bytes 1130504 | tf_op jit(solution)/shard_map/ppermute | solution.py:210
  114.1 12.1 %collective-permute-start.36 = (bf16[64,2944]{1,0:T(8,128)(2,1)S(1)}, bf16[64,2944]{1,0:T(8,128)(2,1)S(1)}, u32[]{:S(2)}, u32[]{:S(2)}) collective-permute-start(bf16[64,2944]{1,0:T(8,128)(2,1)S(1)} %add_convert_fusion.9), channel_id=1, source_target_pairs={{0,2},{1,5},{2,0},{3,7},{4,6},{5,1},{6,4},{7,3},{8,10},{9,13},{10,... | collective-permute-start | bytes 1130504 | tf_op jit(solution)/shard_map/ppermute | solution.py:210
  115.7 10.8 %collective-permute-start.34 = (bf16[128,2944]{1,0:T(8,128)(2,1)S(1)}, bf16[128,2944]{1,0:T(8,128)(2,1)S(1)}, u32[]{:S(2)}, u32[]{:S(2)}) collective-permute-start(bf16[128,2944]{1,0:T(8,128)(2,1)S(1)} %get-tuple-element.91), channel_id=1, source_target_pairs={{0,1},{1,0},{2,3},{3,2},{4,5},{5,4},{6,7},{7,6},{8,9},{9,8},{10,11... | collective-permute-start | bytes 2261000 | tf_op jit(solution)/shard_map/ppermute | solution.py:210
  126.6 7.7 %collective-permute-start.37 = (bf16[64,2944]{1,0:T(8,128)(2,1)S(1)}, bf16[64,2944]{1,0:T(8,128)(2,1)S(1)}, u32[]{:S(2)}, u32[]{:S(2)}) collective-permute-start(bf16[64,2944]{1,0:T(8,128)(2,1)S(1)} %add_convert_fusion.8), channel_id=1, source_target_pairs={{0,2},{1,5},{2,0},{3,7},{4,6},{5,1},{6,4},{7,3},{8,10},{9,13},{10,... | collective-permute-start | bytes 1130504 | tf_op jit(solution)/shard_map/ppermute | solution.py:210
  128.0 13.5 %collective-permute-start.38 = (bf16[64,2944]{1,0:T(8,128)(2,1)S(1)}, bf16[64,2944]{1,0:T(8,128)(2,1)S(1)}, u32[]{:S(2)}, u32[]{:S(2)}) collective-permute-start(bf16[64,2944]{1,0:T(8,128)(2,1)S(1)} %add_convert_fusion.7), channel_id=1, source_target_pairs={{0,24},{1,25},{2,26},{3,27},{4,28},{5,29},{6,30},{7,31},{8,16},{9,... | collective-permute-start | bytes 1130504 | tf_op jit(solution)/shard_map/ppermute | solution.py:210
  130.2 17.4 %collective-permute-start.39 = (bf16[64,2944]{1,0:T(8,128)(2,1)S(1)}, bf16[64,2944]{1,0:T(8,128)(2,1)S(1)}, u32[]{:S(2)}, u32[]{:S(2)}) collective-permute-start(bf16[64,2944]{1,0:T(8,128)(2,1)S(1)} %add_convert_fusion.6), channel_id=1, source_target_pairs={{0,8},{1,9},{2,10},{3,11},{4,12},{5,13},{6,14},{7,15},{8,0},{9,1},... | collective-permute-start | bytes 1130504 | tf_op jit(solution)/shard_map/ppermute | solution.py:210

commit v5 on v4

--- a/solution.py
+++ b/solution.py
@@ -10,7 +10,7 @@
 SLICES = 4
 LANES = 128
 UNITS = 2 * LANES
-COLUMNS = 6 * LANES
+COLUMNS = 12 * LANES
 BF16 = jnp.bfloat16
 F32 = jnp.float32
 
@@ -303,12 +303,12 @@
     p1[2] = swap(z[2], first)
     outward = inner(crossed, True)
     run_late(0)
+    gather_full(1)
+    z[3] = z[3] + order(outward)
+    p1[3] = swap(z[3], first)
     gather_half(2, z[2])
-    gather_full(1)
     run_other(0)
     run_own(1)
-    z[3] = z[3] + order(outward)
-    p1[3] = swap(z[3], first)
     run_other(1)
     gather_half(3, z[3])
     gather_full(2)

time: 149 us -> 147 us (0.987)
  waiting for transfers between devices: 74.7 us -> 68.3 us
  starting transfers between devices: 32.4 us -> 37.2 us
    ppermute x4, waiting for transfers between devices: 8.39 us -> 1.1 us  [inner(): return lax.ppermute(array, 'ex', low + high)]
    ppermute x36, starting transfers between devices: 28.3 us -> 33.1 us  [swap(): return lax.ppermute(array, 'ex', [(i, partner(i)) for i in range(devices)])]
  transfers between devices with their start and end apart: 40 -> 40, of which waited for: 18 -> 16; matrix products, arithmetic and copies ran while one was open for 2% -> 2% of each run, Pallas kernels for 25% -> 25%
where the time goes in v5:
time: 147 us
  waiting for transfers between devices  68.3 us (46%)
  Pallas kernels  37.6 us (26%)
  starting transfers between devices  37.2 us (25%)
  other arithmetic  3.31 us (2%)
    ppermute x36, waiting for transfers between devices, swap(): return lax.ppermute(array, 'ex', [(i, partner(i)) for i in range(devices)])  67.2 us
    pallas_call x9, Pallas kernels, expert_call(): pl.pallas_call(functools.partial(first_kernel if first else expert_kernel...  36.3 us
    ppermute x36, starting transfers between devices, swap(): return lax.ppermute(array, 'ex', [(i, partner(i)) for i in range(devices)])  33.1 us
    ppermute x4, starting transfers between devices, inner(): return lax.ppermute(array, 'ex', low + high)  4.1 us
  transfers between devices with their start and end apart: 40, of which 16 were waited for; matrix products, arithmetic and copies ran while one was open for 2% of the time, Pallas kernels for 25%

profile of v5, /device:TPU:0, one launch (start us, length us, event | category | flops | bytes accessed | tf_op | source)
XLA Modules:
  0.0 146.8 jit_solution(9839742948572078835)
XLA Ops:
  0.0 1.3 shard_map.73
  1.3 3.0 %collective-permute-start.1 = (bf16[64,2944]{1,0:T(8,128)(2,1)S(1)}, bf16[64,2944]{1,0:T(8,128)(2,1)S(1)}, u32[]{:S(2)}, u32[]{:S(2)}) collective-permute-start(bf16[64,2944]{1,0:T(8,128)(2,1)S(1)} %shard_map.73), channel_id=1, source_target_pairs={{0,2},{1,5},{2,0},{3,7},{4,6},{5,1},{6,4},{7,3},{8,10},{9,13},{10,... | collective-permute-start | bytes 1130504 | tf_op jit(solution)/shard_map/ppermute | solution.py:210
  4.3 1.6 %collective-permute-start = (bf16[64,2944]{1,0:T(8,128)(2,1)S(1)}, bf16[64,2944]{1,0:T(8,128)(2,1)S(1)}, u32[]{:S(2)}, u32[]{:S(2)}) collective-permute-start(bf16[64,2944]{1,0:T(8,128)(2,1)S(1)} %shard_map.73), channel_id=1, source_target_pairs={{0,8},{1,9},{2,10},{3,11},{4,12},{5,13},{6,14},{7,15},{8,0},{9,1},... | collective-permute-start | bytes 1130504 | tf_op jit(solution)/shard_map/ppermute | solution.py:210
  5.9 0.7 collective-permute-start.3
  6.6 3.3 %collective-permute-done.1 = bf16[64,2944]{1,0:T(8,128)(2,1)S(1)} collective-permute-done((bf16[64,2944]{1,0:T(8,128)(2,1)S(1)}, bf16[64,2944]{1,0:T(8,128)(2,1)S(1)}, u32[]{:S(2)}, u32[]{:S(2)}) %collective-permute-start.1) | collective-permute-done | bytes 376864 | tf_op jit(solution)/shard_map/ppermute | solution.py:210
  9.9 4.7 %collective-permute-done = bf16[64,2944]{1,0:T(8,128)(2,1)S(1)} collective-permute-done((bf16[64,2944]{1,0:T(8,128)(2,1)S(1)}, bf16[64,2944]{1,0:T(8,128)(2,1)S(1)}, u32[]{:S(2)}, u32[]{:S(2)}) %collective-permute-start) | collective-permute-done | bytes 376864 | tf_op jit(solution)/shard_map/ppermute | solution.py:210
  14.6 0.7 collective-permute-start.2
  15.2 1.3 collective-permute-start.4
  16.5 1.5 %collective-permute-start.6 = (bf16[64,2944]{1,0:T(8,128)(2,1)S(1)}, bf16[64,2944]{1,0:T(8,128)(2,1)S(1)}, u32[]{:S(2)}, u32[]{:S(2)}) collective-permute-start(bf16[64,2944]{1,0:T(8,128)(2,1)S(1)} %collective-permute-done), channel_id=1, source_target_pairs={{0,2},{1,5},{2,0},{3,7},{4,6},{5,1},{6,4},{7,3},{8,10},{9,13},{10,... | collective-permute-start | bytes 1130504 | tf_op jit(solution)/shard_map/ppermute | solution.py:210
  18.8 6.4 %shard_map.74 = (bf16[64,2944]{1,0:T(8,128)(2,1)S(1)}, bf16[64,2944]{1,0:T(8,128)(2,1)S(1)}, bf16[2880,1280]{1,0:T(8,128)(2,1)S(1)}, bf16[2880,640]{1,0:T(8,128)(2,1)S(1)}) custom-call(bf16[128,2944]{1,0:T(8,128)(2,1)S(1)} %pad_maximum_fusion.refs_0_, f32[1,128]{1,0:T(1,128)S(1)} %and_convert_fusion.refs_1_.refs_2_, bf16[1,2880,640]{2,1,0:T(8,128)(2,1)} %refs_2_.1, ...), custom_call_target="tpu_custom_call" | custom-call | tf_op jit(solution)/shard_map/pallas_call | solution.py:191
  25.1 3.1 %collective-permute-done.6 = bf16[64,2944]{1,0:T(8,128)(2,1)S(1)} collective-permute-done((bf16[64,2944]{1,0:T(8,128)(2,1)S(1)}, bf16[64,2944]{1,0:T(8,128)(2,1)S(1)}, u32[]{:S(2)}, u32[]{:S(2)}) %collective-permute-start.6) | collective-permute-done | bytes 376864 | tf_op jit(solution)/shard_map/ppermute | solution.py:210
  28.4 1.6 %collective-permute-done.5.refs_0_ = bf16[128,2944]{1,0:T(8,128)(2,1)S(1)} collective-permute-done((bf16[128,2944]{1,0:T(8,128)(2,1)S(1)}, bf16[128,2944]{1,0:T(8,128)(2,1)S(1)}, u32[]{:S(2)}, u32[]{:S(2)}) %collective-permute-start.5) | collective-permute-done | bytes 753696 | tf_op jit(solution)/shard_map/ppermute | solution.py:210
  30.0 1.5 collective-permute-start.8
  31.6 3.0 %collective-permute-start.7 = (bf16[64,2944]{1,0:T(8,128)(2,1)S(1)}, bf16[64,2944]{1,0:T(8,128)(2,1)S(1)}, u32[]{:S(2)}, u32[]{:S(2)}) collective-permute-start(bf16[64,2944]{1,0:T(8,128)(2,1)S(1)} %add.116), channel_id=1, source_target_pairs={{0,2},{1,5},{2,0},{3,7},{4,6},{5,1},{6,4},{7,3},{8,10},{9,13},{10,... | collective-permute-start | bytes 1130504 | tf_op jit(solution)/shard_map/ppermute | solution.py:210
  35.0 2.5 %shard_map.75 = bf16[128,2944]{1,0:T(8,128)(2,1)S(1)} custom-call(bf16[128,2944]{1,0:T(8,128)(2,1)S(1)} %collective-permute-done.5.refs_0_, f32[1,128]{1,0:T(1,128)S(1)} %and_convert_fusion.refs_1_.refs_2_, bf16[2880,1280]{1,0:T(8,128)(2,1)S(1)} %get-tuple-element.85.refs_2_.refs_3_, bf16[2880,640]{1,0:T(8,128)(2,1)S(1)} %get-tuple-element.86.refs_3_.refs_4_), custom_call_target="tpu_custom_call" | custom-call | tf_op jit(solution)/shard_map/pallas_call | solution.py:191
  37.6 6.4 %collective-permute-done.9.refs_1_ = bf16[128,2944]{1,0:T(8,128)(2,1)S(1)} collective-permute-done((bf16[128,2944]{1,0:T(8,128)(2,1)S(1)}, bf16[128,2944]{1,0:T(8,128)(2,1)S(1)}, u32[]{:S(2)}, u32[]{:S(2)}) %collective-permute-start.9) | collective-permute-done | bytes 753696 | tf_op jit(solution)/shard_map/ppermute | solution.py:210
  44.0 1.1 collective-permute-done.8
  45.8 2.2 %collective-permute-start.11 = (bf16[64,2944]{1,0:T(8,128)(2,1)S(1)}, bf16[64,2944]{1,0:T(8,128)(2,1)S(1)}, u32[]{:S(2)}, u32[]{:S(2)}) collective-permute-start(bf16[64,2944]{1,0:T(8,128)(2,1)S(1)} %add.117), channel_id=1, source_target_pairs={{0,2},{1,5},{2,0},{3,7},{4,6},{5,1},{6,4},{7,3},{8,10},{9,13},{10,... | collective-permute-start | bytes 1130504 | tf_op jit(solution)/shard_map/ppermute | solution.py:210
  48.0 3.8 %shard_map.76 = (bf16[128,2944]{1,0:T(8,128)(2,1)S(1)}, bf16[128,2944]{1,0:T(8,128)(2,1)S(1)}) custom-call(bf16[128,2944]{1,0:T(8,128)(2,1)S(1)} %collective-permute-done.13.refs_0_, bf16[128,2944]{1,0:T(8,128)(2,1)S(1)} %collective-permute-done.14.refs_1_, f32[1,128]{1,0:T(1,128)S(1)} %and_convert_fusion.refs_1_.refs_2_, ...), custom_call_target="tpu_custom_call" | custom-call | tf_op jit(solution)/shard_map/pallas_call | solution.py:191
  51.8 3.9 %shard_map.77 = (bf16[64,2944]{1,0:T(8,128)(2,1)S(1)}, bf16[64,2944]{1,0:T(8,128)(2,1)S(1)}, bf16[128,2944]{1,0:T(8,128)(2,1)S(1)}) custom-call(bf16[128,2944]{1,0:T(8,128)(2,1)S(1)} %constant_dynamic-update-slice_fusion.refs_0_, bf16[128,2944]{1,0:T(8,128)(2,1)S(1)} %collective-permute-done.9.refs_1_, f32[1,128]{1,0:T(1,128)S(1)} %and_convert_fusion.refs_1_.refs_2_, ...), custom_call_target="tpu_custom_call" | custom-call | tf_op jit(solution)/shard_map/pallas_call | solution.py:191
  55.7 4.1 %shard_map.78 = (bf16[128,2944]{1,0:T(8,128)(2,1)S(1)}, bf16[128,2944]{1,0:T(8,128)(2,1)S(1)}) custom-call(bf16[128,2944]{1,0:T(8,128)(2,1)S(1)} %collective-permute-done.12.refs_0_, bf16[128,2944]{1,0:T(8,128)(2,1)S(1)} %collective-permute-done.15.refs_1_, f32[1,128]{1,0:T(1,128)S(1)} %and_convert_fusion.refs_1_.refs_2_, ...), custom_call_target="tpu_custom_call" | custom-call | tf_op jit(solution)/shard_map/pallas_call | solution.py:191
  59.8 1.1 collective-permute-done.10.refs_1_
  61.0 0.8 collective-permute-start.21
  61.9 1.0 collective-permute-start.20
  62.9 3.8 %shard_map.79 = (bf16[64,2944]{1,0:T(8,128)(2,1)S(1)}, bf16[64,2944]{1,0:T(8,128)(2,1)S(1)}, bf16[128,2944]{1,0:T(8,128)(2,1)S(1)}) custom-call(bf16[128,2944]{1,0:T(8,128)(2,1)S(1)} %pad_maximum_fusion.1.refs_0_, bf16[128,2944]{1,0:T(8,128)(2,1)S(1)} %collective-permute-done.10.refs_1_, f32[1,128]{1,0:T(1,128)S(1)} %and_convert_fusion.refs_1_.refs_2_, ...), custom_call_target="tpu_custom_call" | custom-call | tf_op jit(solution)/shard_map/pallas_call | solution.py:191
  66.8 3.9 %shard_map.80 = (bf16[128,2944]{1,0:T(8,128)(2,1)S(1)}, bf16[128,2944]{1,0:T(8,128)(2,1)S(1)}) custom-call(bf16[128,2944]{1,0:T(8,128)(2,1)S(1)} %collective-permute-done.16.refs_0_, bf16[128,2944]{1,0:T(8,128)(2,1)S(1)} %collective-permute-done.17.refs_1_, f32[1,128]{1,0:T(1,128)S(1)} %and_convert_fusion.refs_1_.refs_2_, ...), custom_call_target="tpu_custom_call" | custom-call | tf_op jit(solution)/shard_map/pallas_call | solution.py:191
  71.3 1.5 %collective-permute-done.21.refs_1_ = bf16[128,2944]{1,0:T(8,128)(2,1)S(1)} collective-permute-done((bf16[128,2944]{1,0:T(8,128)(2,1)S(1)}, bf16[128,2944]{1,0:T(8,128)(2,1)S(1)}, u32[]{:S(2)}, u32[]{:S(2)}) %collective-permute-start.21) | collective-permute-done | bytes 753696 | tf_op jit(solution)/shard_map/ppermute | solution.py:210
  72.9 0.8 collective-permute-start.24
  74.0 1.3 collective-permute-start.22
  75.3 3.8 %shard_map.81 = (bf16[64,2944]{1,0:T(8,128)(2,1)S(1)}, bf16[64,2944]{1,0:T(8,128)(2,1)S(1)}, bf16[128,2944]{1,0:T(8,128)(2,1)S(1)}) custom-call(bf16[128,2944]{1,0:T(8,128)(2,1)S(1)} %pad_maximum_fusion.2.refs_0_, bf16[128,2944]{1,0:T(8,128)(2,1)S(1)} %collective-permute-done.21.refs_1_, f32[1,128]{1,0:T(1,128)S(1)} %and_convert_fusion.refs_1_.refs_2_, ...), custom_call_target="tpu_custom_call" | custom-call | tf_op jit(solution)/shard_map/pallas_call | solution.py:191
  79.7 4.1 %shard_map.82 = (bf16[128,2944]{1,0:T(8,128)(2,1)S(1)}, bf16[128,2944]{1,0:T(8,128)(2,1)S(1)}) custom-call(bf16[128,2944]{1,0:T(8,128)(2,1)S(1)} %collective-permute-done.25.refs_0_, bf16[128,2944]{1,0:T(8,128)(2,1)S(1)} %collective-permute-done.26.refs_1_, f32[1,128]{1,0:T(1,128)S(1)} %and_convert_fusion.refs_1_.refs_2_, ...), custom_call_target="tpu_custom_call" | custom-call | tf_op jit(solution)/shard_map/pallas_call | solution.py:191
  83.8 0.8 collective-permute-done.24
  85.3 7.4 %collective-permute-done.22 = bf16[128,2944]{1,0:T(8,128)(2,1)S(1)} collective-permute-done((bf16[128,2944]{1,0:T(8,128)(2,1)S(1)}, bf16[128,2944]{1,0:T(8,128)(2,1)S(1)}, u32[]{:S(2)}, u32[]{:S(2)}) %collective-permute-start.22) | collective-permute-done | bytes 753696 | tf_op jit(solution)/shard_map/ppermute | solution.py:210
  92.7 1.6 %collective-permute-start.28 = (bf16[64,2944]{1,0:T(8,128)(2,1)S(1)}, bf16[64,2944]{1,0:T(8,128)(2,1)S(1)}, u32[]{:S(2)}, u32[]{:S(2)}) collective-permute-start(bf16[64,2944]{1,0:T(8,128)(2,1)S(1)} %add_convert_fusion.11), channel_id=1, source_target_pairs={{0,2},{1,5},{2,0},{3,7},{4,6},{5,1},{6,4},{7,3},{8,10},{9,13},{10,... | collective-permute-start | bytes 1130504 | tf_op jit(solution)/shard_map/ppermute | solution.py:210
  95.0 5.4 %collective-permute-done.28 = bf16[64,2944]{1,0:T(8,128)(2,1)S(1)} collective-permute-done((bf16[64,2944]{1,0:T(8,128)(2,1)S(1)}, bf16[64,2944]{1,0:T(8,128)(2,1)S(1)}, u32[]{:S(2)}, u32[]{:S(2)}) %collective-permute-start.28) | collective-permute-done | bytes 376864 | tf_op jit(solution)/shard_map/ppermute | solution.py:210
  100.5 0.8 collective-permute-start.32
  101.3 5.4 %collective-permute-done.27 = bf16[64,2944]{1,0:T(8,128)(2,1)S(1)} collective-permute-done((bf16[64,2944]{1,0:T(8,128)(2,1)S(1)}, bf16[64,2944]{1,0:T(8,128)(2,1)S(1)}, u32[]{:S(2)}, u32[]{:S(2)}) %collective-permute-start.27) | collective-permute-done | bytes 376864 | tf_op jit(solution)/shard_map/ppermute | solution.py:210
  106.9 0.8 collective-permute-start.35
  107.9 4.7 %collective-permute-start.30 = (bf16[64,2944]{1,0:T(8,128)(2,1)S(1)}, bf16[64,2944]{1,0:T(8,128)(2,1)S(1)}, u32[]{:S(2)}, u32[]{:S(2)}) collective-permute-start(bf16[64,2944]{1,0:T(8,128)(2,1)S(1)} %add_convert_fusion.10), channel_id=1, source_target_pairs={{0,16},{1,17},{2,18},{3,19},{4,20},{5,21},{6,22},{7,23},{8,24},{9,... | collective-permute-start | bytes 1130504 | tf_op jit(solution)/shard_map/ppermute | solution.py:210
  112.7 1.2 collective-permute-start.36
  114.0 11.9 %collective-permute-done.30 = bf16[64,2944]{1,0:T(8,128)(2,1)S(1)} collective-permute-done((bf16[64,2944]{1,0:T(8,128)(2,1)S(1)}, bf16[64,2944]{1,0:T(8,128)(2,1)S(1)}, u32[]{:S(2)}, u32[]{:S(2)}) %collective-permute-start.30) | collective-permute-done | bytes 376864 | tf_op jit(solution)/shard_map/ppermute | solution.py:210
  126.2 1.1 collective-permute-start.37
  127.3 1.7 %collective-permute-start.38 = (bf16[64,2944]{1,0:T(8,128)(2,1)S(1)}, bf16[64,2944]{1,0:T(8,128)(2,1)S(1)}, u32[]{:S(2)}, u32[]{:S(2)}) collective-permute-start(bf16[64,2944]{1,0:T(8,128)(2,1)S(1)} %add_convert_fusion.7), channel_id=1, source_target_pairs={{0,24},{1,25},{2,26},{3,27},{4,28},{5,29},{6,30},{7,31},{8,16},{9,... | collective-permute-start | bytes 1130504 | tf_op jit(solution)/shard_map/ppermute | solution.py:210
  129.2 1.8 %collective-permute-start.39 = (bf16[64,2944]{1,0:T(8,128)(2,1)S(1)}, bf16[64,2944]{1,0:T(8,128)(2,1)S(1)}, u32[]{:S(2)}, u32[]{:S(2)}) collective-permute-start(bf16[64,2944]{1,0:T(8,128)(2,1)S(1)} %add_convert_fusion.6), channel_id=1, source_target_pairs={{0,8},{1,9},{2,10},{3,11},{4,12},{5,13},{6,14},{7,15},{8,0},{9,1},... | collective-permute-start | bytes 1130504 | tf_op jit(solution)/shard_map/ppermute | solution.py:210
  131.0 2.9 %collective-permute-done.37 = bf16[64,2944]{1,0:T(8,128)(2,1)S(1)} collective-permute-done((bf16[64,2944]{1,0:T(8,128)(2,1)S(1)}, bf16[64,2944]{1,0:T(8,128)(2,1)S(1)}, u32[]{:S(2)}, u32[]{:S(2)}) %collective-permute-start.37) | collective-permute-done | bytes 376864 | tf_op jit(solution)/shard_map/ppermute | solution.py:210
  133.9 7.0 %collective-permute-done.38 = bf16[64,2944]{1,0:T(8,128)(2,1)S(1)} collective-permute-done((bf16[64,2944]{1,0:T(8,128)(2,1)S(1)}, bf16[64,2944]{1,0:T(8,128)(2,1)S(1)}, u32[]{:S(2)}, u32[]{:S(2)}) %collective-permute-start.38) | collective-permute-done | bytes 376864 | tf_op jit(solution)/shard_map/ppermute | solution.py:210
  141.1 4.7 %collective-permute-done.39 = bf16[64,2944]{1,0:T(8,128)(2,1)S(1)} collective-permute-done((bf16[64,2944]{1,0:T(8,128)(2,1)S(1)}, bf16[64,2944]{1,0:T(8,128)(2,1)S(1)}, u32[]{:S(2)}, u32[]{:S(2)}) %collective-permute-start.39) | collective-permute-done | bytes 376864 | tf_op jit(solution)/shard_map/ppermute | solution.py:210
  145.8 1.0 add_convert_fusion.4
  (63 shorter events, 6.5 us)
Async XLA Ops:
  1.3 8.6 %collective-permute-start.1 = (bf16[64,2944]{1,0:T(8,128)(2,1)S(1)}, bf16[64,2944]{1,0:T(8,128)(2,1)S(1)}, u32[]{:S(2)}, u32[]{:S(2)}) collective-permute-start(bf16[64,2944]{1,0:T(8,128)(2,1)S(1)} %shard_map.73), channel_id=1, source_target_pairs={{0,2},{1,5},{2,0},{3,7},{4,6},{5,1},{6,4},{7,3},{8,10},{9,13},{10,... | collective-permute-start | bytes 1130504 | tf_op jit(solution)/shard_map/ppermute | solution.py:210
  4.3 10.3 %collective-permute-start = (bf16[64,2944]{1,0:T(8,128)(2,1)S(1)}, bf16[64,2944]{1,0:T(8,128)(2,1)S(1)}, u32[]{:S(2)}, u32[]{:S(2)}) collective-permute-start(bf16[64,2944]{1,0:T(8,128)(2,1)S(1)} %shard_map.73), channel_id=1, source_target_pairs={{0,8},{1,9},{2,10},{3,11},{4,12},{5,13},{6,14},{7,15},{8,0},{9,1},... | collective-permute-start | bytes 1130504 | tf_op jit(solution)/shard_map/ppermute | solution.py:210
  5.9 9.4 %collective-permute-start.3 = (bf16[64,2944]{1,0:T(8,128)(2,1)S(1)}, bf16[64,2944]{1,0:T(8,128)(2,1)S(1)}, u32[]{:S(2)}, u32[]{:S(2)}) collective-permute-start(bf16[64,2944]{1,0:T(8,128)(2,1)S(1)} %shard_map.73), channel_id=1, source_target_pairs={{8,16},{9,17},{10,18},{11,19},{12,20},{13,21},{14,22},{15,23},{16,... | collective-permute-start | bytes 1130504 | tf_op jit(solution)/shard_map/ppermute | solution.py:227
  14.6 15.4 %collective-permute-start.2 = (bf16[64,2944]{1,0:T(8,128)(2,1)S(1)}, bf16[64,2944]{1,0:T(8,128)(2,1)S(1)}, u32[]{:S(2)}, u32[]{:S(2)}) collective-permute-start(bf16[64,2944]{1,0:T(8,128)(2,1)S(1)} %collective-permute-done), channel_id=1, source_target_pairs={{8,16},{9,17},{10,18},{11,19},{12,20},{13,21},{14,22},{15,23},{16,... | collective-permute-start | bytes 1130504 | tf_op jit(solution)/shard_map/ppermute | solution.py:227
  15.2 14.8 %collective-permute-start.4 = (bf16[64,2944]{1,0:T(8,128)(2,1)S(1)}, bf16[64,2944]{1,0:T(8,128)(2,1)S(1)}, u32[]{:S(2)}, u32[]{:S(2)}) collective-permute-start(bf16[64,2944]{1,0:T(8,128)(2,1)S(1)} %collective-permute-done.3), channel_id=1, source_target_pairs={{8,0},{9,1},{10,2},{11,3},{12,4},{13,5},{14,6},{15,7},{16,24},{17,... | collective-permute-start | bytes 1130504 | tf_op jit(solution)/shard_map/ppermute | solution.py:227
  16.5 11.7 %collective-permute-start.6 = (bf16[64,2944]{1,0:T(8,128)(2,1)S(1)}, bf16[64,2944]{1,0:T(8,128)(2,1)S(1)}, u32[]{:S(2)}, u32[]{:S(2)}) collective-permute-start(bf16[64,2944]{1,0:T(8,128)(2,1)S(1)} %collective-permute-done), channel_id=1, source_target_pairs={{0,2},{1,5},{2,0},{3,7},{4,6},{5,1},{6,4},{7,3},{8,10},{9,13},{10,... | collective-permute-start | bytes 1130504 | tf_op jit(solution)/shard_map/ppermute | solution.py:210
  18.1 11.9 %collective-permute-start.5 = (bf16[128,2944]{1,0:T(8,128)(2,1)S(1)}, bf16[128,2944]{1,0:T(8,128)(2,1)S(1)}, u32[]{:S(2)}, u32[]{:S(2)}) collective-permute-start(bf16[128,2944]{1,0:T(8,128)(2,1)S(1)} %pad_maximum_fusion.refs_0_), channel_id=1, source_target_pairs={{0,4},{1,3},{2,6},{3,1},{4,0},{5,7},{6,2},{7,5},{8,12},{9,11},{10,... | collective-permute-start | bytes 2261000 | tf_op jit(solution)/shard_map/ppermute | solution.py:210
  28.3 15.7 %collective-permute-start.9 = (bf16[128,2944]{1,0:T(8,128)(2,1)S(1)}, bf16[128,2944]{1,0:T(8,128)(2,1)S(1)}, u32[]{:S(2)}, u32[]{:S(2)}) collective-permute-start(bf16[128,2944]{1,0:T(8,128)(2,1)S(1)} %constant_dynamic-update-slice_fusion.refs_0_), channel_id=1, source_target_pairs={{0,4},{1,3},{2,6},{3,1},{4,0},{5,7},{6,2},{7,5},{8,12},{9,11},{10,... | collective-permute-start | bytes 2261000 | tf_op jit(solution)/shard_map/ppermute | solution.py:210
  30.0 15.1 %collective-permute-start.8 = (bf16[64,2944]{1,0:T(8,128)(2,1)S(1)}, bf16[64,2944]{1,0:T(8,128)(2,1)S(1)}, u32[]{:S(2)}, u32[]{:S(2)}) collective-permute-start(bf16[64,2944]{1,0:T(8,128)(2,1)S(1)} %collective-permute-done.2), channel_id=1, source_target_pairs={{8,0},{9,1},{10,2},{11,3},{12,4},{13,5},{14,6},{15,7},{16,24},{17,... | collective-permute-start | bytes 1130504 | tf_op jit(solution)/shard_map/ppermute | solution.py:227
  31.6 13.6 %collective-permute-start.7 = (bf16[64,2944]{1,0:T(8,128)(2,1)S(1)}, bf16[64,2944]{1,0:T(8,128)(2,1)S(1)}, u32[]{:S(2)}, u32[]{:S(2)}) collective-permute-start(bf16[64,2944]{1,0:T(8,128)(2,1)S(1)} %add.116), channel_id=1, source_target_pairs={{0,2},{1,5},{2,0},{3,7},{4,6},{5,1},{6,4},{7,3},{8,10},{9,13},{10,... | collective-permute-start | bytes 1130504 | tf_op jit(solution)/shard_map/ppermute | solution.py:210
  34.5 11.2 %collective-permute-start.13 = (bf16[128,2944]{1,0:T(8,128)(2,1)S(1)}, bf16[128,2944]{1,0:T(8,128)(2,1)S(1)}, u32[]{:S(2)}, u32[]{:S(2)}) collective-permute-start(bf16[128,2944]{1,0:T(8,128)(2,1)S(1)} %pad_maximum_fusion.refs_0_), channel_id=1, source_target_pairs={{0,1},{1,0},{2,3},{3,2},{4,5},{5,4},{6,7},{7,6},{8,9},{9,8},{10,11... | collective-permute-start | bytes 2261000 | tf_op jit(solution)/shard_map/ppermute | solution.py:210
  34.5 21.2 %collective-permute-start.12 = (bf16[128,2944]{1,0:T(8,128)(2,1)S(1)}, bf16[128,2944]{1,0:T(8,128)(2,1)S(1)}, u32[]{:S(2)}, u32[]{:S(2)}) collective-permute-start(bf16[128,2944]{1,0:T(8,128)(2,1)S(1)} %constant_dynamic-update-slice_fusion.refs_0_), channel_id=1, source_target_pairs={{0,1},{1,0},{2,3},{3,2},{4,5},{5,4},{6,7},{7,6},{8,9},{9,8},{10,11... | collective-permute-start | bytes 2261000 | tf_op jit(solution)/shard_map/ppermute | solution.py:210
  44.0 4.0 %collective-permute-start.14 = (bf16[128,2944]{1,0:T(8,128)(2,1)S(1)}, bf16[128,2944]{1,0:T(8,128)(2,1)S(1)}, u32[]{:S(2)}, u32[]{:S(2)}) collective-permute-start(bf16[128,2944]{1,0:T(8,128)(2,1)S(1)} %collective-permute-done.5.refs_0_), channel_id=1, source_target_pairs={{0,1},{1,0},{2,3},{3,2},{4,5},{5,4},{6,7},{7,6},{8,9},{9,8},{10,11... | collective-permute-start | bytes 2261000 | tf_op jit(solution)/shard_map/ppermute | solution.py:210
  45.1 10.6 %collective-permute-start.15 = (bf16[128,2944]{1,0:T(8,128)(2,1)S(1)}, bf16[128,2944]{1,0:T(8,128)(2,1)S(1)}, u32[]{:S(2)}, u32[]{:S(2)}) collective-permute-start(bf16[128,2944]{1,0:T(8,128)(2,1)S(1)} %collective-permute-done.9.refs_1_), channel_id=1, source_target_pairs={{0,1},{1,0},{2,3},{3,2},{4,5},{5,4},{6,7},{7,6},{8,9},{9,8},{10,11... | collective-permute-start | bytes 2261000 | tf_op jit(solution)/shard_map/ppermute | solution.py:210
  45.2 15.7 %collective-permute-start.10 = (bf16[128,2944]{1,0:T(8,128)(2,1)S(1)}, bf16[128,2944]{1,0:T(8,128)(2,1)S(1)}, u32[]{:S(2)}, u32[]{:S(2)}) collective-permute-start(bf16[128,2944]{1,0:T(8,128)(2,1)S(1)} %pad_maximum_fusion.1.refs_0_), channel_id=1, source_target_pairs={{0,4},{1,3},{2,6},{3,1},{4,0},{5,7},{6,2},{7,5},{8,12},{9,11},{10,... | collective-permute-start | bytes 2261000 | tf_op jit(solution)/shard_map/ppermute | solution.py:210
  45.8 14.0 %collective-permute-start.11 = (bf16[64,2944]{1,0:T(8,128)(2,1)S(1)}, bf16[64,2944]{1,0:T(8,128)(2,1)S(1)}, u32[]{:S(2)}, u32[]{:S(2)}) collective-permute-start(bf16[64,2944]{1,0:T(8,128)(2,1)S(1)} %add.117), channel_id=1, source_target_pairs={{0,2},{1,5},{2,0},{3,7},{4,6},{5,1},{6,4},{7,3},{8,10},{9,13},{10,... | collective-permute-start | bytes 1130504 | tf_op jit(solution)/shard_map/ppermute | solution.py:210
  48.0 18.8 %collective-permute-start.16 = (bf16[128,2944]{1,0:T(8,128)(2,1)S(1)}, bf16[128,2944]{1,0:T(8,128)(2,1)S(1)}, u32[]{:S(2)}, u32[]{:S(2)}) collective-permute-start(bf16[128,2944]{1,0:T(8,128)(2,1)S(1)} %pad_maximum_fusion.1.refs_0_), channel_id=1, source_target_pairs={{0,1},{1,0},{2,3},{3,2},{4,5},{5,4},{6,7},{7,6},{8,9},{9,8},{10,11... | collective-permute-start | bytes 2261000 | tf_op jit(solution)/shard_map/ppermute | solution.py:210
  61.0 5.8 %collective-permute-start.17 = (bf16[128,2944]{1,0:T(8,128)(2,1)S(1)}, bf16[128,2944]{1,0:T(8,128)(2,1)S(1)}, u32[]{:S(2)}, u32[]{:S(2)}) collective-permute-start(bf16[128,2944]{1,0:T(8,128)(2,1)S(1)} %collective-permute-done.10.refs_1_), channel_id=1, source_target_pairs={{0,1},{1,0},{2,3},{3,2},{4,5},{5,4},{6,7},{7,6},{8,9},{9,8},{10,11... | collective-permute-start | bytes 2261000 | tf_op jit(solution)/shard_map/ppermute | solution.py:210
  61.0 11.7 %collective-permute-start.21 = (bf16[128,2944]{1,0:T(8,128)(2,1)S(1)}, bf16[128,2944]{1,0:T(8,128)(2,1)S(1)}, u32[]{:S(2)}, u32[]{:S(2)}) collective-permute-start(bf16[128,2944]{1,0:T(8,128)(2,1)S(1)} %pad_maximum_fusion.2.refs_0_), channel_id=1, source_target_pairs={{0,4},{1,3},{2,6},{3,1},{4,0},{5,7},{6,2},{7,5},{8,12},{9,11},{10,... | collective-permute-start | bytes 2261000 | tf_op jit(solution)/shard_map/ppermute | solution.py:210
  61.9 10.9 %collective-permute-start.20 = (bf16[128,2944]{1,0:T(8,128)(2,1)S(1)}, bf16[128,2944]{1,0:T(8,128)(2,1)S(1)}, u32[]{:S(2)}, u32[]{:S(2)}) collective-permute-start(bf16[128,2944]{1,0:T(8,128)(2,1)S(1)} %get-tuple-element.107), channel_id=1, source_target_pairs={{0,1},{1,0},{2,3},{3,2},{4,5},{5,4},{6,7},{7,6},{8,9},{9,8},{10,11... | collective-permute-start | bytes 2261000 | tf_op jit(solution)/shard_map/ppermute | solution.py:210
  70.6 3.2 %collective-permute-start.19 = (bf16[128,2944]{1,0:T(8,128)(2,1)S(1)}, bf16[128,2944]{1,0:T(8,128)(2,1)S(1)}, u32[]{:S(2)}, u32[]{:S(2)}) collective-permute-start(bf16[128,2944]{1,0:T(8,128)(2,1)S(1)} %get-tuple-element.106), channel_id=1, source_target_pairs={{0,1},{1,0},{2,3},{3,2},{4,5},{5,4},{6,7},{7,6},{8,9},{9,8},{10,11... | collective-permute-start | bytes 2261000 | tf_op jit(solution)/shard_map/ppermute | solution.py:210
  70.7 13.9 %collective-permute-start.23 = (bf16[128,2944]{1,0:T(8,128)(2,1)S(1)}, bf16[128,2944]{1,0:T(8,128)(2,1)S(1)}, u32[]{:S(2)}, u32[]{:S(2)}) collective-permute-start(bf16[128,2944]{1,0:T(8,128)(2,1)S(1)} %get-tuple-element.97), channel_id=1, source_target_pairs={{0,1},{1,0},{2,3},{3,2},{4,5},{5,4},{6,7},{7,6},{8,9},{9,8},{10,11... | collective-permute-start | bytes 2261000 | tf_op jit(solution)/shard_map/ppermute | solution.py:210
  71.2 4.1 %collective-permute-start.25 = (bf16[128,2944]{1,0:T(8,128)(2,1)S(1)}, bf16[128,2944]{1,0:T(8,128)(2,1)S(1)}, u32[]{:S(2)}, u32[]{:S(2)}) collective-permute-start(bf16[128,2944]{1,0:T(8,128)(2,1)S(1)} %pad_maximum_fusion.2.refs_0_), channel_id=1, source_target_pairs={{0,1},{1,0},{2,3},{3,2},{4,5},{5,4},{6,7},{7,6},{8,9},{9,8},{10,11... | collective-permute-start | bytes 2261000 | tf_op jit(solution)/shard_map/ppermute | solution.py:210
  72.8 6.4 %collective-permute-start.26 = (bf16[128,2944]{1,0:T(8,128)(2,1)S(1)}, bf16[128,2944]{1,0:T(8,128)(2,1)S(1)}, u32[]{:S(2)}, u32[]{:S(2)}) collective-permute-start(bf16[128,2944]{1,0:T(8,128)(2,1)S(1)} %collective-permute-done.21.refs_1_), channel_id=1, source_target_pairs={{0,1},{1,0},{2,3},{3,2},{4,5},{5,4},{6,7},{7,6},{8,9},{9,8},{10,11... | collective-permute-start | bytes 2261000 | tf_op jit(solution)/shard_map/ppermute | solution.py:210
  72.9 11.7 %collective-permute-start.24 = (bf16[128,2944]{1,0:T(8,128)(2,1)S(1)}, bf16[128,2944]{1,0:T(8,128)(2,1)S(1)}, u32[]{:S(2)}, u32[]{:S(2)}) collective-permute-start(bf16[128,2944]{1,0:T(8,128)(2,1)S(1)} %add_convert_fusion.2), channel_id=1, source_target_pairs={{0,4},{1,3},{2,6},{3,1},{4,0},{5,7},{6,2},{7,5},{8,12},{9,11},{10,... | collective-permute-start | bytes 2261000 | tf_op jit(solution)/shard_map/ppermute | solution.py:210
  74.0 18.8 %collective-permute-start.22 = (bf16[128,2944]{1,0:T(8,128)(2,1)S(1)}, bf16[128,2944]{1,0:T(8,128)(2,1)S(1)}, u32[]{:S(2)}, u32[]{:S(2)}) collective-permute-start(bf16[128,2944]{1,0:T(8,128)(2,1)S(1)} %add_convert_fusion.3), channel_id=1, source_target_pairs={{0,4},{1,3},{2,6},{3,1},{4,0},{5,7},{6,2},{7,5},{8,12},{9,11},{10,... | collective-permute-start | bytes 2261000 | tf_op jit(solution)/shard_map/ppermute | solution.py:210
  75.3 19.0 %collective-permute-start.18 = (bf16[128,2944]{1,0:T(8,128)(2,1)S(1)}, bf16[128,2944]{1,0:T(8,128)(2,1)S(1)}, u32[]{:S(2)}, u32[]{:S(2)}) collective-permute-start(bf16[128,2944]{1,0:T(8,128)(2,1)S(1)} %get-tuple-element.104), channel_id=1, source_target_pairs={{0,1},{1,0},{2,3},{3,2},{4,5},{5,4},{6,7},{7,6},{8,9},{9,8},{10,11... | collective-permute-start | bytes 2261000 | tf_op jit(solution)/shard_map/ppermute | solution.py:210
  79.2 27.5 %collective-permute-start.33 = (bf16[128,2944]{1,0:T(8,128)(2,1)S(1)}, bf16[128,2944]{1,0:T(8,128)(2,1)S(1)}, u32[]{:S(2)}, u32[]{:S(2)}) collective-permute-start(bf16[128,2944]{1,0:T(8,128)(2,1)S(1)} %get-tuple-element.128), channel_id=1, source_target_pairs={{0,1},{1,0},{2,3},{3,2},{4,5},{5,4},{6,7},{7,6},{8,9},{9,8},{10,11... | collective-permute-start | bytes 2261000 | tf_op jit(solution)/shard_map/ppermute | solution.py:210
  84.6 28.0 %collective-permute-start.31 = (bf16[128,2944]{1,0:T(8,128)(2,1)S(1)}, bf16[128,2944]{1,0:T(8,128)(2,1)S(1)}, u32[]{:S(2)}, u32[]{:S(2)}) collective-permute-start(bf16[128,2944]{1,0:T(8,128)(2,1)S(1)} %get-tuple-element.116), channel_id=1, source_target_pairs={{0,1},{1,0},{2,3},{3,2},{4,5},{5,4},{6,7},{7,6},{8,9},{9,8},{10,11... | collective-permute-start | bytes 2261000 | tf_op jit(solution)/shard_map/ppermute | solution.py:210
  84.7 10.3 %collective-permute-start.29 = (bf16[128,2944]{1,0:T(8,128)(2,1)S(1)}, bf16[128,2944]{1,0:T(8,128)(2,1)S(1)}, u32[]{:S(2)}, u32[]{:S(2)}) collective-permute-start(bf16[128,2944]{1,0:T(8,128)(2,1)S(1)} %get-tuple-element.123), channel_id=1, source_target_pairs={{0,1},{1,0},{2,3},{3,2},{4,5},{5,4},{6,7},{7,6},{8,9},{9,8},{10,11... | collective-permute-start | bytes 2261000 | tf_op jit(solution)/shard_map/ppermute | solution.py:210
  92.7 7.6 %collective-permute-start.28 = (bf16[64,2944]{1,0:T(8,128)(2,1)S(1)}, bf16[64,2944]{1,0:T(8,128)(2,1)S(1)}, u32[]{:S(2)}, u32[]{:S(2)}) collective-permute-start(bf16[64,2944]{1,0:T(8,128)(2,1)S(1)} %add_convert_fusion.11), channel_id=1, source_target_pairs={{0,2},{1,5},{2,0},{3,7},{4,6},{5,1},{6,4},{7,3},{8,10},{9,13},{10,... | collective-permute-start | bytes 1130504 | tf_op jit(solution)/shard_map/ppermute | solution.py:210
  94.4 12.3 %collective-permute-start.27 = (bf16[64,2944]{1,0:T(8,128)(2,1)S(1)}, bf16[64,2944]{1,0:T(8,128)(2,1)S(1)}, u32[]{:S(2)}, u32[]{:S(2)}) collective-permute-start(bf16[64,2944]{1,0:T(8,128)(2,1)S(1)} %add_convert_fusion.12), channel_id=1, source_target_pairs={{0,2},{1,5},{2,0},{3,7},{4,6},{5,1},{6,4},{7,3},{8,10},{9,13},{10,... | collective-permute-start | bytes 1130504 | tf_op jit(solution)/shard_map/ppermute | solution.py:210
  100.5 12.1 %collective-permute-start.32 = (bf16[128,2944]{1,0:T(8,128)(2,1)S(1)}, bf16[128,2944]{1,0:T(8,128)(2,1)S(1)}, u32[]{:S(2)}, u32[]{:S(2)}) collective-permute-start(bf16[128,2944]{1,0:T(8,128)(2,1)S(1)} %add_convert_fusion.1), channel_id=1, source_target_pairs={{0,4},{1,3},{2,6},{3,1},{4,0},{5,7},{6,2},{7,5},{8,12},{9,11},{10,... | collective-permute-start | bytes 2261000 | tf_op jit(solution)/shard_map/ppermute | solution.py:210
  106.9 19.0 %collective-permute-start.35 = (bf16[128,2944]{1,0:T(8,128)(2,1)S(1)}, bf16[128,2944]{1,0:T(8,128)(2,1)S(1)}, u32[]{:S(2)}, u32[]{:S(2)}) collective-permute-start(bf16[128,2944]{1,0:T(8,128)(2,1)S(1)} %add_convert_fusion), channel_id=1, source_target_pairs={{0,4},{1,3},{2,6},{3,1},{4,0},{5,7},{6,2},{7,5},{8,12},{9,11},{10,... | collective-permute-start | bytes 2261000 | tf_op jit(solution)/shard_map/ppermute | solution.py:210
  107.9 17.9 %collective-permute-start.30 = (bf16[64,2944]{1,0:T(8,128)(2,1)S(1)}, bf16[64,2944]{1,0:T(8,128)(2,1)S(1)}, u32[]{:S(2)}, u32[]{:S(2)}) collective-permute-start(bf16[64,2944]{1,0:T(8,128)(2,1)S(1)} %add_convert_fusion.10), channel_id=1, source_target_pairs={{0,16},{1,17},{2,18},{3,19},{4,20},{5,21},{6,22},{7,23},{8,24},{9,... | collective-permute-start | bytes 1130504 | tf_op jit(solution)/shard_map/ppermute | solution.py:210
  112.7 13.1 %collective-permute-start.36 = (bf16[64,2944]{1,0:T(8,128)(2,1)S(1)}, bf16[64,2944]{1,0:T(8,128)(2,1)S(1)}, u32[]{:S(2)}, u32[]{:S(2)}) collective-permute-start(bf16[64,2944]{1,0:T(8,128)(2,1)S(1)} %add_convert_fusion.9), channel_id=1, source_target_pairs={{0,2},{1,5},{2,0},{3,7},{4,6},{5,1},{6,4},{7,3},{8,10},{9,13},{10,... | collective-permute-start | bytes 1130504 | tf_op jit(solution)/shard_map/ppermute | solution.py:210
  114.0 12.1 %collective-permute-start.34 = (bf16[128,2944]{1,0:T(8,128)(2,1)S(1)}, bf16[128,2944]{1,0:T(8,128)(2,1)S(1)}, u32[]{:S(2)}, u32[]{:S(2)}) collective-permute-start(bf16[128,2944]{1,0:T(8,128)(2,1)S(1)} %get-tuple-element.92), channel_id=1, source_target_pairs={{0,1},{1,0},{2,3},{3,2},{4,5},{5,4},{6,7},{7,6},{8,9},{9,8},{10,11... | collective-permute-start | bytes 2261000 | tf_op jit(solution)/shard_map/ppermute | solution.py:210
  126.2 7.7 %collective-permute-start.37 = (bf16[64,2944]{1,0:T(8,128)(2,1)S(1)}, bf16[64,2944]{1,0:T(8,128)(2,1)S(1)}, u32[]{:S(2)}, u32[]{:S(2)}) collective-permute-start(bf16[64,2944]{1,0:T(8,128)(2,1)S(1)} %add_convert_fusion.8), channel_id=1, source_target_pairs={{0,2},{1,5},{2,0},{3,7},{4,6},{5,1},{6,4},{7,3},{8,10},{9,13},{10,... | collective-permute-start | bytes 1130504 | tf_op jit(solution)/shard_map/ppermute | solution.py:210
  127.3 13.5 %collective-permute-start.38 = (bf16[64,2944]{1,0:T(8,128)(2,1)S(1)}, bf16[64,2944]{1,0:T(8,128)(2,1)S(1)}, u32[]{:S(2)}, u32[]{:S(2)}) collective-permute-start(bf16[64,2944]{1,0:T(8,128)(2,1)S(1)} %add_convert_fusion.7), channel_id=1, source_target_pairs={{0,24},{1,25},{2,26},{3,27},{4,28},{5,29},{6,30},{7,31},{8,16},{9,... | collective-permute-start | bytes 1130504 | tf_op jit(solution)/shard_map/ppermute | solution.py:210
  129.2 16.6 %collective-permute-start.39 = (bf16[64,2944]{1,0:T(8,128)(2,1)S(1)}, bf16[64,2944]{1,0:T(8,128)(2,1)S(1)}, u32[]{:S(2)}, u32[]{:S(2)}) collective-permute-start(bf16[64,2944]{1,0:T(8,128)(2,1)S(1)} %add_convert_fusion.6), channel_id=1, source_target_pairs={{0,8},{1,9},{2,10},{3,11},{4,12},{5,13},{6,14},{7,15},{8,0},{9,1},... | collective-permute-start | bytes 1130504 | tf_op jit(solution)/shard_map/ppermute | solution.py:210

commit v6 on v5

--- a/solution.py
+++ b/solution.py
@@ -10,7 +10,7 @@
 SLICES = 4
 LANES = 128
 UNITS = 2 * LANES
-COLUMNS = 12 * LANES
+COLUMNS = 23 * LANES
 BF16 = jnp.bfloat16
 F32 = jnp.float32
 

time: 147 us -> 147 us (level)
  transfers between devices with their start and end apart: 40 -> 40, of which waited for: 16 -> 16; matrix products, arithmetic and copies ran while one was open for 2% -> 2% of each run, Pallas kernels for 25% -> 24%
where the time goes in v6:
time: 147 us
  waiting for transfers between devices  68.8 us (47%)
  starting transfers between devices  37.2 us (25%)
  Pallas kernels  37.1 us (25%)
  other arithmetic  3.31 us (2%)
    ppermute x36, waiting for transfers between devices, swap(): return lax.ppermute(array, 'ex', [(i, partner(i)) for i in range(devices)])  67.7 us
    pallas_call x9, Pallas kernels, expert_call(): pl.pallas_call(functools.partial(first_kernel if first else expert_kernel...  35.8 us
    ppermute x36, starting transfers between devices, swap(): return lax.ppermute(array, 'ex', [(i, partner(i)) for i in range(devices)])  33.1 us
    ppermute x4, starting transfers between devices, inner(): return lax.ppermute(array, 'ex', low + high)  4.1 us
  transfers between devices with their start and end apart: 40, of which 16 were waited for; matrix products, arithmetic and copies ran while one was open for 2% of the time, Pallas kernels for 24%

profile of v6, /device:TPU:0, one launch (start us, length us, event | category | flops | bytes accessed | tf_op | source)
XLA Modules:
  0.0 146.8 jit_solution(8018393843333062210)
XLA Ops:
  0.0 1.3 shard_map.73
  1.3 3.0 %collective-permute-start.1 = (bf16[64,2944]{1,0:T(8,128)(2,1)S(1)}, bf16[64,2944]{1,0:T(8,128)(2,1)S(1)}, u32[]{:S(2)}, u32[]{:S(2)}) collective-permute-start(bf16[64,2944]{1,0:T(8,128)(2,1)S(1)} %shard_map.73), channel_id=1, source_target_pairs={{0,2},{1,5},{2,0},{3,7},{4,6},{5,1},{6,4},{7,3},{8,10},{9,13},{10,... | collective-permute-start | bytes 1130504 | tf_op jit(solution)/shard_map/ppermute | solution.py:210
  4.3 1.6 %collective-permute-start = (bf16[64,2944]{1,0:T(8,128)(2,1)S(1)}, bf16[64,2944]{1,0:T(8,128)(2,1)S(1)}, u32[]{:S(2)}, u32[]{:S(2)}) collective-permute-start(bf16[64,2944]{1,0:T(8,128)(2,1)S(1)} %shard_map.73), channel_id=1, source_target_pairs={{0,8},{1,9},{2,10},{3,11},{4,12},{5,13},{6,14},{7,15},{8,0},{9,1},... | collective-permute-start | bytes 1130504 | tf_op jit(solution)/shard_map/ppermute | solution.py:210
  5.9 0.7 collective-permute-start.3
  6.6 3.3 %collective-permute-done.1 = bf16[64,2944]{1,0:T(8,128)(2,1)S(1)} collective-permute-done((bf16[64,2944]{1,0:T(8,128)(2,1)S(1)}, bf16[64,2944]{1,0:T(8,128)(2,1)S(1)}, u32[]{:S(2)}, u32[]{:S(2)}) %collective-permute-start.1) | collective-permute-done | bytes 376864 | tf_op jit(solution)/shard_map/ppermute | solution.py:210
  9.9 4.7 %collective-permute-done = bf16[64,2944]{1,0:T(8,128)(2,1)S(1)} collective-permute-done((bf16[64,2944]{1,0:T(8,128)(2,1)S(1)}, bf16[64,2944]{1,0:T(8,128)(2,1)S(1)}, u32[]{:S(2)}, u32[]{:S(2)}) %collective-permute-start) | collective-permute-done | bytes 376864 | tf_op jit(solution)/shard_map/ppermute | solution.py:210
  14.6 0.7 collective-permute-start.2
  15.2 1.3 collective-permute-start.4
  16.5 1.5 %collective-permute-start.6 = (bf16[64,2944]{1,0:T(8,128)(2,1)S(1)}, bf16[64,2944]{1,0:T(8,128)(2,1)S(1)}, u32[]{:S(2)}, u32[]{:S(2)}) collective-permute-start(bf16[64,2944]{1,0:T(8,128)(2,1)S(1)} %collective-permute-done), channel_id=1, source_target_pairs={{0,2},{1,5},{2,0},{3,7},{4,6},{5,1},{6,4},{7,3},{8,10},{9,13},{10,... | collective-permute-start | bytes 1130504 | tf_op jit(solution)/shard_map/ppermute | solution.py:210
  18.8 5.8 %shard_map.74 = (bf16[64,2944]{1,0:T(8,128)(2,1)S(1)}, bf16[64,2944]{1,0:T(8,128)(2,1)S(1)}, bf16[2880,1280]{1,0:T(8,128)(2,1)S(1)}, bf16[2880,640]{1,0:T(8,128)(2,1)S(1)}) custom-call(bf16[128,2944]{1,0:T(8,128)(2,1)S(1)} %pad_maximum_fusion.refs_0_, f32[1,128]{1,0:T(1,128)S(1)} %and_convert_fusion.refs_1_.refs_2_, bf16[1,2880,640]{2,1,0:T(8,128)(2,1)} %refs_2_.1, ...), custom_call_target="tpu_custom_call" | custom-call | tf_op jit(solution)/shard_map/pallas_call | solution.py:191
  24.5 3.7 %collective-permute-done.6 = bf16[64,2944]{1,0:T(8,128)(2,1)S(1)} collective-permute-done((bf16[64,2944]{1,0:T(8,128)(2,1)S(1)}, bf16[64,2944]{1,0:T(8,128)(2,1)S(1)}, u32[]{:S(2)}, u32[]{:S(2)}) %collective-permute-start.6) | collective-permute-done | bytes 376864 | tf_op jit(solution)/shard_map/ppermute | solution.py:210
  28.4 1.6 %collective-permute-done.5.refs_0_ = bf16[128,2944]{1,0:T(8,128)(2,1)S(1)} collective-permute-done((bf16[128,2944]{1,0:T(8,128)(2,1)S(1)}, bf16[128,2944]{1,0:T(8,128)(2,1)S(1)}, u32[]{:S(2)}, u32[]{:S(2)}) %collective-permute-start.5) | collective-permute-done | bytes 753696 | tf_op jit(solution)/shard_map/ppermute | solution.py:210
  30.0 1.5 collective-permute-start.8
  31.6 3.0 %collective-permute-start.7 = (bf16[64,2944]{1,0:T(8,128)(2,1)S(1)}, bf16[64,2944]{1,0:T(8,128)(2,1)S(1)}, u32[]{:S(2)}, u32[]{:S(2)}) collective-permute-start(bf16[64,2944]{1,0:T(8,128)(2,1)S(1)} %add.116), channel_id=1, source_target_pairs={{0,2},{1,5},{2,0},{3,7},{4,6},{5,1},{6,4},{7,3},{8,10},{9,13},{10,... | collective-permute-start | bytes 1130504 | tf_op jit(solution)/shard_map/ppermute | solution.py:210
  35.0 2.5 %shard_map.75 = bf16[128,2944]{1,0:T(8,128)(2,1)S(1)} custom-call(bf16[128,2944]{1,0:T(8,128)(2,1)S(1)} %collective-permute-done.5.refs_0_, f32[1,128]{1,0:T(1,128)S(1)} %and_convert_fusion.refs_1_.refs_2_, bf16[2880,1280]{1,0:T(8,128)(2,1)S(1)} %get-tuple-element.85.refs_2_.refs_3_, bf16[2880,640]{1,0:T(8,128)(2,1)S(1)} %get-tuple-element.86.refs_3_.refs_4_), custom_call_target="tpu_custom_call" | custom-call | tf_op jit(solution)/shard_map/pallas_call | solution.py:191
  37.6 6.5 %collective-permute-done.9.refs_1_ = bf16[128,2944]{1,0:T(8,128)(2,1)S(1)} collective-permute-done((bf16[128,2944]{1,0:T(8,128)(2,1)S(1)}, bf16[128,2944]{1,0:T(8,128)(2,1)S(1)}, u32[]{:S(2)}, u32[]{:S(2)}) %collective-permute-start.9) | collective-permute-done | bytes 753696 | tf_op jit(solution)/shard_map/ppermute | solution.py:210
  44.0 1.1 collective-permute-done.8
  45.8 2.2 %collective-permute-start.11 = (bf16[64,2944]{1,0:T(8,128)(2,1)S(1)}, bf16[64,2944]{1,0:T(8,128)(2,1)S(1)}, u32[]{:S(2)}, u32[]{:S(2)}) collective-permute-start(bf16[64,2944]{1,0:T(8,128)(2,1)S(1)} %add.117), channel_id=1, source_target_pairs={{0,2},{1,5},{2,0},{3,7},{4,6},{5,1},{6,4},{7,3},{8,10},{9,13},{10,... | collective-permute-start | bytes 1130504 | tf_op jit(solution)/shard_map/ppermute | solution.py:210
  48.0 3.9 %shard_map.76 = (bf16[128,2944]{1,0:T(8,128)(2,1)S(1)}, bf16[128,2944]{1,0:T(8,128)(2,1)S(1)}) custom-call(bf16[128,2944]{1,0:T(8,128)(2,1)S(1)} %collective-permute-done.13.refs_0_, bf16[128,2944]{1,0:T(8,128)(2,1)S(1)} %collective-permute-done.14.refs_1_, f32[1,128]{1,0:T(1,128)S(1)} %and_convert_fusion.refs_1_.refs_2_, ...), custom_call_target="tpu_custom_call" | custom-call | tf_op jit(solution)/shard_map/pallas_call | solution.py:191
  51.9 3.9 %shard_map.77 = (bf16[64,2944]{1,0:T(8,128)(2,1)S(1)}, bf16[64,2944]{1,0:T(8,128)(2,1)S(1)}, bf16[128,2944]{1,0:T(8,128)(2,1)S(1)}) custom-call(bf16[128,2944]{1,0:T(8,128)(2,1)S(1)} %constant_dynamic-update-slice_fusion.refs_0_, bf16[128,2944]{1,0:T(8,128)(2,1)S(1)} %collective-permute-done.9.refs_1_, f32[1,128]{1,0:T(1,128)S(1)} %and_convert_fusion.refs_1_.refs_2_, ...), custom_call_target="tpu_custom_call" | custom-call | tf_op jit(solution)/shard_map/pallas_call | solution.py:191
  55.8 4.1 %shard_map.78 = (bf16[128,2944]{1,0:T(8,128)(2,1)S(1)}, bf16[128,2944]{1,0:T(8,128)(2,1)S(1)}) custom-call(bf16[128,2944]{1,0:T(8,128)(2,1)S(1)} %collective-permute-done.12.refs_0_, bf16[128,2944]{1,0:T(8,128)(2,1)S(1)} %collective-permute-done.15.refs_1_, f32[1,128]{1,0:T(1,128)S(1)} %and_convert_fusion.refs_1_.refs_2_, ...), custom_call_target="tpu_custom_call" | custom-call | tf_op jit(solution)/shard_map/pallas_call | solution.py:191
  59.9 1.1 collective-permute-done.10.refs_1_
  61.0 0.9 collective-permute-start.21
  61.9 1.0 collective-permute-start.20
  62.9 3.9 %shard_map.79 = (bf16[64,2944]{1,0:T(8,128)(2,1)S(1)}, bf16[64,2944]{1,0:T(8,128)(2,1)S(1)}, bf16[128,2944]{1,0:T(8,128)(2,1)S(1)}) custom-call(bf16[128,2944]{1,0:T(8,128)(2,1)S(1)} %pad_maximum_fusion.1.refs_0_, bf16[128,2944]{1,0:T(8,128)(2,1)S(1)} %collective-permute-done.10.refs_1_, f32[1,128]{1,0:T(1,128)S(1)} %and_convert_fusion.refs_1_.refs_2_, ...), custom_call_target="tpu_custom_call" | custom-call | tf_op jit(solution)/shard_map/pallas_call | solution.py:191
  66.8 3.9 %shard_map.80 = (bf16[128,2944]{1,0:T(8,128)(2,1)S(1)}, bf16[128,2944]{1,0:T(8,128)(2,1)S(1)}) custom-call(bf16[128,2944]{1,0:T(8,128)(2,1)S(1)} %collective-permute-done.16.refs_0_, bf16[128,2944]{1,0:T(8,128)(2,1)S(1)} %collective-permute-done.17.refs_1_, f32[1,128]{1,0:T(1,128)S(1)} %and_convert_fusion.refs_1_.refs_2_, ...), custom_call_target="tpu_custom_call" | custom-call | tf_op jit(solution)/shard_map/pallas_call | solution.py:191
  71.3 1.4 collective-permute-done.21.refs_1_
  72.9 0.9 collective-permute-start.24
  74.0 1.3 collective-permute-start.22
  75.3 3.9 %shard_map.81 = (bf16[64,2944]{1,0:T(8,128)(2,1)S(1)}, bf16[64,2944]{1,0:T(8,128)(2,1)S(1)}, bf16[128,2944]{1,0:T(8,128)(2,1)S(1)}) custom-call(bf16[128,2944]{1,0:T(8,128)(2,1)S(1)} %pad_maximum_fusion.2.refs_0_, bf16[128,2944]{1,0:T(8,128)(2,1)S(1)} %collective-permute-done.21.refs_1_, f32[1,128]{1,0:T(1,128)S(1)} %and_convert_fusion.refs_1_.refs_2_, ...), custom_call_target="tpu_custom_call" | custom-call | tf_op jit(solution)/shard_map/pallas_call | solution.py:191
  79.7 4.1 %shard_map.82 = (bf16[128,2944]{1,0:T(8,128)(2,1)S(1)}, bf16[128,2944]{1,0:T(8,128)(2,1)S(1)}) custom-call(bf16[128,2944]{1,0:T(8,128)(2,1)S(1)} %collective-permute-done.25.refs_0_, bf16[128,2944]{1,0:T(8,128)(2,1)S(1)} %collective-permute-done.26.refs_1_, f32[1,128]{1,0:T(1,128)S(1)} %and_convert_fusion.refs_1_.refs_2_, ...), custom_call_target="tpu_custom_call" | custom-call | tf_op jit(solution)/shard_map/pallas_call | solution.py:191
  83.9 0.8 collective-permute-done.24
  85.3 7.4 %collective-permute-done.22 = bf16[128,2944]{1,0:T(8,128)(2,1)S(1)} collective-permute-done((bf16[128,2944]{1,0:T(8,128)(2,1)S(1)}, bf16[128,2944]{1,0:T(8,128)(2,1)S(1)}, u32[]{:S(2)}, u32[]{:S(2)}) %collective-permute-start.22) | collective-permute-done | bytes 753696 | tf_op jit(solution)/shard_map/ppermute | solution.py:210
  92.7 1.6 %collective-permute-start.28 = (bf16[64,2944]{1,0:T(8,128)(2,1)S(1)}, bf16[64,2944]{1,0:T(8,128)(2,1)S(1)}, u32[]{:S(2)}, u32[]{:S(2)}) collective-permute-start(bf16[64,2944]{1,0:T(8,128)(2,1)S(1)} %add_convert_fusion.11), channel_id=1, source_target_pairs={{0,2},{1,5},{2,0},{3,7},{4,6},{5,1},{6,4},{7,3},{8,10},{9,13},{10,... | collective-permute-start | bytes 1130504 | tf_op jit(solution)/shard_map/ppermute | solution.py:210
  95.0 5.4 %collective-permute-done.28 = bf16[64,2944]{1,0:T(8,128)(2,1)S(1)} collective-permute-done((bf16[64,2944]{1,0:T(8,128)(2,1)S(1)}, bf16[64,2944]{1,0:T(8,128)(2,1)S(1)}, u32[]{:S(2)}, u32[]{:S(2)}) %collective-permute-start.28) | collective-permute-done | bytes 376864 | tf_op jit(solution)/shard_map/ppermute | solution.py:210
  100.5 0.9 collective-permute-start.32
  101.4 5.3 %collective-permute-done.27 = bf16[64,2944]{1,0:T(8,128)(2,1)S(1)} collective-permute-done((bf16[64,2944]{1,0:T(8,128)(2,1)S(1)}, bf16[64,2944]{1,0:T(8,128)(2,1)S(1)}, u32[]{:S(2)}, u32[]{:S(2)}) %collective-permute-start.27) | collective-permute-done | bytes 376864 | tf_op jit(solution)/shard_map/ppermute | solution.py:210
  106.9 0.9 collective-permute-start.35
  107.9 4.6 %collective-permute-start.30 = (bf16[64,2944]{1,0:T(8,128)(2,1)S(1)}, bf16[64,2944]{1,0:T(8,128)(2,1)S(1)}, u32[]{:S(2)}, u32[]{:S(2)}) collective-permute-start(bf16[64,2944]{1,0:T(8,128)(2,1)S(1)} %add_convert_fusion.10), channel_id=1, source_target_pairs={{0,16},{1,17},{2,18},{3,19},{4,20},{5,21},{6,22},{7,23},{8,24},{9,... | collective-permute-start | bytes 1130504 | tf_op jit(solution)/shard_map/ppermute | solution.py:210
  112.7 1.2 collective-permute-start.36
  114.0 11.9 %collective-permute-done.30 = bf16[64,2944]{1,0:T(8,128)(2,1)S(1)} collective-permute-done((bf16[64,2944]{1,0:T(8,128)(2,1)S(1)}, bf16[64,2944]{1,0:T(8,128)(2,1)S(1)}, u32[]{:S(2)}, u32[]{:S(2)}) %collective-permute-start.30) | collective-permute-done | bytes 376864 | tf_op jit(solution)/shard_map/ppermute | solution.py:210
  126.2 1.1 collective-permute-start.37
  127.3 1.7 %collective-permute-start.38 = (bf16[64,2944]{1,0:T(8,128)(2,1)S(1)}, bf16[64,2944]{1,0:T(8,128)(2,1)S(1)}, u32[]{:S(2)}, u32[]{:S(2)}) collective-permute-start(bf16[64,2944]{1,0:T(8,128)(2,1)S(1)} %add_convert_fusion.7), channel_id=1, source_target_pairs={{0,24},{1,25},{2,26},{3,27},{4,28},{5,29},{6,30},{7,31},{8,16},{9,... | collective-permute-start | bytes 1130504 | tf_op jit(solution)/shard_map/ppermute | solution.py:210
  129.2 1.8 %collective-permute-start.39 = (bf16[64,2944]{1,0:T(8,128)(2,1)S(1)}, bf16[64,2944]{1,0:T(8,128)(2,1)S(1)}, u32[]{:S(2)}, u32[]{:S(2)}) collective-permute-start(bf16[64,2944]{1,0:T(8,128)(2,1)S(1)} %add_convert_fusion.6), channel_id=1, source_target_pairs={{0,8},{1,9},{2,10},{3,11},{4,12},{5,13},{6,14},{7,15},{8,0},{9,1},... | collective-permute-start | bytes 1130504 | tf_op jit(solution)/shard_map/ppermute | solution.py:210
  131.0 2.9 %collective-permute-done.37 = bf16[64,2944]{1,0:T(8,128)(2,1)S(1)} collective-permute-done((bf16[64,2944]{1,0:T(8,128)(2,1)S(1)}, bf16[64,2944]{1,0:T(8,128)(2,1)S(1)}, u32[]{:S(2)}, u32[]{:S(2)}) %collective-permute-start.37) | collective-permute-done | bytes 376864 | tf_op jit(solution)/shard_map/ppermute | solution.py:210
  133.9 7.0 %collective-permute-done.38 = bf16[64,2944]{1,0:T(8,128)(2,1)S(1)} collective-permute-done((bf16[64,2944]{1,0:T(8,128)(2,1)S(1)}, bf16[64,2944]{1,0:T(8,128)(2,1)S(1)}, u32[]{:S(2)}, u32[]{:S(2)}) %collective-permute-start.38) | collective-permute-done | bytes 376864 | tf_op jit(solution)/shard_map/ppermute | solution.py:210
  141.1 4.8 %collective-permute-done.39 = bf16[64,2944]{1,0:T(8,128)(2,1)S(1)} collective-permute-done((bf16[64,2944]{1,0:T(8,128)(2,1)S(1)}, bf16[64,2944]{1,0:T(8,128)(2,1)S(1)}, u32[]{:S(2)}, u32[]{:S(2)}) %collective-permute-start.39) | collective-permute-done | bytes 376864 | tf_op jit(solution)/shard_map/ppermute | solution.py:210
  145.9 1.0 add_convert_fusion.4
  (63 shorter events, 6.5 us)
Async XLA Ops:
  1.3 8.6 %collective-permute-start.1 = (bf16[64,2944]{1,0:T(8,128)(2,1)S(1)}, bf16[64,2944]{1,0:T(8,128)(2,1)S(1)}, u32[]{:S(2)}, u32[]{:S(2)}) collective-permute-start(bf16[64,2944]{1,0:T(8,128)(2,1)S(1)} %shard_map.73), channel_id=1, source_target_pairs={{0,2},{1,5},{2,0},{3,7},{4,6},{5,1},{6,4},{7,3},{8,10},{9,13},{10,... | collective-permute-start | bytes 1130504 | tf_op jit(solution)/shard_map/ppermute | solution.py:210
  4.3 10.3 %collective-permute-start = (bf16[64,2944]{1,0:T(8,128)(2,1)S(1)}, bf16[64,2944]{1,0:T(8,128)(2,1)S(1)}, u32[]{:S(2)}, u32[]{:S(2)}) collective-permute-start(bf16[64,2944]{1,0:T(8,128)(2,1)S(1)} %shard_map.73), channel_id=1, source_target_pairs={{0,8},{1,9},{2,10},{3,11},{4,12},{5,13},{6,14},{7,15},{8,0},{9,1},... | collective-permute-start | bytes 1130504 | tf_op jit(solution)/shard_map/ppermute | solution.py:210
  5.9 9.4 %collective-permute-start.3 = (bf16[64,2944]{1,0:T(8,128)(2,1)S(1)}, bf16[64,2944]{1,0:T(8,128)(2,1)S(1)}, u32[]{:S(2)}, u32[]{:S(2)}) collective-permute-start(bf16[64,2944]{1,0:T(8,128)(2,1)S(1)} %shard_map.73), channel_id=1, source_target_pairs={{8,16},{9,17},{10,18},{11,19},{12,20},{13,21},{14,22},{15,23},{16,... | collective-permute-start | bytes 1130504 | tf_op jit(solution)/shard_map/ppermute | solution.py:227
  14.6 15.4 %collective-permute-start.2 = (bf16[64,2944]{1,0:T(8,128)(2,1)S(1)}, bf16[64,2944]{1,0:T(8,128)(2,1)S(1)}, u32[]{:S(2)}, u32[]{:S(2)}) collective-permute-start(bf16[64,2944]{1,0:T(8,128)(2,1)S(1)} %collective-permute-done), channel_id=1, source_target_pairs={{8,16},{9,17},{10,18},{11,19},{12,20},{13,21},{14,22},{15,23},{16,... | collective-permute-start | bytes 1130504 | tf_op jit(solution)/shard_map/ppermute | solution.py:227
  15.2 14.8 %collective-permute-start.4 = (bf16[64,2944]{1,0:T(8,128)(2,1)S(1)}, bf16[64,2944]{1,0:T(8,128)(2,1)S(1)}, u32[]{:S(2)}, u32[]{:S(2)}) collective-permute-start(bf16[64,2944]{1,0:T(8,128)(2,1)S(1)} %collective-permute-done.3), channel_id=1, source_target_pairs={{8,0},{9,1},{10,2},{11,3},{12,4},{13,5},{14,6},{15,7},{16,24},{17,... | collective-permute-start | bytes 1130504 | tf_op jit(solution)/shard_map/ppermute | solution.py:227
  16.5 11.7 %collective-permute-start.6 = (bf16[64,2944]{1,0:T(8,128)(2,1)S(1)}, bf16[64,2944]{1,0:T(8,128)(2,1)S(1)}, u32[]{:S(2)}, u32[]{:S(2)}) collective-permute-start(bf16[64,2944]{1,0:T(8,128)(2,1)S(1)} %collective-permute-done), channel_id=1, source_target_pairs={{0,2},{1,5},{2,0},{3,7},{4,6},{5,1},{6,4},{7,3},{8,10},{9,13},{10,... | collective-permute-start | bytes 1130504 | tf_op jit(solution)/shard_map/ppermute | solution.py:210
  18.1 11.9 %collective-permute-start.5 = (bf16[128,2944]{1,0:T(8,128)(2,1)S(1)}, bf16[128,2944]{1,0:T(8,128)(2,1)S(1)}, u32[]{:S(2)}, u32[]{:S(2)}) collective-permute-start(bf16[128,2944]{1,0:T(8,128)(2,1)S(1)} %pad_maximum_fusion.refs_0_), channel_id=1, source_target_pairs={{0,4},{1,3},{2,6},{3,1},{4,0},{5,7},{6,2},{7,5},{8,12},{9,11},{10,... | collective-permute-start | bytes 2261000 | tf_op jit(solution)/shard_map/ppermute | solution.py:210
  28.3 15.7 %collective-permute-start.9 = (bf16[128,2944]{1,0:T(8,128)(2,1)S(1)}, bf16[128,2944]{1,0:T(8,128)(2,1)S(1)}, u32[]{:S(2)}, u32[]{:S(2)}) collective-permute-start(bf16[128,2944]{1,0:T(8,128)(2,1)S(1)} %constant_dynamic-update-slice_fusion.refs_0_), channel_id=1, source_target_pairs={{0,4},{1,3},{2,6},{3,1},{4,0},{5,7},{6,2},{7,5},{8,12},{9,11},{10,... | collective-permute-start | bytes 2261000 | tf_op jit(solution)/shard_map/ppermute | solution.py:210
  30.0 15.1 %collective-permute-start.8 = (bf16[64,2944]{1,0:T(8,128)(2,1)S(1)}, bf16[64,2944]{1,0:T(8,128)(2,1)S(1)}, u32[]{:S(2)}, u32[]{:S(2)}) collective-permute-start(bf16[64,2944]{1,0:T(8,128)(2,1)S(1)} %collective-permute-done.2), channel_id=1, source_target_pairs={{8,0},{9,1},{10,2},{11,3},{12,4},{13,5},{14,6},{15,7},{16,24},{17,... | collective-permute-start | bytes 1130504 | tf_op jit(solution)/shard_map/ppermute | solution.py:227
  31.6 13.6 %collective-permute-start.7 = (bf16[64,2944]{1,0:T(8,128)(2,1)S(1)}, bf16[64,2944]{1,0:T(8,128)(2,1)S(1)}, u32[]{:S(2)}, u32[]{:S(2)}) collective-permute-start(bf16[64,2944]{1,0:T(8,128)(2,1)S(1)} %add.116), channel_id=1, source_target_pairs={{0,2},{1,5},{2,0},{3,7},{4,6},{5,1},{6,4},{7,3},{8,10},{9,13},{10,... | collective-permute-start | bytes 1130504 | tf_op jit(solution)/shard_map/ppermute | solution.py:210
  34.5 11.2 %collective-permute-start.13 = (bf16[128,2944]{1,0:T(8,128)(2,1)S(1)}, bf16[128,2944]{1,0:T(8,128)(2,1)S(1)}, u32[]{:S(2)}, u32[]{:S(2)}) collective-permute-start(bf16[128,2944]{1,0:T(8,128)(2,1)S(1)} %pad_maximum_fusion.refs_0_), channel_id=1, source_target_pairs={{0,1},{1,0},{2,3},{3,2},{4,5},{5,4},{6,7},{7,6},{8,9},{9,8},{10,11... | collective-permute-start | bytes 2261000 | tf_op jit(solution)/shard_map/ppermute | solution.py:210
  34.5 21.2 %collective-permute-start.12 = (bf16[128,2944]{1,0:T(8,128)(2,1)S(1)}, bf16[128,2944]{1,0:T(8,128)(2,1)S(1)}, u32[]{:S(2)}, u32[]{:S(2)}) collective-permute-start(bf16[128,2944]{1,0:T(8,128)(2,1)S(1)} %constant_dynamic-update-slice_fusion.refs_0_), channel_id=1, source_target_pairs={{0,1},{1,0},{2,3},{3,2},{4,5},{5,4},{6,7},{7,6},{8,9},{9,8},{10,11... | collective-permute-start | bytes 2261000 | tf_op jit(solution)/shard_map/ppermute | solution.py:210
  44.0 4.0 %collective-permute-start.14 = (bf16[128,2944]{1,0:T(8,128)(2,1)S(1)}, bf16[128,2944]{1,0:T(8,128)(2,1)S(1)}, u32[]{:S(2)}, u32[]{:S(2)}) collective-permute-start(bf16[128,2944]{1,0:T(8,128)(2,1)S(1)} %collective-permute-done.5.refs_0_), channel_id=1, source_target_pairs={{0,1},{1,0},{2,3},{3,2},{4,5},{5,4},{6,7},{7,6},{8,9},{9,8},{10,11... | collective-permute-start | bytes 2261000 | tf_op jit(solution)/shard_map/ppermute | solution.py:210
  45.1 10.6 %collective-permute-start.15 = (bf16[128,2944]{1,0:T(8,128)(2,1)S(1)}, bf16[128,2944]{1,0:T(8,128)(2,1)S(1)}, u32[]{:S(2)}, u32[]{:S(2)}) collective-permute-start(bf16[128,2944]{1,0:T(8,128)(2,1)S(1)} %collective-permute-done.9.refs_1_), channel_id=1, source_target_pairs={{0,1},{1,0},{2,3},{3,2},{4,5},{5,4},{6,7},{7,6},{8,9},{9,8},{10,11... | collective-permute-start | bytes 2261000 | tf_op jit(solution)/shard_map/ppermute | solution.py:210
  45.2 15.7 %collective-permute-start.10 = (bf16[128,2944]{1,0:T(8,128)(2,1)S(1)}, bf16[128,2944]{1,0:T(8,128)(2,1)S(1)}, u32[]{:S(2)}, u32[]{:S(2)}) collective-permute-start(bf16[128,2944]{1,0:T(8,128)(2,1)S(1)} %pad_maximum_fusion.1.refs_0_), channel_id=1, source_target_pairs={{0,4},{1,3},{2,6},{3,1},{4,0},{5,7},{6,2},{7,5},{8,12},{9,11},{10,... | collective-permute-start | bytes 2261000 | tf_op jit(solution)/shard_map/ppermute | solution.py:210
  45.8 14.1 %collective-permute-start.11 = (bf16[64,2944]{1,0:T(8,128)(2,1)S(1)}, bf16[64,2944]{1,0:T(8,128)(2,1)S(1)}, u32[]{:S(2)}, u32[]{:S(2)}) collective-permute-start(bf16[64,2944]{1,0:T(8,128)(2,1)S(1)} %add.117), channel_id=1, source_target_pairs={{0,2},{1,5},{2,0},{3,7},{4,6},{5,1},{6,4},{7,3},{8,10},{9,13},{10,... | collective-permute-start | bytes 1130504 | tf_op jit(solution)/shard_map/ppermute | solution.py:210
  48.0 18.8 %collective-permute-start.16 = (bf16[128,2944]{1,0:T(8,128)(2,1)S(1)}, bf16[128,2944]{1,0:T(8,128)(2,1)S(1)}, u32[]{:S(2)}, u32[]{:S(2)}) collective-permute-start(bf16[128,2944]{1,0:T(8,128)(2,1)S(1)} %pad_maximum_fusion.1.refs_0_), channel_id=1, source_target_pairs={{0,1},{1,0},{2,3},{3,2},{4,5},{5,4},{6,7},{7,6},{8,9},{9,8},{10,11... | collective-permute-start | bytes 2261000 | tf_op jit(solution)/shard_map/ppermute | solution.py:210
  61.0 5.8 %collective-permute-start.17 = (bf16[128,2944]{1,0:T(8,128)(2,1)S(1)}, bf16[128,2944]{1,0:T(8,128)(2,1)S(1)}, u32[]{:S(2)}, u32[]{:S(2)}) collective-permute-start(bf16[128,2944]{1,0:T(8,128)(2,1)S(1)} %collective-permute-done.10.refs_1_), channel_id=1, source_target_pairs={{0,1},{1,0},{2,3},{3,2},{4,5},{5,4},{6,7},{7,6},{8,9},{9,8},{10,11... | collective-permute-start | bytes 2261000 | tf_op jit(solution)/shard_map/ppermute | solution.py:210
  61.0 11.7 %collective-permute-start.21 = (bf16[128,2944]{1,0:T(8,128)(2,1)S(1)}, bf16[128,2944]{1,0:T(8,128)(2,1)S(1)}, u32[]{:S(2)}, u32[]{:S(2)}) collective-permute-start(bf16[128,2944]{1,0:T(8,128)(2,1)S(1)} %pad_maximum_fusion.2.refs_0_), channel_id=1, source_target_pairs={{0,4},{1,3},{2,6},{3,1},{4,0},{5,7},{6,2},{7,5},{8,12},{9,11},{10,... | collective-permute-start | bytes 2261000 | tf_op jit(solution)/shard_map/ppermute | solution.py:210
  61.9 10.8 %collective-permute-start.20 = (bf16[128,2944]{1,0:T(8,128)(2,1)S(1)}, bf16[128,2944]{1,0:T(8,128)(2,1)S(1)}, u32[]{:S(2)}, u32[]{:S(2)}) collective-permute-start(bf16[128,2944]{1,0:T(8,128)(2,1)S(1)} %get-tuple-element.107), channel_id=1, source_target_pairs={{0,1},{1,0},{2,3},{3,2},{4,5},{5,4},{6,7},{7,6},{8,9},{9,8},{10,11... | collective-permute-start | bytes 2261000 | tf_op jit(solution)/shard_map/ppermute | solution.py:210
  70.7 3.2 %collective-permute-start.19 = (bf16[128,2944]{1,0:T(8,128)(2,1)S(1)}, bf16[128,2944]{1,0:T(8,128)(2,1)S(1)}, u32[]{:S(2)}, u32[]{:S(2)}) collective-permute-start(bf16[128,2944]{1,0:T(8,128)(2,1)S(1)} %get-tuple-element.106), channel_id=1, source_target_pairs={{0,1},{1,0},{2,3},{3,2},{4,5},{5,4},{6,7},{7,6},{8,9},{9,8},{10,11... | collective-permute-start | bytes 2261000 | tf_op jit(solution)/shard_map/ppermute | solution.py:210
  70.7 13.9 %collective-permute-start.23 = (bf16[128,2944]{1,0:T(8,128)(2,1)S(1)}, bf16[128,2944]{1,0:T(8,128)(2,1)S(1)}, u32[]{:S(2)}, u32[]{:S(2)}) collective-permute-start(bf16[128,2944]{1,0:T(8,128)(2,1)S(1)} %get-tuple-element.97), channel_id=1, source_target_pairs={{0,1},{1,0},{2,3},{3,2},{4,5},{5,4},{6,7},{7,6},{8,9},{9,8},{10,11... | collective-permute-start | bytes 2261000 | tf_op jit(solution)/shard_map/ppermute | solution.py:210
  71.2 4.1 %collective-permute-start.25 = (bf16[128,2944]{1,0:T(8,128)(2,1)S(1)}, bf16[128,2944]{1,0:T(8,128)(2,1)S(1)}, u32[]{:S(2)}, u32[]{:S(2)}) collective-permute-start(bf16[128,2944]{1,0:T(8,128)(2,1)S(1)} %pad_maximum_fusion.2.refs_0_), channel_id=1, source_target_pairs={{0,1},{1,0},{2,3},{3,2},{4,5},{5,4},{6,7},{7,6},{8,9},{9,8},{10,11... | collective-permute-start | bytes 2261000 | tf_op jit(solution)/shard_map/ppermute | solution.py:210
  72.8 6.4 %collective-permute-start.26 = (bf16[128,2944]{1,0:T(8,128)(2,1)S(1)}, bf16[128,2944]{1,0:T(8,128)(2,1)S(1)}, u32[]{:S(2)}, u32[]{:S(2)}) collective-permute-start(bf16[128,2944]{1,0:T(8,128)(2,1)S(1)} %collective-permute-done.21.refs_1_), channel_id=1, source_target_pairs={{0,1},{1,0},{2,3},{3,2},{4,5},{5,4},{6,7},{7,6},{8,9},{9,8},{10,11... | collective-permute-start | bytes 2261000 | tf_op jit(solution)/shard_map/ppermute | solution.py:210
  72.9 11.7 %collective-permute-start.24 = (bf16[128,2944]{1,0:T(8,128)(2,1)S(1)}, bf16[128,2944]{1,0:T(8,128)(2,1)S(1)}, u32[]{:S(2)}, u32[]{:S(2)}) collective-permute-start(bf16[128,2944]{1,0:T(8,128)(2,1)S(1)} %add_convert_fusion.2), channel_id=1, source_target_pairs={{0,4},{1,3},{2,6},{3,1},{4,0},{5,7},{6,2},{7,5},{8,12},{9,11},{10,... | collective-permute-start | bytes 2261000 | tf_op jit(solution)/shard_map/ppermute | solution.py:210
  74.0 18.7 %collective-permute-start.22 = (bf16[128,2944]{1,0:T(8,128)(2,1)S(1)}, bf16[128,2944]{1,0:T(8,128)(2,1)S(1)}, u32[]{:S(2)}, u32[]{:S(2)}) collective-permute-start(bf16[128,2944]{1,0:T(8,128)(2,1)S(1)} %add_convert_fusion.3), channel_id=1, source_target_pairs={{0,4},{1,3},{2,6},{3,1},{4,0},{5,7},{6,2},{7,5},{8,12},{9,11},{10,... | collective-permute-start | bytes 2261000 | tf_op jit(solution)/shard_map/ppermute | solution.py:210
  75.3 19.0 %collective-permute-start.18 = (bf16[128,2944]{1,0:T(8,128)(2,1)S(1)}, bf16[128,2944]{1,0:T(8,128)(2,1)S(1)}, u32[]{:S(2)}, u32[]{:S(2)}) collective-permute-start(bf16[128,2944]{1,0:T(8,128)(2,1)S(1)} %get-tuple-element.104), channel_id=1, source_target_pairs={{0,1},{1,0},{2,3},{3,2},{4,5},{5,4},{6,7},{7,6},{8,9},{9,8},{10,11... | collective-permute-start | bytes 2261000 | tf_op jit(solution)/shard_map/ppermute | solution.py:210
  79.2 27.5 %collective-permute-start.33 = (bf16[128,2944]{1,0:T(8,128)(2,1)S(1)}, bf16[128,2944]{1,0:T(8,128)(2,1)S(1)}, u32[]{:S(2)}, u32[]{:S(2)}) collective-permute-start(bf16[128,2944]{1,0:T(8,128)(2,1)S(1)} %get-tuple-element.128), channel_id=1, source_target_pairs={{0,1},{1,0},{2,3},{3,2},{4,5},{5,4},{6,7},{7,6},{8,9},{9,8},{10,11... | collective-permute-start | bytes 2261000 | tf_op jit(solution)/shard_map/ppermute | solution.py:210
  84.6 28.0 %collective-permute-start.31 = (bf16[128,2944]{1,0:T(8,128)(2,1)S(1)}, bf16[128,2944]{1,0:T(8,128)(2,1)S(1)}, u32[]{:S(2)}, u32[]{:S(2)}) collective-permute-start(bf16[128,2944]{1,0:T(8,128)(2,1)S(1)} %get-tuple-element.116), channel_id=1, source_target_pairs={{0,1},{1,0},{2,3},{3,2},{4,5},{5,4},{6,7},{7,6},{8,9},{9,8},{10,11... | collective-permute-start | bytes 2261000 | tf_op jit(solution)/shard_map/ppermute | solution.py:210
  84.7 10.3 %collective-permute-start.29 = (bf16[128,2944]{1,0:T(8,128)(2,1)S(1)}, bf16[128,2944]{1,0:T(8,128)(2,1)S(1)}, u32[]{:S(2)}, u32[]{:S(2)}) collective-permute-start(bf16[128,2944]{1,0:T(8,128)(2,1)S(1)} %get-tuple-element.123), channel_id=1, source_target_pairs={{0,1},{1,0},{2,3},{3,2},{4,5},{5,4},{6,7},{7,6},{8,9},{9,8},{10,11... | collective-permute-start | bytes 2261000 | tf_op jit(solution)/shard_map/ppermute | solution.py:210
  92.7 7.6 %collective-permute-start.28 = (bf16[64,2944]{1,0:T(8,128)(2,1)S(1)}, bf16[64,2944]{1,0:T(8,128)(2,1)S(1)}, u32[]{:S(2)}, u32[]{:S(2)}) collective-permute-start(bf16[64,2944]{1,0:T(8,128)(2,1)S(1)} %add_convert_fusion.11), channel_id=1, source_target_pairs={{0,2},{1,5},{2,0},{3,7},{4,6},{5,1},{6,4},{7,3},{8,10},{9,13},{10,... | collective-permute-start | bytes 1130504 | tf_op jit(solution)/shard_map/ppermute | solution.py:210
  94.4 12.3 %collective-permute-start.27 = (bf16[64,2944]{1,0:T(8,128)(2,1)S(1)}, bf16[64,2944]{1,0:T(8,128)(2,1)S(1)}, u32[]{:S(2)}, u32[]{:S(2)}) collective-permute-start(bf16[64,2944]{1,0:T(8,128)(2,1)S(1)} %add_convert_fusion.12), channel_id=1, source_target_pairs={{0,2},{1,5},{2,0},{3,7},{4,6},{5,1},{6,4},{7,3},{8,10},{9,13},{10,... | collective-permute-start | bytes 1130504 | tf_op jit(solution)/shard_map/ppermute | solution.py:210
  100.5 12.1 %collective-permute-start.32 = (bf16[128,2944]{1,0:T(8,128)(2,1)S(1)}, bf16[128,2944]{1,0:T(8,128)(2,1)S(1)}, u32[]{:S(2)}, u32[]{:S(2)}) collective-permute-start(bf16[128,2944]{1,0:T(8,128)(2,1)S(1)} %add_convert_fusion.1), channel_id=1, source_target_pairs={{0,4},{1,3},{2,6},{3,1},{4,0},{5,7},{6,2},{7,5},{8,12},{9,11},{10,... | collective-permute-start | bytes 2261000 | tf_op jit(solution)/shard_map/ppermute | solution.py:210
  106.9 19.0 %collective-permute-start.35 = (bf16[128,2944]{1,0:T(8,128)(2,1)S(1)}, bf16[128,2944]{1,0:T(8,128)(2,1)S(1)}, u32[]{:S(2)}, u32[]{:S(2)}) collective-permute-start(bf16[128,2944]{1,0:T(8,128)(2,1)S(1)} %add_convert_fusion), channel_id=1, source_target_pairs={{0,4},{1,3},{2,6},{3,1},{4,0},{5,7},{6,2},{7,5},{8,12},{9,11},{10,... | collective-permute-start | bytes 2261000 | tf_op jit(solution)/shard_map/ppermute | solution.py:210
  107.9 17.9 %collective-permute-start.30 = (bf16[64,2944]{1,0:T(8,128)(2,1)S(1)}, bf16[64,2944]{1,0:T(8,128)(2,1)S(1)}, u32[]{:S(2)}, u32[]{:S(2)}) collective-permute-start(bf16[64,2944]{1,0:T(8,128)(2,1)S(1)} %add_convert_fusion.10), channel_id=1, source_target_pairs={{0,16},{1,17},{2,18},{3,19},{4,20},{5,21},{6,22},{7,23},{8,24},{9,... | collective-permute-start | bytes 1130504 | tf_op jit(solution)/shard_map/ppermute | solution.py:210
  112.7 13.1 %collective-permute-start.36 = (bf16[64,2944]{1,0:T(8,128)(2,1)S(1)}, bf16[64,2944]{1,0:T(8,128)(2,1)S(1)}, u32[]{:S(2)}, u32[]{:S(2)}) collective-permute-start(bf16[64,2944]{1,0:T(8,128)(2,1)S(1)} %add_convert_fusion.9), channel_id=1, source_target_pairs={{0,2},{1,5},{2,0},{3,7},{4,6},{5,1},{6,4},{7,3},{8,10},{9,13},{10,... | collective-permute-start | bytes 1130504 | tf_op jit(solution)/shard_map/ppermute | solution.py:210
  114.0 12.1 %collective-permute-start.34 = (bf16[128,2944]{1,0:T(8,128)(2,1)S(1)}, bf16[128,2944]{1,0:T(8,128)(2,1)S(1)}, u32[]{:S(2)}, u32[]{:S(2)}) collective-permute-start(bf16[128,2944]{1,0:T(8,128)(2,1)S(1)} %get-tuple-element.92), channel_id=1, source_target_pairs={{0,1},{1,0},{2,3},{3,2},{4,5},{5,4},{6,7},{7,6},{8,9},{9,8},{10,11... | collective-permute-start | bytes 2261000 | tf_op jit(solution)/shard_map/ppermute | solution.py:210
  126.2 7.7 %collective-permute-start.37 = (bf16[64,2944]{1,0:T(8,128)(2,1)S(1)}, bf16[64,2944]{1,0:T(8,128)(2,1)S(1)}, u32[]{:S(2)}, u32[]{:S(2)}) collective-permute-start(bf16[64,2944]{1,0:T(8,128)(2,1)S(1)} %add_convert_fusion.8), channel_id=1, source_target_pairs={{0,2},{1,5},{2,0},{3,7},{4,6},{5,1},{6,4},{7,3},{8,10},{9,13},{10,... | collective-permute-start | bytes 1130504 | tf_op jit(solution)/shard_map/ppermute | solution.py:210
  127.3 13.5 %collective-permute-start.38 = (bf16[64,2944]{1,0:T(8,128)(2,1)S(1)}, bf16[64,2944]{1,0:T(8,128)(2,1)S(1)}, u32[]{:S(2)}, u32[]{:S(2)}) collective-permute-start(bf16[64,2944]{1,0:T(8,128)(2,1)S(1)} %add_convert_fusion.7), channel_id=1, source_target_pairs={{0,24},{1,25},{2,26},{3,27},{4,28},{5,29},{6,30},{7,31},{8,16},{9,... | collective-permute-start | bytes 1130504 | tf_op jit(solution)/shard_map/ppermute | solution.py:210
  129.2 16.7 %collective-permute-start.39 = (bf16[64,2944]{1,0:T(8,128)(2,1)S(1)}, bf16[64,2944]{1,0:T(8,128)(2,1)S(1)}, u32[]{:S(2)}, u32[]{:S(2)}) collective-permute-start(bf16[64,2944]{1,0:T(8,128)(2,1)S(1)} %add_convert_fusion.6), channel_id=1, source_target_pairs={{0,8},{1,9},{2,10},{3,11},{4,12},{5,13},{6,14},{7,15},{8,0},{9,1},... | collective-permute-start | bytes 1130504 | tf_op jit(solution)/shard_map/ppermute | solution.py:210
